TPU v7x, 32 devices: a whole 2x2x4 slice. The times are simulated.
32 devices in a mesh: ctx: 8 (over z, y), wsh: 4 (over x, core).
Axes of the slice: x: 2, y: 2, z: 4, core: 2. Of those that a mesh axis runs over, the one named last changes fastest.
Arguments:
- hidden_in: bfloat16 [4, 2048, 768], P('wsh', 'ctx'), may hold values from -6 to 6
- w_query: bfloat16 [768, 768], P('wsh'), may hold values from -0.09375 to 0.09375
- w_key: bfloat16 [768, 768], P('wsh'), may hold values from -0.09375 to 0.09375
- w_value: bfloat16 [768, 768], P('wsh'), may hold values from -0.21875 to 0.21875
- w_output: bfloat16 [768, 768], P('wsh'), may hold values from -3 to 3
- w_router: bfloat16 [768, 16], P('wsh'), may hold values from -0.109375 to 0.109375
- gain_attn: bfloat16 [768], P('wsh'), may hold values from 0.5 to 1.5
- gain_moe: bfloat16 [768], P('wsh'), may hold values from 0.5 to 1.5
- rel_bias: bfloat16 [32, 12], P('wsh'), may hold values from -124 to 124
- w_in: bfloat16 [16, 768, 3072], P('ctx', None, 'wsh'), may hold values from -0.21875 to 0.21875
- w_out: bfloat16 [16, 3072, 768], P('ctx', 'wsh'), may hold values from -2 to 2
- routes: int32 [4, 2048, 1], P('wsh', 'ctx'), may hold values from 0 to 15; in each aligned block of 256 rows (0 to 255, 256 to 511, ..., all dimensions but the last counted through in order) at most 32 rows name the same one
- block_pairs: int32 [8, 2], replicated, may hold values from 0 to 15, as said below
- cotangent: bfloat16 [4, 2048, 768], P('wsh', 'ctx'), may hold values from -6 to 6
Outputs:
- output: bfloat16 [4, 2048, 768], P('wsh', 'ctx')
- input_grad: bfloat16 [4, 2048, 768], P('wsh', 'ctx')
- grad_query: float32 [768, 768], P('wsh')
- grad_key: float32 [768, 768], P('wsh')
- grad_value: float32 [768, 768], P('wsh')
- grad_output: float32 [768, 768], P('wsh')
- grad_router: float32 [768, 16], P('wsh')
- grad_gain_attn: float32 [768], P('wsh')
- grad_gain_moe: float32 [768], P('wsh')
- grad_rel_bias: float32 [32, 12], P('wsh')
- grad_w_in: float32 [16, 768, 3072], P('ctx', None, 'wsh')
- grad_w_out: float32 [16, 3072, 768], P('ctx', 'wsh')
Inputs may be any that keep to these rules, and one draw needn't show every extreme that they name: `block_pairs`: row c names the two blocks of 128 tokens that ctx index c holds, in the order of its rows: a block b and the block that is b places from the end; every block of a sequence is named once. `routes`: in the rows of one device no expert is named more than 32 times, and in some device's rows an expert is named exactly 32 times.
All inputs are finite; a program needn't handle non-finite values.
Results may differ from a plain program's by a relative error of at most 0.017.
Values may be sent and summed in bfloat16 or wider, within the bound.
A program may use at most 256 MiB of HBM per device.

v0:
```python
import math

import jax
import jax.numpy as jnp
from jax import lax
from jax.sharding import PartitionSpec as P

HEADS = 12
HEAD_DIM = 64


bucket_edges = [math.ceil(16 * 8 ** (marker / 16)) for marker in range(1, 16)]
epsilon = 1e-06


def bucket_index(distance):
    gap_ahead = jnp.maximum(distance, 0)
    bucket_count = jnp.full(gap_ahead.shape, 16, jnp.int32)
    for threshold in bucket_edges:
        bucket_count = bucket_count + (gap_ahead >= threshold).astype(jnp.int32)
    return jnp.where(gap_ahead < 16, gap_ahead, bucket_count)


def gelu_tanh(values):
    return jax.nn.gelu(values, approximate=True)


def rms_forward(values, gain_vec):
    inv_rms = lax.rsqrt(jnp.mean(values * values, axis=-1, keepdims=True) + epsilon)
    return (values * inv_rms * gain_vec, inv_rms)


def rms_backward(values, inv_rms, gain_vec, upstream):
    grad_gain = jnp.sum(upstream * values * inv_rms, axis=0)
    scaled = upstream * gain_vec
    grad_values = inv_rms * scaled - values * inv_rms**3 * jnp.mean(
        scaled * values, axis=-1, keepdims=True
    )
    return (grad_values, grad_gain)


def bias_tiles(extended, query_starts, key_starts, block_len, length):
    num_heads = extended.shape[0]

    def one_tile(query_start, key_start):
        offset = query_start - key_start - (block_len - 1) + length
        window = lax.dynamic_slice_in_dim(extended, offset, 2 * block_len - 1, 1)
        flipped = jnp.concatenate(
            [window[:, ::-1], jnp.zeros((num_heads, 1), extended.dtype)], axis=1
        )
        widened = jnp.broadcast_to(flipped[:, None, :], (num_heads, block_len, 2 * block_len))
        widened = widened.reshape(num_heads, 2 * block_len * block_len)[
            :, : block_len * (2 * block_len - 1)
        ]
        return widened.reshape(num_heads, block_len, 2 * block_len - 1)[:, :, block_len - 1 :]

    tile_grid = jax.vmap(
        lambda query_start: jax.vmap(lambda key_start: one_tile(query_start, key_start))(key_starts)
    )(query_starts)
    query_count = query_starts.shape[0]
    key_count = key_starts.shape[0]
    return jnp.transpose(tile_grid, (2, 0, 3, 1, 4)).reshape(
        num_heads, query_count * block_len, key_count * block_len
    )


def per_device(
    hidden_in,
    w_query,
    w_key,
    w_value,
    w_output,
    w_router,
    gain_attn,
    gain_moe,
    rel_bias,
    w_in,
    w_out,
    routes,
    block_pairs,
    cotangent,
):
    tokens = hidden_in.shape[1]
    model_width = hidden_in.shape[2]
    block_len = tokens // 2
    num_heads = HEADS
    head_size = HEAD_DIM
    ctx_count = lax.axis_size("ctx")
    wsh_count = lax.axis_size("wsh")
    length = tokens * ctx_count
    experts = w_router.shape[1]
    exp_dev = w_in.shape[0]
    slot_most = 2 * tokens // experts
    capacity = (9 * length // (8 * experts) + 7) // 8 * 8
    key_block = max(min(512, length), block_len)
    key_steps = length // key_block
    sub_blocks = key_block // block_len
    ctx_rank = lax.axis_index("ctx")
    wsh_rank = lax.axis_index("wsh")
    all_pos = (
        block_pairs.reshape(-1)[:, None] * block_len
        + jnp.arange(block_len, dtype=jnp.int32)[None, :]
    ).reshape(-1)
    my_pos = lax.dynamic_slice_in_dim(all_pos, ctx_rank * tokens, tokens)
    query_starts = my_pos.reshape(2, block_len)[:, 0]
    (
        full_query,
        full_key,
        full_value,
        full_output,
        full_router,
        full_gain_a,
        full_gain_m,
        full_bias,
    ) = (
        lax.all_gather(w_query, "wsh", axis=0, tiled=True),
        lax.all_gather(w_key, "wsh", axis=0, tiled=True),
        lax.all_gather(w_value, "wsh", axis=0, tiled=True),
        lax.all_gather(w_output, "wsh", axis=0, tiled=True),
        lax.all_gather(w_router, "wsh", axis=0, tiled=True),
        lax.all_gather(gain_attn, "wsh", axis=0, tiled=True),
        lax.all_gather(gain_moe, "wsh", axis=0, tiled=True),
        lax.all_gather(rel_bias, "wsh", axis=0, tiled=True),
    )
    gain_one = full_gain_a.astype(jnp.float32)
    gain_two = full_gain_m.astype(jnp.float32)
    bias_table = full_bias.astype(jnp.float32)
    buckets = bias_table.shape[0]
    bucket_ids = jnp.arange(buckets, dtype=jnp.int32)
    signed_gap = jnp.arange(2 * length, dtype=jnp.int32) - length
    gap_onehot = (bucket_index(signed_gap)[:, None] == bucket_ids[None, :]).astype(jnp.float32)
    gap_extended = jnp.dot(gap_onehot, bias_table, precision=lax.Precision.HIGHEST).T
    resid_in = hidden_in[0].astype(jnp.float32)
    normed_one, inv_one = rms_forward(resid_in, gain_one)
    normed_one = normed_one.astype(jnp.bfloat16)
    queries = jnp.dot(normed_one, full_query, preferred_element_type=jnp.float32).astype(
        jnp.bfloat16
    )
    key_local = jnp.dot(normed_one, full_key, preferred_element_type=jnp.float32).astype(
        jnp.bfloat16
    )
    value_local = jnp.dot(normed_one, full_value, preferred_element_type=jnp.float32).astype(
        jnp.bfloat16
    )
    keys_all, values_all = (
        lax.all_gather(key_local, "ctx", axis=0, tiled=True),
        lax.all_gather(value_local, "ctx", axis=0, tiled=True),
    )
    query_heads = queries.reshape(tokens, num_heads, head_size)
    key_blocks = keys_all.reshape(key_steps, key_block, num_heads, head_size)
    value_blocks = values_all.reshape(key_steps, key_block, num_heads, head_size)
    pos_blocks = all_pos.reshape(key_steps, key_block)

    def make_bias(extended, pos_part):
        key_starts = pos_part.reshape(sub_blocks, block_len)[:, 0]
        return bias_tiles(extended, query_starts, key_starts, block_len, length)

    def block_scores(key_part, pos_part, bias_part):
        gap_mat = my_pos[:, None] - pos_part[None, :]
        raw = jnp.einsum("qhd,khd->hqk", query_heads, key_part, preferred_element_type=jnp.float32)
        raw = raw + bias_part
        return jnp.where((gap_mat >= 0)[None], raw, -1e30)

    def stats_step(carry, items):
        run_max, run_sum = carry
        scores = block_scores(items[0], items[1], make_bias(gap_extended, items[1]))
        new_max = jnp.maximum(run_max, jnp.max(scores, axis=-1))
        run_sum = run_sum * jnp.exp(run_max - new_max) + jnp.sum(
            jnp.exp(scores - new_max[..., None]), axis=-1
        )
        return ((new_max, run_sum), None)

    start_max = jnp.full((num_heads, tokens), -1e30, jnp.float32)
    (row_max, row_sum), unused = lax.scan(
        stats_step, (start_max, jnp.zeros_like(start_max)), (key_blocks, pos_blocks)
    )
    log_total = row_max + jnp.log(row_sum)

    def output_step(carry, items):
        scores = block_scores(items[0], items[1], make_bias(gap_extended, items[1]))
        weights_f = jnp.exp(scores - log_total[..., None])
        weights_b = weights_f.astype(jnp.bfloat16)
        weights_r = (weights_f - weights_b.astype(jnp.float32)).astype(jnp.bfloat16)
        stacked = jnp.concatenate([weights_b, weights_r], axis=1)
        return (
            carry
            + jnp.einsum("hqk,khd->qhd", stacked, items[2], preferred_element_type=jnp.float32),
            None,
        )

    both_out, unused = lax.scan(
        output_step,
        jnp.zeros((2 * tokens, num_heads, head_size), jnp.float32),
        (key_blocks, pos_blocks, value_blocks),
    )
    attn_main = both_out[:tokens]
    attn_exact = attn_main + both_out[tokens:]
    attn_low = attn_main.reshape(tokens, model_width).astype(jnp.bfloat16)
    branch_attn = jnp.dot(attn_low, full_output, preferred_element_type=jnp.float32)
    resid_mid = resid_in + branch_attn
    normed_two, inv_two = rms_forward(resid_mid, gain_two)
    normed_two = normed_two.astype(jnp.bfloat16)
    logits = jnp.dot(normed_two, full_router, preferred_element_type=jnp.float32)
    probs = jax.nn.softmax(logits, axis=-1)
    route_ids = routes[0, :, 0]
    chosen = route_ids[:, None] == jnp.arange(experts, dtype=jnp.int32)[None, :]
    gate_val = jnp.sum(jnp.where(chosen, probs, 0.0), axis=-1)
    chosen_int = chosen.astype(jnp.int32)
    local_rank = jnp.sum((jnp.cumsum(chosen_int, axis=0) - chosen_int) * chosen_int, axis=-1)
    expert_counts = jnp.sum(chosen_int, axis=0)
    local_slot = route_ids * slot_most + local_rank
    placement = (
        jnp.arange(experts * slot_most, dtype=jnp.int32)[:, None] == local_slot[None, :]
    ).astype(jnp.bfloat16)
    outgoing = jnp.dot(placement, normed_two, preferred_element_type=jnp.float32).astype(
        jnp.bfloat16
    )
    outgoing = outgoing.reshape(ctx_count, exp_dev, slot_most, model_width)
    incoming, income_counts = (
        lax.all_to_all(outgoing, "ctx", split_axis=0, concat_axis=0, tiled=True),
        lax.all_to_all(
            expert_counts.reshape(ctx_count, exp_dev),
            "ctx",
            split_axis=0,
            concat_axis=0,
            tiled=True,
        ),
    )
    offsets = jnp.cumsum(income_counts, axis=0) - income_counts
    slot_index = jnp.arange(slot_most, dtype=jnp.int32)
    target = offsets.T[:, :, None] + slot_index[None, None, :]
    target = jnp.where(slot_index[None, None, :] < income_counts.T[:, :, None], target, capacity)
    cap_map = (
        target[:, None, :, :] == jnp.arange(capacity, dtype=jnp.int32)[None, :, None, None]
    ).astype(jnp.bfloat16)
    expert_rows = jnp.einsum(
        "ecsr,serd->ecd", cap_map, incoming, preferred_element_type=jnp.float32
    ).astype(jnp.bfloat16)
    full_in, full_out = (
        lax.all_gather(w_in, "wsh", axis=2, tiled=True),
        lax.all_gather(w_out, "wsh", axis=1, tiled=True),
    )
    pre_act = jnp.einsum("ecd,edf->ecf", expert_rows, full_in, preferred_element_type=jnp.float32)
    hidden_act = gelu_tanh(pre_act).astype(jnp.bfloat16)
    expert_out = jnp.einsum(
        "ecf,efd->ecd", hidden_act, full_out, preferred_element_type=jnp.float32
    ).astype(jnp.bfloat16)
    returning = jnp.einsum(
        "ecsr,ecd->serd", cap_map, expert_out, preferred_element_type=jnp.float32
    ).astype(jnp.bfloat16)
    returned = lax.all_to_all(returning, "ctx", split_axis=0, concat_axis=0, tiled=True)
    token_out = jnp.einsum(
        "st,sd->td",
        placement,
        returned.reshape(experts * slot_most, model_width),
        preferred_element_type=jnp.float32,
    )
    output_rows = resid_mid + gate_val[:, None] * token_out
    upstream = cotangent[0].astype(jnp.float32)
    grad_gate = jnp.sum(upstream * token_out, axis=-1)
    grad_token = (gate_val[:, None] * upstream).astype(jnp.bfloat16)
    grad_send = jnp.dot(placement, grad_token, preferred_element_type=jnp.float32).astype(
        jnp.bfloat16
    )
    grad_send = grad_send.reshape(ctx_count, exp_dev, slot_most, model_width)
    grad_recv = lax.all_to_all(grad_send, "ctx", split_axis=0, concat_axis=0, tiled=True)
    grad_slots = jnp.einsum(
        "ecsr,serd->ecd", cap_map, grad_recv, preferred_element_type=jnp.float32
    ).astype(jnp.bfloat16)
    grad_hidden = jnp.einsum(
        "ecd,efd->ecf", grad_slots, full_out, preferred_element_type=jnp.float32
    )
    grad_pre = jax.vjp(gelu_tanh, pre_act)[1](grad_hidden)[0].astype(jnp.bfloat16)
    grad_w_out = jnp.einsum(
        "ecf,ecd->efd", hidden_act, grad_slots, preferred_element_type=jnp.float32
    )
    grad_w_in = jnp.einsum(
        "ecd,ecf->edf", expert_rows, grad_pre, preferred_element_type=jnp.float32
    )
    grad_rows = jnp.einsum(
        "ecf,edf->ecd", grad_pre, full_in, preferred_element_type=jnp.float32
    ).astype(jnp.bfloat16)
    shard_in, shard_out = (
        lax.psum_scatter(
            grad_w_in.astype(jnp.bfloat16), "wsh", scatter_dimension=2, tiled=True
        ).astype(jnp.float32),
        lax.psum_scatter(
            grad_w_out.astype(jnp.bfloat16), "wsh", scatter_dimension=1, tiled=True
        ).astype(jnp.float32),
    )
    grad_back = jnp.einsum(
        "ecsr,ecd->serd", cap_map, grad_rows, preferred_element_type=jnp.float32
    ).astype(jnp.bfloat16)
    grad_home = lax.all_to_all(grad_back, "ctx", split_axis=0, concat_axis=0, tiled=True)
    grad_expert_in = jnp.einsum(
        "st,sd->td",
        placement,
        grad_home.reshape(experts * slot_most, model_width),
        preferred_element_type=jnp.float32,
    )
    grad_logits = ((gate_val * grad_gate)[:, None] * (chosen.astype(jnp.float32) - probs)).astype(
        jnp.bfloat16
    )
    grad_normed_two = grad_expert_in + jnp.einsum(
        "te,de->td", grad_logits, full_router, preferred_element_type=jnp.float32
    )
    grad_router = jnp.einsum(
        "td,te->de", normed_two, grad_logits, preferred_element_type=jnp.float32
    )
    grad_mid_norm, grad_gain_m = rms_backward(resid_mid, inv_two, gain_two, grad_normed_two)
    grad_mid = upstream + grad_mid_norm
    grad_branch = grad_mid.astype(jnp.bfloat16)
    grad_wout_attn = jnp.einsum(
        "td,te->de", attn_low, grad_branch, preferred_element_type=jnp.float32
    )
    grad_attn = jnp.einsum(
        "te,de->td", grad_branch, full_output, preferred_element_type=jnp.float32
    ).astype(jnp.bfloat16)
    grad_heads = grad_attn.reshape(tokens, num_heads, head_size)
    row_delta = jnp.einsum("qhd,qhd->hq", grad_heads.astype(jnp.float32), attn_exact)

    def grad_step(carry, items):
        grad_q, grad_extended = carry
        key_part, pos_part, value_part = items
        bias_part, bias_pull = jax.vjp(lambda extended: make_bias(extended, pos_part), gap_extended)
        scores = block_scores(key_part, pos_part, bias_part)
        weights_f = jnp.exp(scores - log_total[..., None])
        weights_b = weights_f.astype(jnp.bfloat16)
        grad_w = jnp.einsum(
            "qhd,khd->hqk", grad_heads, value_part, preferred_element_type=jnp.float32
        )
        grad_s = (weights_f * (grad_w - row_delta[..., None])).astype(jnp.bfloat16)
        grad_q = grad_q + jnp.einsum(
            "hqk,khd->qhd", grad_s, key_part, preferred_element_type=jnp.float32
        )
        grad_k = jnp.einsum("hqk,qhd->khd", grad_s, query_heads, preferred_element_type=jnp.float32)
        grad_v = jnp.einsum(
            "hqk,qhd->khd", weights_b, grad_heads, preferred_element_type=jnp.float32
        )
        grad_extended = grad_extended + bias_pull(grad_s.astype(jnp.float32))[0]
        return ((grad_q, grad_extended), (grad_k, grad_v))

    start_grads = (
        jnp.zeros((tokens, num_heads, head_size), jnp.float32),
        jnp.zeros_like(gap_extended),
    )
    (grad_q_all, grad_ext_sum), (grad_k_all, grad_v_all) = lax.scan(
        grad_step, start_grads, (key_blocks, pos_blocks, value_blocks)
    )
    grad_table = jnp.dot(gap_onehot.T, grad_ext_sum.T, precision=lax.Precision.HIGHEST)
    grad_k_sum, grad_v_sum = (
        lax.psum_scatter(
            grad_k_all.reshape(length, model_width).astype(jnp.bfloat16),
            "ctx",
            scatter_dimension=0,
            tiled=True,
        ).astype(jnp.float32),
        lax.psum_scatter(
            grad_v_all.reshape(length, model_width).astype(jnp.bfloat16),
            "ctx",
            scatter_dimension=0,
            tiled=True,
        ).astype(jnp.float32),
    )
    grad_q_low = grad_q_all.reshape(tokens, model_width).astype(jnp.bfloat16)
    grad_k_low = grad_k_sum.astype(jnp.bfloat16)
    grad_v_low = grad_v_sum.astype(jnp.bfloat16)
    grad_normed_one = jnp.einsum(
        "te,de->td", grad_q_low, full_query, preferred_element_type=jnp.float32
    )
    grad_normed_one = grad_normed_one + jnp.einsum(
        "te,de->td", grad_k_low, full_key, preferred_element_type=jnp.float32
    )
    grad_normed_one = grad_normed_one + jnp.einsum(
        "te,de->td", grad_v_low, full_value, preferred_element_type=jnp.float32
    )
    grad_wq = jnp.einsum("td,te->de", normed_one, grad_q_low, preferred_element_type=jnp.float32)
    grad_wk = jnp.einsum("td,te->de", normed_one, grad_k_low, preferred_element_type=jnp.float32)
    grad_wv = jnp.einsum("td,te->de", normed_one, grad_v_low, preferred_element_type=jnp.float32)
    grad_in_norm, grad_gain_a = rms_backward(resid_in, inv_one, gain_one, grad_normed_one)
    grad_input = (grad_mid + grad_in_norm).astype(jnp.bfloat16)
    row_share = model_width // wsh_count
    bucket_share = buckets // wsh_count

    def own_rows(whole, share):
        return lax.dynamic_slice_in_dim(whole, wsh_rank * share, share, 0)

    summed = lax.psum(
        (
            grad_wq,
            grad_wk,
            grad_wv,
            grad_wout_attn,
            grad_router,
            grad_gain_a,
            grad_gain_m,
            grad_table,
        ),
        ("ctx", "wsh"),
    )
    shares = (
        own_rows(summed[0], row_share),
        own_rows(summed[1], row_share),
        own_rows(summed[2], row_share),
        own_rows(summed[3], row_share),
        own_rows(summed[4], row_share),
        own_rows(summed[5], row_share),
        own_rows(summed[6], row_share),
        own_rows(summed[7], bucket_share),
    )
    return (
        output_rows.astype(jnp.bfloat16)[None],
        grad_input[None],
        shares[0],
        shares[1],
        shares[2],
        shares[3],
        shares[4],
        shares[5],
        shares[6],
        shares[7],
        shard_in,
        shard_out,
    )


def solution(mesh):
    in_specs = (
        P("wsh", "ctx", None),
        P("wsh", None),
        P("wsh", None),
        P("wsh", None),
        P("wsh", None),
        P("wsh", None),
        P("wsh"),
        P("wsh"),
        P("wsh", None),
        P("ctx", None, "wsh"),
        P("ctx", "wsh", None),
        P("wsh", "ctx", None),
        P(),
        P("wsh", "ctx", None),
    )
    out_specs = (
        P("wsh", "ctx", None),
        P("wsh", "ctx", None),
        P("wsh", None),
        P("wsh", None),
        P("wsh", None),
        P("wsh", None),
        P("wsh", None),
        P("wsh"),
        P("wsh"),
        P("wsh", None),
        P("ctx", None, "wsh"),
        P("ctx", "wsh", None),
    )
    return jax.shard_map(
        per_device, mesh=mesh, in_specs=in_specs, out_specs=out_specs, check_vma=False
    )
```

profile of v0, /device:TPU:0, one launch (start us, length us, event | category | flops | bytes accessed | tf_op | source)
XLA Modules:
  0.0 2785.4 jit_solution(16260398537073955361)
XLA Ops:
  32.6 16.3 all-gather.10.cloned.1.call-done
  78.1 52.9 %all-gather.16.cloned.1.call-done = bf16[2048,768]{1,0:T(8,128)(2,1)} async-done(((bf16[256,768]{1,0:T(8,128)(2,1)}), bf16[2048,768]{1,0:T(8,128)(2,1)}) %all-gather.16.cloned.1.call-update) | async-done | bytes 3145744 | tf_op jit(solution)/shard_map/all_gather | solution.py:146
  141.2 488.5 %while.66 = (s32[]{:T(128)}, f32[12,256]{1,0:T(8,128)S(1)}, f32[12,256]{1,0:T(8,128)}, s32[256]{0:T(256)}, s32[4,512]{1,0:T(4,128)}, /*index=5*/bf16[4,512,12,64...) while((s32[]{:T(128)}, f32[12,256]{1,0:T(8,128)S(1)}, ...), condition=%wide.region_4.5_spmd.clone, body=%wide.region_1.4_spmd.clone.sunk | while | flops 209468464 | bytes 147138896 | solution.py:174
  146.6 26.7 while.72
  181.6 15.9 reshape.885
  208.1 21.8 reshape.886
  269.0 26.7 while.72
  304.0 15.9 reshape.885
  330.3 21.8 reshape.886
  391.1 26.7 while.72
  452.3 21.8 reshape.886
  513.1 26.7 while.72
  574.3 21.8 reshape.886
  645.5 445.5 %while.68 = (s32[]{:T(128)}, f32[512,12,64]{0,2,1:T(8,128)}, bf16[4,512,12,64]{1,3,2,0:T(8,128)(2,1)}, s32[256]{0:T(256)}, s32[4,512]{1,0:T(4,128)}, /*index=5*/...) while((s32[]{:T(128)}, f32[512,12,64]{0,2,1:T(8,128)}, ...), condition=%wide.region_6.7_spmd.clone, body=%wide.region_5.6_spmd.clone.sunk | while | flops 628621376 | bytes 163400000 | solution.py:191
  649.0 21.2 while.73
  704.8 21.8 reshape.890
  760.2 21.2 while.73
  816.0 21.8 reshape.890
  871.4 21.2 while.73
  900.9 15.9 reshape.889
  927.2 21.8 reshape.890
  982.6 21.2 while.73
  1038.4 21.8 reshape.890
  1106.5 17.3 all-to-all-done.3
  1212.7 15.9 all-to-all-done.4
  1240.9 1012.7 %while.71 = (s32[]{:T(128)}, f32[256,12,64]{0,2,1:T(8,128)}, f32[12,4096]{1,0:T(8,128)}, bf16[4,512,12,64]{1,3,2,0:T(8,128)(2,1)}, bf16[4,512,12,64]{1,3,2,0:T(8...) while((s32[]{:T(128)}, f32[256,12,64]{0,2,1:T(8,128)}, ...), condition=%wide.region_21.22_spmd.clone, body=%wide.region_18.21_spmd.clone.sunk | while | flops 1024571456 | bytes 317072576 | solution.py:347
  1244.9 20.7 while.74
  1300.1 21.8 reshape.895
  1380.4 16.0 reshape.899
  1433.4 60.5 %while.75 = (s32[]{:T(128)}, f32[12,4096]{1,0:T(8,128)}, s32[8,2]{0,1:T(2,128)}, f32[8,12,255]{2,1,0:T(8,128)}, s32[]{:T(128)}, /*index=5*/s32[]{:T(128)}) while((s32[]{:T(128)}, f32[12,4096]{1,0:T(8,128)}, s32[8,2]{0,1:T(2,128)}, f32[8,12,255]{2,1,0:T(8,128)}, s32[]{:T(128)}, /*index=5*/s32[]{:T(128)}) %tuple.273), condition=%wide.while_cond.3, body=%wide.while_body.3.sunk | while | flops 6133 | bytes 61335 | solution.py:47
  1497.7 20.7 while.74
  1553.0 21.8 reshape.895
  1633.5 16.0 reshape.899
  1686.5 60.5 %while.75 = (s32[]{:T(128)}, f32[12,4096]{1,0:T(8,128)}, s32[8,2]{0,1:T(2,128)}, f32[8,12,255]{2,1,0:T(8,128)}, s32[]{:T(128)}, /*index=5*/s32[]{:T(128)}) while((s32[]{:T(128)}, f32[12,4096]{1,0:T(8,128)}, s32[8,2]{0,1:T(2,128)}, f32[8,12,255]{2,1,0:T(8,128)}, s32[]{:T(128)}, /*index=5*/s32[]{:T(128)}) %tuple.273), condition=%wide.while_cond.3, body=%wide.while_body.3.sunk | while | flops 6133 | bytes 61335 | solution.py:47
  1750.8 20.7 while.74
  1806.0 21.8 reshape.895
  1886.6 16.0 reshape.899
  1939.5 60.5 %while.75 = (s32[]{:T(128)}, f32[12,4096]{1,0:T(8,128)}, s32[8,2]{0,1:T(2,128)}, f32[8,12,255]{2,1,0:T(8,128)}, s32[]{:T(128)}, /*index=5*/s32[]{:T(128)}) while((s32[]{:T(128)}, f32[12,4096]{1,0:T(8,128)}, s32[8,2]{0,1:T(2,128)}, f32[8,12,255]{2,1,0:T(8,128)}, s32[]{:T(128)}, /*index=5*/s32[]{:T(128)}) %tuple.273), condition=%wide.while_cond.3, body=%wide.while_body.3.sunk | while | flops 6133 | bytes 61335 | solution.py:47
  2003.9 20.7 while.74
  2059.1 21.8 reshape.895
  2139.7 16.0 reshape.899
  2192.6 60.5 %while.75 = (s32[]{:T(128)}, f32[12,4096]{1,0:T(8,128)}, s32[8,2]{0,1:T(2,128)}, f32[8,12,255]{2,1,0:T(8,128)}, s32[]{:T(128)}, /*index=5*/s32[]{:T(128)}) while((s32[]{:T(128)}, f32[12,4096]{1,0:T(8,128)}, s32[8,2]{0,1:T(2,128)}, f32[8,12,255]{2,1,0:T(8,128)}, s32[]{:T(128)}, /*index=5*/s32[]{:T(128)}) %tuple.273), condition=%wide.while_cond.3, body=%wide.while_body.3.sunk | while | flops 6133 | bytes 61335 | solution.py:47
  2273.0 61.4 %reduce-scatter.7.cloned.1.call-done = bf16[256,768]{0,1:T(8,128)(2,1)} async-done(((bf16[2048,768]{0,1:T(8,128)(2,1)}), bf16[256,768]{0,1:T(8,128)(2,1)}) %reduce-scatter.7.cloned.1.call-update) | async-done | bytes 393232 | tf_op jit(solution)/shard_map/reduce_scatter | solution.py:358
  2337.4 75.4 %reduce-scatter.5.cloned.1.call-done = bf16[256,768]{0,1:T(8,128)(2,1)} async-done(((bf16[2048,768]{0,1:T(8,128)(2,1)}), bf16[256,768]{0,1:T(8,128)(2,1)}) %reduce-scatter.5.cloned.1.call-update) | async-done | bytes 393232 | tf_op jit(solution)/shard_map/reduce_scatter | solution.py:352
  2438.4 42.8 %all-reduce.10 = (f32[768,16]{0,1:T(8,128)S(1)}, f32[768]{0:T(1024)S(1)}, f32[768]{0:T(1024)S(1)}, f32[32,12]{1,0:T(8,128)S(1)}) all-reduce(f32[768,16]{0,1:T(8,128)S(1)} %fusion.116, f32[768]{0:T(1024)S(1)} %get-tuple-element.1060, f32[768]{0:T(1024)S(1)} %copy-done.52, ...), channel_id=1, replica_groups=mesh['ctx'=8,'wsh'=4] {'ctx','wsh'}, use_global_device_ids=true, to_apply=%region_29.30 | all-reduce | flops 14208 | bytes 113664 | tf_op jit(solution)/shard_map/psum | solution.py:388
  2484.7 127.4 %all-reduce.15.cloned.1.call-done = (f32[768,768]{1,0:T(8,128)}, f32[768,768]{1,0:T(8,128)}, f32[768,768]{1,0:T(8,128)}, f32[768,768]{1,0:T(8,128)}) async-done(((f32[768,768]{1,0:T(8,128)}, f32[768,768]{1,0:T(8,128)}, f32[768,768]{1,0:T(8,128)}, f32[768,768]{1,0:T(8,128)}), (f32[768,768]{1,0:T(8,128)}, f32[768,768]{1,0:T(8,128)}, f32[768,768]{1,0:T(8,128)}, ...) | async-done | bytes 9437200 | tf_op jit(solution)/shard_map/psum | solution.py:388
  2616.7 76.5 %reduce-scatter.9.cloned.1.call-done = bf16[2,768,768]{2,1,0:T(8,128)(2,1)} async-done(((bf16[2,768,3072]{2,1,0:T(8,128)(2,1)}), bf16[2,768,768]{2,1,0:T(8,128)(2,1)}) %reduce-scatter.9.cloned.1.call-update) | async-done | bytes 2359312 | tf_op jit(solution)/shard_map/reduce_scatter | solution.py:284
  2697.4 77.0 %reduce-scatter.11.cloned.1.call-done = bf16[2,768,768]{2,1,0:T(8,128)(2,1)} async-done(((bf16[2,3072,768]{2,1,0:T(8,128)(2,1)}), bf16[2,768,768]{2,1,0:T(8,128)(2,1)}) %reduce-scatter.11.cloned.1.call-update) | async-done | bytes 2359312 | tf_op jit(solution)/shard_map/reduce_scatter | solution.py:287
  (1101 shorter events, 1831.2 us)
Async XLA Ops:
  7.2 41.6 %copy-start.5 = (bf16[1,256,768]{2,1,0:T(8,128)(2,1)S(1)}, bf16[1,256,768]{2,1,0:T(8,128)(2,1)}, u32[]{:S(2)}) copy-start(bf16[1,256,768]{2,1,0:T(8,128)(2,1)} %param.20) | copy-start | bytes 1179652
  7.2 22.6 all-gather.14.cloned.1.call-start
  7.9 40.9 %all-gather.10.cloned.1.call-start = ((), (), s32[]{:S(2)}) async-start(), calls=%async_computation.9 | async-start | bytes 1474560 | tf_op jit(solution)/shard_map/all_gather | solution.py:118
  8.7 67.4 %all-gather.18.cloned.1.call-start = ((), (), s32[]{:S(2)}) async-start(), calls=%async_computation.13 | async-start | bytes 1474560 | tf_op jit(solution)/shard_map/all_gather | solution.py:116
  9.4 121.6 %all-gather.16.cloned.1.call-start = ((), (), s32[]{:S(2)}) async-start(), calls=%async_computation.12 | async-start | bytes 3538944 | tf_op jit(solution)/shard_map/all_gather | solution.py:146
  21.4 54.7 %copy-start.37 = (f32[768]{0:T(1024)}, f32[768]{0:T(1024)S(1)}, u32[]{:S(2)}) copy-start(f32[768]{0:T(1024)S(1)} %convert_element_type.340) | copy-start | bytes 9220
  23.1 53.1 %copy-start.43 = (f32[256]{0:T(256)}, f32[256]{0:T(256)S(1)}, u32[]{:S(2)}) copy-start(f32[256]{0:T(256)S(1)} %get-tuple-element.1185) | copy-start | bytes 3076
  29.8 22.9 copy-start.45
  32.5 28.2 %copy-start.64 = (s32[8,2]{0,1:T(2,128)S(1)}, s32[8,2]{0,1:T(2,128)}, u32[]{:S(2)}) copy-start(s32[8,2]{0,1:T(2,128)} %param.32) | copy-start | bytes 196
  32.5 30.5 %copy-start.63 = (bf16[8,12]{1,0:T(8,128)(2,1)S(1)}, bf16[8,12]{1,0:T(8,128)(2,1)}, u32[]{:S(2)}) copy-start(bf16[8,12]{1,0:T(8,128)(2,1)} %param.28) | copy-start | bytes 580
  32.5 36.2 %copy-start.60 = (bf16[192,16]{0,1:T(8,128)(2,1)S(1)}, bf16[192,16]{0,1:T(8,128)(2,1)}, u32[]{:S(2)}) copy-start(bf16[192,16]{0,1:T(8,128)(2,1)} %param.25) | copy-start | bytes 18436
  32.5 597.1 %all-gather.12.cloned.1.call-start = ((), (), s32[]{:S(2)}) async-start(), calls=%async_computation.10 | async-start | bytes 3538944 | tf_op jit(solution)/shard_map/all_gather | solution.py:147
  51.4 1041.5 %all-gather.20.cloned.1.call-start = ((), (), s32[]{:S(2)}) async-start(), calls=%async_computation.14 | async-start | bytes 1474560 | tf_op jit(solution)/shard_map/all_gather | solution.py:119
  52.0 1098.2 %all-gather.24.cloned.1.call-start = ((), (), s32[]{:S(2)}) async-start(), calls=%async_computation.16 | async-start | bytes 11796480 | tf_op jit(solution)/shard_map/all_gather | solution.py:241
  54.4 1045.7 %all-to-all-start = ((s32[8,1,2]{2,1,0:T(1,128)}), s32[8,1,2]{2,1,0:T(1,128)}, u32[]{:S(2)}, u32[]{:S(2)}) async-start(s32[8,1,2]{2,1,0:T(1,128)} %bitcast.14), calls=%async_computation | async-start | bytes 8192 | tf_op jit(solution)/shard_map/all_to_all | solution.py:221
  59.9 1099.1 %all-gather.22.cloned.1.call-start = ((), (), s32[]{:S(2)}) async-start(), calls=%async_computation.15 | async-start | bytes 11796480 | tf_op jit(solution)/shard_map/all_gather | solution.py:240
  61.7 14.4 copy-start.39
  1090.9 5.0 copy-start.41
  1092.9 4.7 copy-start.46
  1092.9 5.8 copy-start.16
  1092.9 5.8 copy-start.51
  1097.1 133.3 %copy-start.34 = (f32[256,16]{0,1:T(8,128)}, f32[256,16]{0,1:T(8,128)S(1)}, u32[]{:S(2)}) copy-start(f32[256,16]{0,1:T(8,128)S(1)} %get-tuple-element.1191) | copy-start | bytes 49156
  1100.1 23.7 all-to-all-start.3
  1123.8 24.1 all-to-all-start.1
  1180.2 24.4 all-to-all-start.2
  1204.6 24.0 all-to-all-start.4
  1208.8 1125.6 %reduce-scatter.7.cloned.1.call-start = ((), (), s32[]{:S(2)}) async-start(), calls=%async_computation.18 | async-start | bytes 3538944 | tf_op jit(solution)/shard_map/reduce_scatter | solution.py:358
  1241.1 108.9 %copy-start = (bf16[256,12,64]{0,2,1:T(8,128)(2,1)}, bf16[256,12,64]{0,2,1:T(8,128)(2,1)S(1)}, u32[]{:S(2)}) copy-start(bf16[256,12,64]{0,2,1:T(8,128)(2,1)S(1)} %get-tuple-element.1764) | copy-start | bytes 1179652 | tf_op jit(solution)/shard_map/while
  1241.1 108.9 %copy-start.2 = (bf16[4,512,12,64]{1,3,2,0:T(8,128)(2,1)}, bf16[4,512,12,64]{1,3,2,0:T(8,128)(2,1)S(1)}, u32[]{:S(2)}) copy-start(bf16[4,512,12,64]{1,3,2,0:T(8,128)(2,1)S(1)} %get-tuple-element.1761) | copy-start | bytes 9437188 | tf_op jit(solution)/shard_map/while
  1423.0 70.9 %copy-start.1 = (bf16[256,12,64]{0,2,1:T(8,128)(2,1)S(1)}, bf16[256,12,64]{0,2,1:T(8,128)(2,1)}, u32[]{:S(2)}) copy-start(bf16[256,12,64]{0,2,1:T(8,128)(2,1)} %copy-done) | copy-start | bytes 1179652 | tf_op jit(solution)/shard_map/while
  1423.0 70.9 %copy-start.3 = (bf16[4,512,12,64]{1,3,2,0:T(8,128)(2,1)S(1)}, bf16[4,512,12,64]{1,3,2,0:T(8,128)(2,1)}, u32[]{:S(2)}) copy-start(bf16[4,512,12,64]{1,3,2,0:T(8,128)(2,1)} %copy-done.2) | copy-start | bytes 9437188 | tf_op jit(solution)/shard_map/while
  1493.9 108.9 %copy-start = (bf16[256,12,64]{0,2,1:T(8,128)(2,1)}, bf16[256,12,64]{0,2,1:T(8,128)(2,1)S(1)}, u32[]{:S(2)}) copy-start(bf16[256,12,64]{0,2,1:T(8,128)(2,1)S(1)} %get-tuple-element.1764) | copy-start | bytes 1179652 | tf_op jit(solution)/shard_map/while
  1493.9 108.9 %copy-start.2 = (bf16[4,512,12,64]{1,3,2,0:T(8,128)(2,1)}, bf16[4,512,12,64]{1,3,2,0:T(8,128)(2,1)S(1)}, u32[]{:S(2)}) copy-start(bf16[4,512,12,64]{1,3,2,0:T(8,128)(2,1)S(1)} %get-tuple-element.1761) | copy-start | bytes 9437188 | tf_op jit(solution)/shard_map/while
  1676.1 70.9 %copy-start.1 = (bf16[256,12,64]{0,2,1:T(8,128)(2,1)S(1)}, bf16[256,12,64]{0,2,1:T(8,128)(2,1)}, u32[]{:S(2)}) copy-start(bf16[256,12,64]{0,2,1:T(8,128)(2,1)} %copy-done) | copy-start | bytes 1179652 | tf_op jit(solution)/shard_map/while
  1676.1 70.9 %copy-start.3 = (bf16[4,512,12,64]{1,3,2,0:T(8,128)(2,1)S(1)}, bf16[4,512,12,64]{1,3,2,0:T(8,128)(2,1)}, u32[]{:S(2)}) copy-start(bf16[4,512,12,64]{1,3,2,0:T(8,128)(2,1)} %copy-done.2) | copy-start | bytes 9437188 | tf_op jit(solution)/shard_map/while
  1747.0 108.9 %copy-start = (bf16[256,12,64]{0,2,1:T(8,128)(2,1)}, bf16[256,12,64]{0,2,1:T(8,128)(2,1)S(1)}, u32[]{:S(2)}) copy-start(bf16[256,12,64]{0,2,1:T(8,128)(2,1)S(1)} %get-tuple-element.1764) | copy-start | bytes 1179652 | tf_op jit(solution)/shard_map/while
  1747.0 108.9 %copy-start.2 = (bf16[4,512,12,64]{1,3,2,0:T(8,128)(2,1)}, bf16[4,512,12,64]{1,3,2,0:T(8,128)(2,1)S(1)}, u32[]{:S(2)}) copy-start(bf16[4,512,12,64]{1,3,2,0:T(8,128)(2,1)S(1)} %get-tuple-element.1761) | copy-start | bytes 9437188 | tf_op jit(solution)/shard_map/while
  1929.2 70.9 %copy-start.1 = (bf16[256,12,64]{0,2,1:T(8,128)(2,1)S(1)}, bf16[256,12,64]{0,2,1:T(8,128)(2,1)}, u32[]{:S(2)}) copy-start(bf16[256,12,64]{0,2,1:T(8,128)(2,1)} %copy-done) | copy-start | bytes 1179652 | tf_op jit(solution)/shard_map/while
  1929.2 70.9 %copy-start.3 = (bf16[4,512,12,64]{1,3,2,0:T(8,128)(2,1)S(1)}, bf16[4,512,12,64]{1,3,2,0:T(8,128)(2,1)}, u32[]{:S(2)}) copy-start(bf16[4,512,12,64]{1,3,2,0:T(8,128)(2,1)} %copy-done.2) | copy-start | bytes 9437188 | tf_op jit(solution)/shard_map/while
  2000.1 108.9 %copy-start = (bf16[256,12,64]{0,2,1:T(8,128)(2,1)}, bf16[256,12,64]{0,2,1:T(8,128)(2,1)S(1)}, u32[]{:S(2)}) copy-start(bf16[256,12,64]{0,2,1:T(8,128)(2,1)S(1)} %get-tuple-element.1764) | copy-start | bytes 1179652 | tf_op jit(solution)/shard_map/while
  2000.1 108.9 %copy-start.2 = (bf16[4,512,12,64]{1,3,2,0:T(8,128)(2,1)}, bf16[4,512,12,64]{1,3,2,0:T(8,128)(2,1)S(1)}, u32[]{:S(2)}) copy-start(bf16[4,512,12,64]{1,3,2,0:T(8,128)(2,1)S(1)} %get-tuple-element.1761) | copy-start | bytes 9437188 | tf_op jit(solution)/shard_map/while
  2182.3 70.9 %copy-start.1 = (bf16[256,12,64]{0,2,1:T(8,128)(2,1)S(1)}, bf16[256,12,64]{0,2,1:T(8,128)(2,1)}, u32[]{:S(2)}) copy-start(bf16[256,12,64]{0,2,1:T(8,128)(2,1)} %copy-done) | copy-start | bytes 1179652 | tf_op jit(solution)/shard_map/while
  2182.3 70.9 %copy-start.3 = (bf16[4,512,12,64]{1,3,2,0:T(8,128)(2,1)S(1)}, bf16[4,512,12,64]{1,3,2,0:T(8,128)(2,1)}, u32[]{:S(2)}) copy-start(bf16[4,512,12,64]{1,3,2,0:T(8,128)(2,1)} %copy-done.2) | copy-start | bytes 9437188 | tf_op jit(solution)/shard_map/while
  2260.6 152.3 %reduce-scatter.5.cloned.1.call-start = ((), (), s32[]{:S(2)}) async-start(), calls=%async_computation.17 | async-start | bytes 3538944 | tf_op jit(solution)/shard_map/reduce_scatter | solution.py:352
  2267.7 344.4 %all-reduce.15.cloned.1.call-start = ((), (), s32[]{:S(2)}) async-start(), calls=%async_computation.21 | async-start | bytes 18874368 | tf_op jit(solution)/shard_map/psum | solution.py:388
  2415.9 277.3 %reduce-scatter.9.cloned.1.call-start = ((), (), s32[]{:S(2)}) async-start(), calls=%async_computation.19 | async-start | bytes 11796480 | tf_op jit(solution)/shard_map/reduce_scatter | solution.py:284
  2423.8 350.7 %reduce-scatter.11.cloned.1.call-start = ((), (), s32[]{:S(2)}) async-start(), calls=%async_computation.20 | async-start | bytes 11796480 | tf_op jit(solution)/shard_map/reduce_scatter | solution.py:287
  2437.1 46.6 %copy-start.61 = (f32[256]{0:T(256)S(1)}, f32[256]{0:T(256)}, u32[]{:S(2)}) copy-start(f32[256]{0:T(256)} %get-tuple-element.1184) | copy-start | bytes 3076
  (74 other events, 171.6 us)
Sparse Core Ops, SparseCore 0:
  9.6 20.1 all-gather.13
  31.3 17.4 all-gather.9
  50.4 17.4 all-gather.17
  70.5 60.4 all-gather.15
  133.6 59.0 all-gather.11
  194.1 16.0 all-gather.19
  211.8 64.2 all-gather.23
  277.6 64.2 all-gather.21
  2260.7 73.7 reduce-scatter.6
  2338.5 74.3 reduce-scatter.4
  2419.7 192.3 all-reduce.14
  2614.7 78.4 reduce-scatter.8
  2696.0 78.4 reduce-scatter.10
where the time goes:
time: 2820 us; the launch traced here: 2790 us
  local copies, waits for them, and re-layouts  1680 us (60%)
  waiting for transfers between devices  552 us (20%)
  other arithmetic  260 us (9%)
  matrix products  192 us (7%)
  blocking collectives  61.4 us (2%)
    reshape x16, local copies, waits for them, and re-layouts, one_tile(): widened.reshape(num_heads, block_len, 2 * block_len - 1)  325 us
    gather x288, local copies, waits for them, and re-layouts  274 us
    reshape x16, local copies, waits for them, and re-layouts, one_tile(): widened.reshape(num_heads, 2 * block_len * block_len)  253 us
    transpose x24, local copies, waits for them, and re-layouts, bias_tiles(): jnp.transpose(tile_grid, (2, 0, 3, 1, 4))  208 us
    reshape x20, local copies, waits for them, and re-layouts, bias_tiles(): jnp.transpose(tile_grid, (2, 0, 3, 1, 4))  144 us
    scatter-add x64, other arithmetic  131 us
    psum x1, waiting for transfers between devices, per_device(): lax.psum((grad_wq, grad_wk, grad_wv, grad_wout_attn, grad_router, grad_ga...  127 us
    slice x12, local copies, waits for them, and re-layouts, one_tile(): widened.reshape(num_heads, 2 * block_len * block_len)  125 us
  transfers between devices with their start and end apart: 18, of which 12 were waited for; matrix products, arithmetic and copies ran while one was open for 38% of the time, Pallas kernels for 0%

commit v1 on v0

v1 whole, which is shorter than its diff:
```python
import functools
import math

import jax
import jax.numpy as jnp
import numpy as np
from jax import lax
from jax.experimental import pallas as pl
from jax.experimental.pallas import tpu as pltpu
from jax.sharding import PartitionSpec as P

HEADS = 12
HEAD_DIM = 64
BLOCK = 128
PAIRS = HEADS // 2
NEAR = 2 * BLOCK
SPAN = 3 * BLOCK
epsilon = 1e-06
MASKED = -1e30
bucket_edges = [math.ceil(16 * 8 ** (marker / 16)) for marker in range(1, 16)]
F32 = jnp.float32
BF16 = jnp.bfloat16
HIGH = lax.Precision.HIGHEST


def bucket_of(distance):
    gap = np.maximum(distance, 0)
    count = np.full(gap.shape, 16, np.int32)
    for edge in bucket_edges:
        count = count + (gap >= edge)
    return np.where(gap < 16, gap, count)


def wrapped_lanes():
    lanes = np.arange(SPAN)
    return np.where(lanes < NEAR, lanes, lanes - SPAN)


def onehot_of(distance, buckets):
    return (bucket_of(distance)[:, None] == np.arange(buckets)[None, :]).astype(np.float32)


def dot(left, right, left_dim=1, right_dim=0):
    return lax.dot_general(
        left, right, (((left_dim,), (right_dim,)), ((), ())), preferred_element_type=F32
    )


def lane_ids(rows, lanes):
    return lax.broadcasted_iota(jnp.int32, (rows, lanes), 1)


def stack_heads(rows):
    first = lane_ids(rows.shape[0], BLOCK) < HEAD_DIM
    zero = jnp.zeros_like(rows)
    return jnp.concatenate([jnp.where(first, rows, zero), jnp.where(first, zero, rows)], axis=0)


def merge_heads(stacked):
    half = stacked.shape[0] // 2
    first = lane_ids(half, BLOCK) < HEAD_DIM
    return jnp.where(first, stacked[:half], stacked[half:])


def fold_lanes(tile, combine):
    return combine(tile[:, :BLOCK], tile[:, BLOCK:])


def near_bias(base_ref):
    tiles = []
    for head in range(2):
        row = jnp.broadcast_to(base_ref[0, head : head + 1, :], (BLOCK, SPAN))
        tiles.append(pltpu.roll(row, 0, 1, stride=1, stride_axis=0)[:, :NEAR])
    return jnp.concatenate(tiles, axis=0)


def aligned(row):
    return pl.ds(pl.multiple_of(row * BLOCK, BLOCK), NEAR)


def own_rows_at(block):
    return pl.ds(pl.multiple_of(block * BLOCK, BLOCK), BLOCK)


def project_kernel(source_ref, first_ref, second_ref, gain_ref, wq_ref, wk_ref, wv_ref, out_ref):
    rows = jnp.concatenate([first_ref[...], second_ref[...]], axis=0).astype(F32)
    inv = lax.rsqrt(jnp.mean(rows * rows, axis=-1, keepdims=True) + epsilon)
    normed = (rows * inv * gain_ref[...]).astype(BF16)
    width = wq_ref.shape[1]
    for place, weight in enumerate((wq_ref, wk_ref, wv_ref)):
        out_ref[:, place * width : (place + 1) * width] = dot(normed, weight[...]).astype(BF16)


def project(rows_all, source, gain, wq, wk, wv):
    length, width = rows_all.shape
    steps = (length // BLOCK + 2) // 2
    whole = pl.BlockSpec((width, width), lambda step, src: (0, 0))
    return pl.pallas_call(
        project_kernel,
        grid_spec=pltpu.PrefetchScalarGridSpec(
            num_scalar_prefetch=1,
            grid=(steps,),
            in_specs=[
                pl.BlockSpec((BLOCK, width), lambda step, src: (src[2 * step], 0)),
                pl.BlockSpec((BLOCK, width), lambda step, src: (src[2 * step + 1], 0)),
                pl.BlockSpec((1, width), lambda step, src: (0, 0)),
                whole,
                whole,
                whole,
            ],
            out_specs=pl.BlockSpec((NEAR, 3 * width), lambda step, src: (step, 0)),
        ),
        out_shape=jax.ShapeDtypeStruct((steps * NEAR, 3 * width), BF16),
        compiler_params=pltpu.CompilerParams(vmem_limit_bytes=40 << 20),
        name="project",
    )(source, rows_all, rows_all, gain, wq, wk, wv)


def back_kernel(source_ref, first_ref, second_ref, weight_ref, out_ref):
    rows = jnp.concatenate([first_ref[...], second_ref[...]], axis=0)
    out_ref[...] = dot(rows, weight_ref[...], 1, 1).astype(BF16)


def back_project(rows_all, source, weight):
    length, width = rows_all.shape
    steps = (length // BLOCK + 2) // 2
    return pl.pallas_call(
        back_kernel,
        grid_spec=pltpu.PrefetchScalarGridSpec(
            num_scalar_prefetch=1,
            grid=(steps,),
            in_specs=[
                pl.BlockSpec((BLOCK, width), lambda step, src: (src[2 * step], 0)),
                pl.BlockSpec((BLOCK, width), lambda step, src: (src[2 * step + 1], 0)),
                pl.BlockSpec((width, width), lambda step, src: (0, 0)),
            ],
            out_specs=pl.BlockSpec((NEAR, width), lambda step, src: (step, 0)),
        ),
        out_shape=jax.ShapeDtypeStruct((steps * NEAR, width), BF16),
        compiler_params=pltpu.CompilerParams(vmem_limit_bytes=40 << 20),
        name="back_project",
    )(source, rows_all, rows_all, weight)


def forward_kernel(place_ref, q_ref, k_ref, v_ref, base_ref, out_ref, exact_ref, lse_ref, scores_ref, bias_ref):
    bias_ref[...] = near_bias(base_ref)
    lanes = lane_ids(2 * BLOCK, NEAR)
    for own in range(2):
        block = place_ref[own]
        stacked = stack_heads(q_ref[own_rows_at(block + 1), :])
        scores = dot(stacked, k_ref[aligned(block), :], 1, 1) + bias_ref[...]
        scores = jnp.where(lanes + block * BLOCK < BLOCK, MASKED, scores)
        scores_ref[0] = scores
        chunks = jnp.maximum(block, 1) // 2

        def score_step(chunk, best):
            start = block - 2 * chunk
            part = dot(stacked, k_ref[aligned(start), :], 1, 1)
            part = jnp.where(lanes + start * BLOCK < BLOCK, MASKED, part)
            scores_ref[chunk] = part
            return jnp.maximum(best, fold_lanes(part, jnp.maximum))

        best = lax.fori_loop(1, chunks + 1, score_step, fold_lanes(scores, jnp.maximum))
        top = jnp.max(best, axis=-1, keepdims=True)

        def value_step(chunk, carry):
            total, summed = carry
            weights = jnp.exp(scores_ref[chunk] - top)
            high = weights.astype(BF16)
            low = (weights - high.astype(F32)).astype(BF16)
            values = v_ref[aligned(block - 2 * chunk), :]
            summed = summed + dot(jnp.concatenate([high, low], axis=0), values)
            return (total + fold_lanes(weights, jnp.add), summed)

        total, summed = lax.fori_loop(
            0,
            chunks + 1,
            value_step,
            (jnp.zeros((2 * BLOCK, BLOCK), F32), jnp.zeros((4 * BLOCK, BLOCK), F32)),
        )
        total = jnp.sum(total, axis=-1, keepdims=True)
        main = summed[: 2 * BLOCK] / total
        exact = main + summed[2 * BLOCK :] / total
        rows = pl.ds(own * BLOCK, BLOCK)
        out_ref[rows, :] = merge_heads(main).astype(BF16)
        exact_ref[rows, :] = merge_heads(exact)
        lse_ref[0, own] = jnp.broadcast_to(top + jnp.log(total), (2 * BLOCK, BLOCK))


def pair_specs(rows, width):
    pairs = width // BLOCK

    def column(offset):
        return pl.BlockSpec((rows, BLOCK), lambda pair, place: (0, offset + pair))

    return [column(0), column(pairs), column(2 * pairs)]


def attend_forward(places, qkv, base, width):
    rows = qkv.shape[0]
    chunks = rows // NEAR
    own = pl.BlockSpec((NEAR, BLOCK), lambda pair, place: (0, pair))
    return pl.pallas_call(
        forward_kernel,
        grid_spec=pltpu.PrefetchScalarGridSpec(
            num_scalar_prefetch=1,
            grid=(PAIRS,),
            in_specs=pair_specs(rows, width)
            + [pl.BlockSpec((1, 8, SPAN), lambda pair, place: (pair, 0, 0))],
            out_specs=[
                own,
                own,
                pl.BlockSpec((1, 2, NEAR, BLOCK), lambda pair, place: (pair, 0, 0, 0)),
            ],
            scratch_shapes=[
                pltpu.VMEM((chunks, NEAR, NEAR), F32),
                pltpu.VMEM((NEAR, NEAR), F32),
            ],
        ),
        out_shape=[
            jax.ShapeDtypeStruct((NEAR, width), BF16),
            jax.ShapeDtypeStruct((NEAR, width), F32),
            jax.ShapeDtypeStruct((PAIRS, 2, NEAR, BLOCK), F32),
        ],
        compiler_params=pltpu.CompilerParams(vmem_limit_bytes=40 << 20),
        name="attend_forward",
    )(places, qkv, qkv, qkv, base)


def query_kernel(
    place_ref, q_ref, k_ref, v_ref, base_ref, do_ref, exact_ref, lse_ref, dq_ref, sums_ref, bias_ref, near_ref
):
    bias_ref[...] = near_bias(base_ref)
    lanes = lane_ids(2 * BLOCK, NEAR)
    far = jnp.zeros((2 * BLOCK, BLOCK), F32)
    for own in range(2):
        block = place_ref[own]
        rows = pl.ds(own * BLOCK, BLOCK)
        stacked = stack_heads(q_ref[own_rows_at(block + 1), :])
        grads = stack_heads(do_ref[rows, :])
        exact = exact_ref[rows, :]
        product = grads.astype(F32) * jnp.concatenate([exact, exact], axis=0)
        delta = jnp.sum(product, axis=-1, keepdims=True)
        lse = lse_ref[0, own][:, :1]

        def grad_scores(scores, start):
            weights = jnp.exp(scores - lse)
            return weights * (dot(grads, v_ref[aligned(start), :], 1, 1) - delta)

        scores = dot(stacked, k_ref[aligned(block), :], 1, 1) + bias_ref[...]
        scores = jnp.where(lanes + block * BLOCK < BLOCK, MASKED, scores)
        near = grad_scores(scores, block)
        if own == 0:
            near_ref[...] = near
        else:
            near_ref[...] += near

        def step(chunk, carry):
            grad_q, far = carry
            start = block - 2 * chunk
            keys = k_ref[aligned(start), :]
            part = dot(stacked, keys, 1, 1)
            part = jnp.where(lanes + start * BLOCK < BLOCK, MASKED, part)
            grad_s = grad_scores(part, start)
            return (grad_q + dot(grad_s.astype(BF16), keys), far + fold_lanes(grad_s, jnp.add))

        grad_q, far = lax.fori_loop(
            1,
            jnp.maximum(block, 1) // 2 + 1,
            step,
            (dot(near.astype(BF16), k_ref[aligned(block), :]), far),
        )
        dq_ref[rows, :] = merge_heads(grad_q).astype(BF16)
    row_ids = lax.broadcasted_iota(jnp.int32, (BLOCK, SPAN), 0)
    for head in range(2):
        part = near_ref[head * BLOCK : (head + 1) * BLOCK, :]
        part = jnp.concatenate([part, jnp.zeros((BLOCK, BLOCK), F32)], axis=1)
        for bit in range(BLOCK.bit_length() - 1):
            moved = pltpu.roll(part, SPAN - (1 << bit), 1)
            part = jnp.where((row_ids >> bit) & 1 == 1, moved, part)
        sums_ref[0, head : head + 1, :] = jnp.sum(part, axis=0, keepdims=True)
        far_part = jnp.sum(far[head * BLOCK : (head + 1) * BLOCK], axis=0, keepdims=True)
        sums_ref[0, 2 + head : 3 + head, :] = jnp.concatenate(
            [far_part, jnp.zeros((1, NEAR), F32)], axis=1
        )
    sums_ref[0, 4:8, :] = jnp.zeros((4, SPAN), F32)


def attend_queries(places, qkv, base, grad_out, exact, lse):
    rows, width = qkv.shape[0], grad_out.shape[1]
    own = pl.BlockSpec((NEAR, BLOCK), lambda pair, place: (0, pair))
    row_spec = pl.BlockSpec((1, 8, SPAN), lambda pair, place: (pair, 0, 0))
    return pl.pallas_call(
        query_kernel,
        grid_spec=pltpu.PrefetchScalarGridSpec(
            num_scalar_prefetch=1,
            grid=(PAIRS,),
            in_specs=pair_specs(rows, width)
            + [
                row_spec,
                own,
                own,
                pl.BlockSpec((1, 2, NEAR, BLOCK), lambda pair, place: (pair, 0, 0, 0)),
            ],
            out_specs=[own, row_spec],
            scratch_shapes=[pltpu.VMEM((NEAR, NEAR), F32), pltpu.VMEM((NEAR, NEAR), F32)],
        ),
        out_shape=[
            jax.ShapeDtypeStruct((NEAR, width), BF16),
            jax.ShapeDtypeStruct((PAIRS, 8, SPAN), F32),
        ],
        compiler_params=pltpu.CompilerParams(vmem_limit_bytes=40 << 20),
        name="attend_queries",
    )(places, qkv, qkv, qkv, base, grad_out, exact, lse)


def key_kernel(place_ref, q_ref, k_ref, v_ref, base_ref, do_ref, stats_ref, dk_ref, dv_ref, bias_ref):
    bias_ref[...] = near_bias(base_ref)
    blocks = q_ref.shape[0] // BLOCK - 2
    lanes = lane_ids(2 * BLOCK, NEAR)

    def spread(row, start):
        window = stats_ref[0, row : row + 2, aligned(start)]
        return jnp.concatenate(
            [
                jnp.broadcast_to(window[:1], (BLOCK, NEAR)),
                jnp.broadcast_to(window[1:], (BLOCK, NEAR)),
            ],
            axis=0,
        )

    for own in range(2):
        block = place_ref[own]
        rows = pl.ds(own * BLOCK, BLOCK)
        keys = stack_heads(k_ref[own_rows_at(block + 1), :])
        values = stack_heads(v_ref[own_rows_at(block + 1), :])

        def grads(scores, start):
            queries, grad_out = q_ref[aligned(start), :], do_ref[aligned(start), :]
            scores = jnp.where((start == blocks) & (lanes >= BLOCK), MASKED, scores)
            weights = jnp.exp(scores - spread(0, start))
            grad_s = weights * (dot(values, grad_out, 1, 1) - spread(2, start))
            return dot(grad_s.astype(BF16), queries), dot(weights.astype(BF16), grad_out)

        def step(chunk, carry):
            start = block + 1 + 2 * chunk
            more_k, more_v = grads(dot(keys, q_ref[aligned(start), :], 1, 1), start)
            return (carry[0] + more_k, carry[1] + more_v)

        near = dot(keys, q_ref[aligned(block + 1), :], 1, 1) + bias_ref[...]
        chunks = jnp.maximum(blocks - 1 - block, 0) // 2
        grad_k, grad_v = lax.fori_loop(1, chunks + 1, step, grads(near, block + 1))
        dk_ref[rows, :] = merge_heads(grad_k).astype(BF16)
        dv_ref[rows, :] = merge_heads(grad_v).astype(BF16)


def attend_keys(places, qkv, base, grad_out, stats):
    rows, width = grad_out.shape
    own = pl.BlockSpec((NEAR, BLOCK), lambda pair, place: (0, pair))
    return pl.pallas_call(
        key_kernel,
        grid_spec=pltpu.PrefetchScalarGridSpec(
            num_scalar_prefetch=1,
            grid=(PAIRS,),
            in_specs=pair_specs(rows, width)
            + [
                pl.BlockSpec((1, 8, SPAN), lambda pair, place: (pair, 0, 0)),
                pl.BlockSpec((rows, BLOCK), lambda pair, place: (0, pair)),
                pl.BlockSpec((1, 8, rows), lambda pair, place: (pair, 0, 0)),
            ],
            out_specs=[own, own],
            scratch_shapes=[pltpu.VMEM((NEAR, NEAR), F32)],
        ),
        out_shape=[jax.ShapeDtypeStruct((NEAR, width), BF16)] * 2,
        compiler_params=pltpu.CompilerParams(vmem_limit_bytes=40 << 20),
        name="attend_keys",
    )(places, qkv, qkv, qkv, base, grad_out, stats)


def gelu_tanh(values):
    return jax.nn.gelu(values, approximate=True)


def rms_forward(values, gain_vec):
    inv_rms = lax.rsqrt(jnp.mean(values * values, axis=-1, keepdims=True) + epsilon)
    return (values * inv_rms * gain_vec, inv_rms)


def rms_backward(values, inv_rms, gain_vec, upstream):
    grad_gain = jnp.sum(upstream * values * inv_rms, axis=0)
    scaled = upstream * gain_vec
    grad_values = inv_rms * scaled - values * inv_rms**3 * jnp.mean(
        scaled * values, axis=-1, keepdims=True
    )
    return (grad_values, grad_gain)


def per_device(
    hidden_in,
    w_query,
    w_key,
    w_value,
    w_output,
    w_router,
    gain_attn,
    gain_moe,
    rel_bias,
    w_in,
    w_out,
    routes,
    block_pairs,
    cotangent,
):
    tokens, width = hidden_in.shape[1:]
    ctx_count, wsh_count = lax.axis_size("ctx"), lax.axis_size("wsh")
    ctx_rank, wsh_rank = lax.axis_index("ctx"), lax.axis_index("wsh")
    length = tokens * ctx_count
    blocks = length // BLOCK
    experts, exp_dev = w_router.shape[1], w_in.shape[0]
    slot_most = 2 * tokens // experts
    capacity = (9 * length // (8 * experts) + 7) // 8 * 8

    def over(axis, array, dim=0):
        return lax.all_gather(array, axis, axis=dim, tiled=True)

    rows_all = over("ctx", hidden_in[0])
    small = jnp.concatenate([w_router, gain_attn[:, None], gain_moe[:, None]], axis=1)
    small = jnp.concatenate(
        [small, jnp.pad(rel_bias, ((0, 0), (0, small.shape[1] - HEADS)))], axis=0
    )
    small = lax.all_gather(small, "wsh", axis=0, tiled=False)
    share = width // wsh_count
    vectors = small[:, :share].reshape(width, experts + 2)
    full_router = vectors[:, :experts]
    gain_one = vectors[:, experts].astype(F32)
    gain_two = vectors[:, experts + 1].astype(F32)
    full_bias = small[:, share:, :HEADS].reshape(-1, HEADS)
    full_query, full_key = over("wsh", w_query), over("wsh", w_key)
    full_value, full_output = over("wsh", w_value), over("wsh", w_output)

    order = block_pairs.reshape(-1)
    places = lax.dynamic_slice_in_dim(order, 2 * ctx_rank, 2)
    ids = jnp.arange(blocks, dtype=jnp.int32)
    inverse = jnp.sum(jnp.where(order[None, :] == ids[:, None], ids[None, :], 0), axis=1)
    source = jnp.pad(inverse, (1, 1))

    buckets = full_bias.shape[0]
    lanes = wrapped_lanes()
    query_hot = onehot_of(BLOCK - lanes, buckets)
    key_hot = onehot_of(lanes, buckets)

    def base_rows(hot, distance):
        table = dot(full_bias, jnp.asarray(hot, BF16), 0, 1)
        table = table - full_bias[buckets - 1].astype(F32)[:, None]
        table = jnp.where(jnp.asarray(distance >= 0)[None, :], table, MASKED)
        return jnp.pad(table.reshape(PAIRS, 2, SPAN), ((0, 0), (0, 6), (0, 0)))

    query_base = base_rows(query_hot, BLOCK - lanes)
    key_base = base_rows(key_hot, lanes)

    route_ids = routes[0, :, 0]
    chosen = route_ids[:, None] == jnp.arange(experts, dtype=jnp.int32)[None, :]
    earlier = jnp.asarray(np.tril(np.ones((tokens, tokens), np.float32), -1), BF16)
    before = dot(earlier, chosen.astype(BF16))
    local_rank = jnp.sum(jnp.where(chosen, before, 0.0), axis=-1).astype(jnp.int32)
    counts = lax.all_gather(jnp.sum(chosen.astype(jnp.int32), axis=0), "ctx", axis=0, tiled=False)
    income = lax.dynamic_slice_in_dim(counts, exp_dev * ctx_rank, exp_dev, 1)
    local_slot = route_ids * slot_most + local_rank
    placement = (
        jnp.arange(experts * slot_most, dtype=jnp.int32)[:, None] == local_slot[None, :]
    ).astype(BF16)
    offsets = jnp.cumsum(income, axis=0) - income
    slot_index = jnp.arange(slot_most, dtype=jnp.int32)
    target = offsets.T[:, :, None] + slot_index[None, None, :]
    target = jnp.where(slot_index[None, None, :] < income.T[:, :, None], target, capacity)
    target = target.reshape(exp_dev, ctx_count * slot_most)
    cap_map = (
        target[:, None, :] == jnp.arange(capacity, dtype=jnp.int32)[None, :, None]
    ).astype(BF16)

    def dispatch(rows):
        outgoing = dot(placement, rows).astype(BF16)
        outgoing = outgoing.reshape(ctx_count, exp_dev * slot_most, width)
        incoming = lax.all_to_all(outgoing, "ctx", split_axis=0, concat_axis=0, tiled=True)
        incoming = incoming.reshape(ctx_count, exp_dev, slot_most, width)
        return jnp.stack(
            [
                dot(cap_map[e], incoming[:, e].reshape(ctx_count * slot_most, width)).astype(BF16)
                for e in range(exp_dev)
            ]
        )

    def bring_back(slots):
        returning = jnp.stack(
            [
                dot(cap_map[e], slots[e], 0, 0)
                .astype(BF16)
                .reshape(ctx_count, slot_most, width)
                for e in range(exp_dev)
            ],
            axis=1,
        ).reshape(ctx_count, exp_dev * slot_most, width)
        returned = lax.all_to_all(returning, "ctx", split_axis=0, concat_axis=0, tiled=True)
        return dot(placement, returned.reshape(experts * slot_most, width), 0, 0)

    def spread_slots(slots):
        return jnp.swapaxes(
            lax.all_gather(slots, "wsh", axis=0, tiled=False), 0, 1
        ).reshape(exp_dev, wsh_count * capacity, width)

    def sum_slots(parts):
        parts = parts.astype(BF16).reshape(exp_dev, wsh_count, capacity, width)
        return lax.psum_scatter(jnp.swapaxes(parts, 0, 1), "wsh", scatter_dimension=0, tiled=False)

    grad_rows = cotangent[0]
    own_g = dispatch(grad_rows)
    all_g = spread_slots(own_g)

    qkv = project(rows_all, source, gain_one[None, :], full_query, full_key, full_value)
    attn_low, attn_exact, lse = attend_forward(places, qkv, query_base, width)

    resid_in = hidden_in[0].astype(F32)
    resid_mid = resid_in + dot(attn_low, full_output)
    normed_two, inv_two = rms_forward(resid_mid, gain_two)
    normed_two = normed_two.astype(BF16)
    own_x = dispatch(normed_two)
    all_x = spread_slots(own_x)

    expert_ids = exp_dev * ctx_rank + jnp.arange(exp_dev, dtype=jnp.int32)
    expert_hot = (
        expert_ids[:, None] == jnp.arange(experts, dtype=jnp.int32)[None, :]
    ).astype(F32)[:, None, :]

    def router(rows):
        logits = jnp.einsum("ecd,dr->ecr", rows, full_router, preferred_element_type=F32)
        probs = jax.nn.softmax(logits, axis=-1)
        return probs, jnp.sum(probs * expert_hot, axis=-1, keepdims=True)

    gate_all = router(all_x)[1]
    grad_slots = (gate_all * all_g.astype(F32)).astype(BF16)
    pre_act = jnp.einsum("ecd,edf->ecf", all_x, w_in, preferred_element_type=F32)
    hidden_act = gelu_tanh(pre_act).astype(BF16)
    out_part = jnp.einsum("ecf,efd->ecd", hidden_act, w_out, preferred_element_type=F32)
    own_out = sum_slots(out_part)
    grad_hidden = jnp.einsum("ecd,efd->ecf", grad_slots, w_out, preferred_element_type=F32)
    grad_pre = jax.vjp(gelu_tanh, pre_act)[1](grad_hidden)[0].astype(BF16)
    in_part = jnp.einsum("ecf,edf->ecd", grad_pre, w_in, preferred_element_type=F32)
    own_dx = sum_slots(in_part)
    grad_w_out = jnp.einsum("ecf,ecd->efd", hidden_act, grad_slots, preferred_element_type=F32)
    grad_w_in = jnp.einsum("ecd,ecf->edf", all_x, grad_pre, preferred_element_type=F32)

    probs, gate_own = router(own_x)
    grad_gate = jnp.sum(own_g.astype(F32) * own_out.astype(F32), axis=-1, keepdims=True)
    grad_logits = (gate_own * grad_gate * (expert_hot - probs)).astype(BF16)
    grad_router = jnp.einsum("ecd,ecr->dr", own_x, grad_logits, preferred_element_type=F32)
    grad_slots_in = own_dx.astype(F32) + jnp.einsum(
        "ecr,dr->ecd", grad_logits, full_router, preferred_element_type=F32
    )
    grad_normed_two = bring_back(grad_slots_in.astype(BF16))
    token_out = bring_back(own_out)

    logits = dot(normed_two, full_router)
    gate_val = jnp.sum(jnp.where(chosen, jax.nn.softmax(logits, axis=-1), 0.0), axis=-1)
    output_rows = resid_mid + gate_val[:, None] * token_out

    upstream = grad_rows.astype(F32)
    grad_mid_norm, grad_gain_m = rms_backward(resid_mid, inv_two, gain_two, grad_normed_two)
    grad_mid = upstream + grad_mid_norm
    grad_branch = grad_mid.astype(BF16)
    branch_all = over("ctx", grad_branch)
    grad_wo = dot(attn_low, grad_branch, 0, 0)
    grad_heads = dot(grad_branch, full_output, 1, 1).astype(BF16)
    head_hot = jnp.asarray(
        (np.arange(width)[:, None] // HEAD_DIM == np.arange(HEADS)[None, :]).astype(np.float32)
    )
    delta = jnp.dot(grad_heads.astype(F32) * attn_exact, head_hot, precision=HIGH)
    lse_rows = lse[..., 0].reshape(PAIRS, 2, 2, BLOCK)
    lse_rows = jnp.transpose(lse_rows, (1, 0, 2, 3))
    delta_rows = jnp.transpose(delta.T.reshape(PAIRS, 2, 2, BLOCK), (2, 0, 1, 3))
    stats = jnp.concatenate([lse_rows, delta_rows], axis=2)
    stats = over("ctx", stats)
    stats = jnp.transpose(jnp.take(stats, source, axis=0), (1, 2, 0, 3))
    stats = jnp.pad(
        stats.reshape(PAIRS, 4, (blocks + 2) * BLOCK), ((0, 0), (0, 4), (0, 0))
    )

    grad_q, sums = attend_queries(places, qkv, query_base, grad_heads, attn_exact, lse)
    near_sums = sums[:, :2].reshape(HEADS, SPAN)
    far_sums = jnp.sum(sums[:, 2:4].reshape(HEADS, SPAN), axis=1)
    grad_table = jnp.dot(jnp.asarray(query_hot.T), near_sums.T, precision=HIGH)
    grad_table = grad_table.at[buckets - 1].add(far_sums)

    heads_all = back_project(branch_all, source, full_output)
    grad_k, grad_v = attend_keys(places, qkv, key_base, heads_all, stats)

    normed_one, inv_one = rms_forward(resid_in, gain_one)
    normed_one = normed_one.astype(BF16)
    grad_normed_one = dot(grad_q, full_query, 1, 1)
    grad_normed_one = grad_normed_one + dot(grad_k, full_key, 1, 1)
    grad_normed_one = grad_normed_one + dot(grad_v, full_value, 1, 1)
    grad_in_norm, grad_gain_a = rms_backward(resid_in, inv_one, gain_one, grad_normed_one)
    grad_input = (grad_mid + grad_in_norm).astype(BF16)

    def reduce_weight(grad):
        part = lax.psum_scatter(grad.astype(BF16), "wsh", scatter_dimension=0, tiled=True)
        return lax.psum(part, "ctx").astype(F32)

    grad_wq = dot(normed_one, grad_q, 0, 0)
    grad_wk = dot(normed_one, grad_k, 0, 0)
    grad_wv = dot(normed_one, grad_v, 0, 0)
    shares = [reduce_weight(grad) for grad in (grad_wq, grad_wk, grad_wv, grad_wo)]
    columns = jnp.concatenate(
        [grad_router, grad_gain_a[:, None], grad_gain_m[:, None]], axis=1
    )
    table = jnp.pad(grad_table, ((0, 0), (0, columns.shape[1] - HEADS)))
    summed = lax.psum(jnp.concatenate([columns, table], axis=0), ("ctx", "wsh"))
    own_columns = lax.dynamic_slice_in_dim(summed[:width], wsh_rank * share, share, 0)
    bucket_share = buckets // wsh_count
    own_table = lax.dynamic_slice_in_dim(
        summed[width:, :HEADS], wsh_rank * bucket_share, bucket_share, 0
    )
    return (
        output_rows.astype(BF16)[None],
        grad_input[None],
        *shares,
        own_columns[:, :experts],
        own_columns[:, experts],
        own_columns[:, experts + 1],
        own_table,
        grad_w_in,
        grad_w_out,
    )


def solution(mesh):
    in_specs = (
        P("wsh", "ctx", None),
        P("wsh", None),
        P("wsh", None),
        P("wsh", None),
        P("wsh", None),
        P("wsh", None),
        P("wsh"),
        P("wsh"),
        P("wsh", None),
        P("ctx", None, "wsh"),
        P("ctx", "wsh", None),
        P("wsh", "ctx", None),
        P(),
        P("wsh", "ctx", None),
    )
    out_specs = (
        P("wsh", "ctx", None),
        P("wsh", "ctx", None),
        P("wsh", None),
        P("wsh", None),
        P("wsh", None),
        P("wsh", None),
        P("wsh", None),
        P("wsh"),
        P("wsh"),
        P("wsh", None),
        P("ctx", None, "wsh"),
        P("ctx", "wsh", None),
    )
    return jax.shard_map(
        per_device, mesh=mesh, in_specs=in_specs, out_specs=out_specs, check_vma=False
    )
```

time: 2820 us -> 618 us (0.22); the launches traced: 2790 us -> 617 us
  local copies, waits for them, and re-layouts: 1680 us -> 48.8 us
  waiting for transfers between devices: 552 us -> 211 us
  other arithmetic: 260 us -> 27.8 us
  matrix products: 192 us -> 57.9 us
  Pallas kernels: 0 us -> 105 us
  blocking collectives: 61.4 us -> 138 us
    reshape x55 -> x9, local copies, waits for them, and re-layouts: 734 us -> 5.61 us  [the longest x2 2.68 us: sum_slots(): parts = parts.astype(BF16).reshape(exp_dev, wsh_count, capacity, width)]
    gather x288 -> x1, local copies, waits for them, and re-layouts: 274 us -> 0.8 us  [per_device(): stats = jnp.transpose(jnp.take(stats, source, axis=0), (1, 2, 0, 3))]
    reduce_scatter x4 -> x6, waiting for transfers between devices: 290 us -> 72.3 us  [the longest x2 55.4 us: sum_slots(): lax.psum_scatter(jnp.swapaxes(parts, 0, 1), 'wsh', scatter_dimension=0, t...]
    transpose x24 -> x3, local copies, waits for them, and re-layouts: 208 us -> 0.24 us  [the longest x2 0.16 us: per_device(): income.T[:, :, None]]
    scatter-add x64 -> x0, other arithmetic: 131 us -> none
    slice x26 -> x10, local copies, waits for them, and re-layouts: 129 us -> 3.87 us  [the longest x2 1.25 us: dispatch(): incoming[:, e].reshape(ctx_count * slot_most, width)]
    dot_general x58 -> x35, matrix products: 166 us -> 48.2 us  [the longest x25 27.7 us: dot(): lax.dot_general(left, right, (((left_dim,), (right_dim,)), ((), ())), pre...]
    scatter-add x96 -> x1, local copies, waits for them, and re-layouts: 111 us -> 0.78 us  [per_device(): grad_table = grad_table.at[buckets - 1].add(far_sums)]
  transfers between devices with their start and end apart: 18 -> 17, of which waited for: 12 -> 8; matrix products, arithmetic and copies ran while one was open for 38% -> 13% of each run, Pallas kernels for 0% -> 17%
where the time goes in v1:
time: 618 us; the launch traced here: 617 us
  waiting for transfers between devices  211 us (34%)
  blocking collectives  138 us (22%)
  Pallas kernels  105 us (17%)
  matrix products  57.9 us (9%)
  local copies, waits for them, and re-layouts  48.8 us (8%)
  other arithmetic  27.8 us (4%)
  between operations  15.7 us (3%)
  starting transfers between devices  12.8 us (2%)
    all_gather x6, waiting for transfers between devices, over(): return lax.all_gather(array, axis, axis=dim, tiled=True)  83.5 us
    reduce_scatter x2, waiting for transfers between devices, sum_slots(): lax.psum_scatter(jnp.swapaxes(parts, 0, 1), 'wsh', scatter_dimension=0, t...  55.4 us
    psum x1, blocking collectives, per_device(): summed = lax.psum(jnp.concatenate([columns, table], axis=0), ('ctx', 'wsh'))  41.3 us
    psum x1, waiting for transfers between devices, reduce_weight(): return lax.psum(part, 'ctx').astype(F32)  36.5 us
    pallas_call x1, Pallas kernels, attend_queries(): pl.pallas_call(query_kernel, grid_spec=pltpu.PrefetchScalarGridSpec(num_s...  33.6 us
    all_gather x1, blocking collectives, over(): return lax.all_gather(array, axis, axis=dim, tiled=True)  30.6 us
    pallas_call x1, Pallas kernels, attend_forward(): pl.pallas_call(forward_kernel, grid_spec=pltpu.PrefetchScalarGridSpec(num...  29.5 us
    dot_general x25, matrix products, dot(): lax.dot_general(left, right, (((left_dim,), (right_dim,)), ((), ())), pre...  27.7 us
  transfers between devices with their start and end apart: 17, of which 8 were waited for; matrix products, arithmetic and copies ran while one was open for 13% of the time, Pallas kernels for 17%

profile of v1, /device:TPU:0, one launch (start us, length us, event | category | flops | bytes accessed | tf_op | source)
XLA Modules:
  0.0 616.6 jit_solution(3377786333432351633)
XLA Ops:
  12.5 2.3 convolution_convert_fusion.6
  14.7 7.3 %all-to-all-start.2 = ((bf16[8,64,768]{2,1,0:T(8,128)(2,1)}), bf16[8,64,768]{2,1,0:T(8,128)(2,1)}, u32[]{:S(2)}, u32[]{:S(2)}) async-start(bf16[8,64,768]{2,1,0:T(8,128)(2,1)} %bitcast.35), calls=%async_computation.3 | async-start | bytes 1572864 | tf_op jit(solution)/shard_map/all_to_all | solution.py:484
  23.0 5.4 all-gather.5
  32.0 11.8 %all-reduce.7 = s32[8,16]{1,0:T(8,128)S(1)} all-reduce(s32[8,16]{1,0:T(8,128)S(1)} %reshape.328), channel_id=4, replica_groups=mesh['ctx'=8,'wsh'=4] {'ctx'}, use_global_device_ids=true, to_apply=%add.6 | all-reduce | flops 128 | bytes 1024
  47.4 1.8 all-gather.17.cloned.1.call-done.wk_ref
  49.2 19.1 %all-gather.19.cloned.1.call-done.wv_ref = bf16[768,768]{1,0:T(8,128)(2,1)} async-done(((bf16[192,768]{1,0:T(8,128)(2,1)}), bf16[768,768]{1,0:T(8,128)(2,1)}) %all-gather.19.cloned.1.call-update) | async-done | bytes 1179664 | tf_op jit(solution)/shard_map/all_gather | solution.py:424
  68.3 62.5 %all-gather.25.cloned.1.call-done = bf16[1,2048,768]{2,1,0:T(8,128)(2,1)} async-done(((bf16[1,256,768]{2,1,0:T(8,128)(2,1)}), bf16[1,2048,768]{2,1,0:T(8,128)(2,1)}) %all-gather.25.cloned.1.call-update) | async-done | bytes 3145744 | tf_op jit(solution)/shard_map/all_gather | solution.py:424
  130.8 1.9 copy-done.4
  136.5 12.5 %project.1.q_ref.k_ref.v_ref = bf16[2304,2304]{1,0:T(8,128)(2,1)} custom-call(s32[18]{0:T(128)S(1)} %pad.25.source_ref, bf16[2048,768]{1,0:T(8,128)(2,1)S(1)} %bitcast.202, bf16[2048,768]{1,0:T(8,128)(2,1)S(1)} %bitcast.203, f32[1,768]{1,0:T(1,128)S(1)} %fusion.68.gain_ref, bf16[768,768]{1,0:T(8,128)(2,1)S(1)} %copy-done.13, ...), custom_call_target="tpu_custom_call" | custom-call | tf_op jit(solution)/shard_map/project/pallas_call | solution.py:98
  149.0 4.0 copy-done.2
  153.1 29.5 %attend_forward.1 = (bf16[256,768]{1,0:T(8,128)(2,1)S(1)}, f32[256,768]{1,0:T(8,128)S(1)}, f32[6,2,256,128]{3,2,1,0:T(8,128)S(1)}) custom-call(s32[2]{0:T(128)S(1)} %dynamic_slice.12.place_ref, bf16[2304,2304]{1,0:T(8,128)(2,1)S(1)} %copy-done.2, bf16[2304,2304]{1,0:T(8,128)(2,1)S(1)} %copy-done.2, bf16[2304,2304]{1,0:T(8,128)(2,1)S(1)} %copy-done.2, ...), custom_call_target="tpu_custom_call" | custom-call | tf_op jit(solution)/shard_map/attend_forward/pallas_call | solution.py:203
  184.6 2.1 multiply_reduce_fusion.2
  187.9 23.3 %all_to_all.20 = bf16[8,64,768]{2,1,0:T(8,128)(2,1)S(1)} all-to-all(bf16[8,64,768]{2,1,0:T(8,128)(2,1)S(1)} %bitcast.209), channel_id=1, replica_groups=mesh['ctx'=8,'wsh'=4] {'ctx'}, dimensions={0} | all-to-all | bytes 1572864 | tf_op jit(solution)/shard_map/all_to_all | solution.py:484
  214.5 1.8 convert_bitcast_fusion
  216.3 2.0 copy.116
  218.3 15.2 %all-gather.27.cloned.1.call-done = bf16[8,144,768]{2,1,0:T(8,128)(2,1)} async-done(((bf16[2,144,768]{2,1,0:T(8,128)(2,1)}), bf16[8,144,768]{2,1,0:T(8,128)(2,1)}) %all-gather.27.cloned.1.call-update) | async-done | bytes 1769488 | tf_op jit(solution)/shard_map/all_gather | solution.py:508
  233.5 2.8 copy.112
  236.3 2.1 fusion.89
  238.5 2.4 fusion.11
  243.3 4.3 fusion.10
  247.6 1.8 convolution_convert_fusion.1
  250.8 3.0 convolution_convert_fusion
  255.9 24.5 %reduce-scatter.7.cloned.1.call-done = bf16[1,2,144,768]{3,2,1,0:T(8,128)(2,1)} async-done(((bf16[4,2,144,768]{3,2,1,0:T(8,128)(2,1)}), bf16[1,2,144,768]{3,2,1,0:T(8,128)(2,1)}) %reduce-scatter.7.cloned.1.call-update) | async-done | bytes 442384 | tf_op jit(solution)/shard_map/reduce_scatter | solution.py:513
  281.6 31.0 %reduce-scatter.9.cloned.1.call-done = bf16[1,2,144,768]{3,2,1,0:T(8,128)(2,1)} async-done(((bf16[4,2,144,768]{3,2,1,0:T(8,128)(2,1)}), bf16[1,2,144,768]{3,2,1,0:T(8,128)(2,1)}) %reduce-scatter.9.cloned.1.call-update) | async-done | bytes 442384 | tf_op jit(solution)/shard_map/reduce_scatter | solution.py:513
  314.7 25.6 %all_to_all.21 = bf16[8,64,768]{2,1,0:T(8,128)(2,1)S(1)} all-to-all(bf16[8,64,768]{2,1,0:T(8,128)(2,1)S(1)} %bitcast.208), channel_id=1, replica_groups=mesh['ctx'=8,'wsh'=4] {'ctx'}, dimensions={0} | all-to-all | bytes 1572864 | tf_op jit(solution)/shard_map/all_to_all | solution.py:503
  346.3 4.4 copy-done.3
  352.8 33.6 %attend_queries.1 = (bf16[256,768]{1,0:T(8,128)(2,1)S(1)}, f32[6,8,384]{2,1,0:T(8,128)S(1)}) custom-call(s32[2]{0:T(128)S(1)} %dynamic_slice.12.place_ref, bf16[2304,2304]{1,0:T(8,128)(2,1)S(1)} %copy-done.3, bf16[2304,2304]{1,0:T(8,128)(2,1)S(1)} %copy-done.3, bf16[2304,2304]{1,0:T(8,128)(2,1)S(1)} %copy-done.3, f32[6,8,384]{2,1,0:T(8,128)S(1)} %copy-done.19, ...), custom_call_target="tpu_custom_call" | custom-call | tf_op jit(solution)/shard_map/attend_queries/pallas_call | solution.py:293
  388.7 2.7 convolution_convert_fusion.2
  391.5 1.7 fusion.27
  399.7 2.0 fusion.41
  401.8 30.6 %all_gather.59 = f32[16,6,4,128]{3,2,1,0:T(4,128)S(1)} all-gather(f32[2,6,4,128]{3,2,1,0:T(4,128)S(1)} %copy.121), channel_id=1, replica_groups=mesh['ctx'=8,'wsh'=4] {'ctx'}, dimensions={0}, use_global_device_ids=true | all-gather | bytes 221184 | tf_op jit(solution)/shard_map/all_gather | solution.py:424
  433.4 1.9 copy-done.5
  435.3 5.2 back_project.1.do_ref
  440.5 24.1 %attend_keys.1 = (bf16[256,768]{1,0:T(8,128)(2,1)S(1)}, bf16[256,768]{1,0:T(8,128)(2,1)S(1)}) custom-call(s32[2]{0:T(128)S(1)} %dynamic_slice.12.place_ref, bf16[2304,2304]{1,0:T(8,128)(2,1)} %project.1.q_ref.k_ref.v_ref, bf16[2304,2304]{1,0:T(8,128)(2,1)} %project.1.q_ref.k_ref.v_ref, bf16[2304,2304]{1,0:T(8,128)(2,1)} %project.1.q_ref.k_ref.v_ref, ...), custom_call_target="tpu_custom_call" | custom-call | tf_op jit(solution)/shard_map/attend_keys/pallas_call | solution.py:360
  464.7 1.6 convolution_convert_fusion.4
  469.0 4.2 all-to-all-start.1
  475.2 7.3 %fusion.84 = f32[2,768,768]{2,1,0:T(8,128)} fusion(bf16[2,576,768]{2,1,0:T(8,128)(2,1)} %copy-done.37, f32[2,576,768]{2,1,0:T(8,128)} %copy-done.86), kind=kOutput, calls=%fused_computation.171 | convolution fusion | flops 1366917120 | bytes 10027008 | tf_op jit(solution)/shard_map/ecf,ecd->efd/dot_general | solution.py:549
  482.6 4.2 fusion.100
  487.8 1.6 slice_reduce_fusion.1
  497.1 2.7 fusion.15
  501.8 16.8 %reduce-scatter.15.cloned.1.call-done = bf16[192,768]{1,0:T(8,128)(2,1)} async-done(((bf16[768,768]{1,0:T(8,128)(2,1)}), bf16[192,768]{1,0:T(8,128)(2,1)}) %reduce-scatter.15.cloned.1.call-update) | async-done | bytes 294928 | tf_op jit(solution)/shard_map/reduce_scatter | solution.py:605
  518.7 2.6 fusion.40
  521.3 41.3 %psum.39 = f32[800,18]{0,1:T(8,128)S(1)} all-reduce(f32[800,18]{0,1:T(8,128)S(1)} %select_maximum_fusion), channel_id=1, replica_groups=mesh['ctx'=8,'wsh'=4] {'ctx','wsh'}, use_global_device_ids=true, to_apply=%region_31.32 | all-reduce | flops 14400 | bytes 115200 | tf_op jit(solution)/shard_map/psum | solution.py:616
  564.7 2.5 fusion.45
  567.3 36.5 %all-reduce.11.cloned.1.call-done = (bf16[192,768]{1,0:T(8,128)(2,1)}, bf16[192,768]{1,0:T(8,128)(2,1)}, bf16[192,768]{1,0:T(8,128)(2,1)}, bf16[192,768]{1,0:T(8,128)(2,1)}) async-done(((bf16[192,768]{1,0:T(8,128)(2,1)}, bf16[192,768]{1,0:T(8,128)(2,1)}, bf16[192,768]{1,0:T(8,128)(2,1)}, bf16[192,768]{1,0:T(8,128)(2,1)}), (bf16[192,768]{1,0:T(8,128)(2,1)}, bf16[192,768]{1,0:T(8,128)(2,1)}, ...) | async-done | bytes 1179664 | tf_op jit(solution)/shard_map/psum | solution.py:606
  603.7 1.9 convert_element_type.241
  605.6 1.8 convert_element_type.243
  607.4 1.8 convert_element_type.245
  (320 shorter events, 67.8 us)
Async XLA Ops:
  7.2 235.6 %copy-start = (bf16[2,768,768]{2,1,0:T(8,128)(2,1)S(1)}, bf16[2,768,768]{2,1,0:T(8,128)(2,1)}, u32[]{:S(2)}) copy-start(bf16[2,768,768]{2,1,0:T(8,128)(2,1)} %param.32) | copy-start | bytes 7077892
  7.2 22.0 %copy-start.80 = (bf16[384,32]{1,0:T(8,128)(2,1)S(1)}, bf16[384,32]{1,0:T(8,128)(2,1)}, u32[]{:S(2)}) copy-start(bf16[384,32]{1,0:T(8,128)(2,1)} %constant.117.clone) | copy-start | bytes 73732
  7.2 22.0 %copy-start.84 = (pred[384]{0:T(512)(128)(4,1)S(1)}, pred[384]{0:T(512)(128)(4,1)}, u32[]{:S(2)}) copy-start(pred[384]{0:T(512)(128)(4,1)} %constant.118.clone) | copy-start | bytes 1156
  7.3 40.1 %all-gather.15.cloned.1.call-start = ((), (), s32[]{:S(2)}) async-start(), calls=%async_computation.10 | async-start | bytes 1474560 | tf_op jit(solution)/shard_map/all_gather | solution.py:424
  8.0 22.3 %copy-start.82 = (u32[32]{0:T(128)S(1)}, u32[32]{0:T(128)}, u32[]{:S(2)}) copy-start(u32[32]{0:T(128)} %constant.143) | copy-start | bytes 388
  8.0 23.5 %copy-start.62 = (s32[1,256,1]{1,2,0:T(1,128)S(1)}, s32[1,256,1]{1,2,0:T(1,128)}, u32[]{:S(2)}) copy-start(s32[1,256,1]{1,2,0:T(1,128)} %param.34) | copy-start | bytes 3076
  8.0 41.2 %all-gather.17.cloned.1.call-start = ((), (), s32[]{:S(2)}) async-start(), calls=%async_computation.11 | async-start | bytes 1474560 | tf_op jit(solution)/shard_map/all_gather | solution.py:424
  8.8 59.5 %all-gather.19.cloned.1.call-start = ((), (), s32[]{:S(2)}) async-start(), calls=%async_computation.12 | async-start | bytes 1474560 | tf_op jit(solution)/shard_map/all_gather | solution.py:424
  9.5 121.3 %all-gather.25.cloned.1.call-start = ((), (), s32[]{:S(2)}) async-start(), calls=%async_computation.21 | async-start | bytes 3538944 | tf_op jit(solution)/shard_map/all_gather | solution.py:424
  14.7 30.0 %all-to-all-start.2 = ((bf16[8,64,768]{2,1,0:T(8,128)(2,1)}), bf16[8,64,768]{2,1,0:T(8,128)(2,1)}, u32[]{:S(2)}, u32[]{:S(2)}) async-start(bf16[8,64,768]{2,1,0:T(8,128)(2,1)} %bitcast.35), calls=%async_computation.3 | async-start | bytes 1572864 | tf_op jit(solution)/shard_map/all_to_all | solution.py:484
  22.0 162.6 %all-gather.21.cloned.1.call-start = ((), (), s32[]{:S(2)}) async-start(), calls=%async_computation.13 | async-start | bytes 1474560 | tf_op jit(solution)/shard_map/all_gather | solution.py:424
  22.6 191.9 %all-gather.29.cloned.1.call-start = ((), (), s32[]{:S(2)}) async-start(), calls=%async_computation.23 | async-start | bytes 2211840 | tf_op jit(solution)/shard_map/all_gather | solution.py:508
  44.6 104.4 %copy-start.18 = (f32[6,8,384]{2,1,0:T(8,128)}, f32[6,8,384]{2,1,0:T(8,128)S(1)}, u32[]{:S(2)}) copy-start(f32[6,8,384]{2,1,0:T(8,128)S(1)} %pad.27.base_ref) | copy-start | bytes 221188
  44.8 86.1 %copy-start.31 = (pred[2,144,256]{2,1,0:T(8,128)(4,1)}, pred[2,144,256]{2,1,0:T(8,128)(4,1)S(1)}, u32[]{:S(2)}) copy-start(pred[2,144,256]{2,1,0:T(8,128)(4,1)S(1)} %iota_compare_fusion.5) | copy-start | bytes 221188
  46.2 84.6 %copy-start.27 = (bf16[1,144,768]{2,1,0:T(8,128)(2,1)}, bf16[1,144,768]{2,1,0:T(8,128)(2,1)S(1)}, u32[]{:S(2)}) copy-start(bf16[1,144,768]{2,1,0:T(8,128)(2,1)S(1)} %fusion.19) | copy-start | bytes 663556
  46.5 102.6 %copy-start.29 = (bf16[1,144,768]{2,1,0:T(8,128)(2,1)}, bf16[1,144,768]{2,1,0:T(8,128)(2,1)S(1)}, u32[]{:S(2)}) copy-start(bf16[1,144,768]{2,1,0:T(8,128)(2,1)S(1)} %fusion.18) | copy-start | bytes 663556
  47.3 186.2 %all-gather.27.cloned.1.call-start = ((), (), s32[]{:S(2)}) async-start(), calls=%async_computation.22 | async-start | bytes 2211840 | tf_op jit(solution)/shard_map/all_gather | solution.py:508
  184.6 31.7 %copy-start.17 = (bf16[256,768]{1,0:T(8,128)(2,1)}, bf16[256,768]{1,0:T(8,128)(2,1)S(1)}, u32[]{:S(2)}) copy-start(bf16[256,768]{1,0:T(8,128)(2,1)S(1)} %get-tuple-element.31) | copy-start | bytes 1179652
  186.7 154.8 %copy-start.22 = (f32[256,768]{1,0:T(8,128)}, f32[256,768]{1,0:T(8,128)S(1)}, u32[]{:S(2)}) copy-start(f32[256,768]{1,0:T(8,128)S(1)} %get-tuple-element.125) | copy-start | bytes 2359300
  187.3 23.9 %copy-start.32 = (pred[2,144,256]{2,1,0:T(8,128)(4,1)S(1)}, pred[2,144,256]{2,1,0:T(8,128)(4,1)}, u32[]{:S(2)}) copy-start(pred[2,144,256]{2,1,0:T(8,128)(4,1)} %copy-done.31) | copy-start | bytes 221188
  213.6 66.7 %reduce-scatter.7.cloned.1.call-start = ((), (), s32[]{:S(2)}) async-start(), calls=%async_computation.14 | async-start | bytes 2211840 | tf_op jit(solution)/shard_map/reduce_scatter | solution.py:513
  250.8 61.7 %reduce-scatter.9.cloned.1.call-start = ((), (), s32[]{:S(2)}) async-start(), calls=%async_computation.15 | async-start | bytes 2211840 | tf_op jit(solution)/shard_map/reduce_scatter | solution.py:513
  255.3 25.1 %copy-start.28 = (bf16[1,144,768]{2,1,0:T(8,128)(2,1)S(1)}, bf16[1,144,768]{2,1,0:T(8,128)(2,1)}, u32[]{:S(2)}) copy-start(bf16[1,144,768]{2,1,0:T(8,128)(2,1)} %copy-done.27) | copy-start | bytes 663556
  255.3 25.1 %copy-start.30 = (bf16[1,144,768]{2,1,0:T(8,128)(2,1)S(1)}, bf16[1,144,768]{2,1,0:T(8,128)(2,1)}, u32[]{:S(2)}) copy-start(bf16[1,144,768]{2,1,0:T(8,128)(2,1)} %copy-done.29) | copy-start | bytes 663556
  255.3 58.6 %copy-start.33 = (pred[2,144,256]{2,1,0:T(8,128)(4,1)S(1)}, pred[2,144,256]{2,1,0:T(8,128)(4,1)}, u32[]{:S(2)}) copy-start(pred[2,144,256]{2,1,0:T(8,128)(4,1)} %copy-done.31) | copy-start | bytes 221188
  255.3 178.1 %all-gather.23.cloned.1.call-start = ((), (), s32[]{:S(2)}) async-start(), calls=%async_computation.16 | async-start | bytes 3538944 | tf_op jit(solution)/shard_map/all_gather | solution.py:424
  255.9 84.4 %copy-start.64 = (f32[2,144,16]{1,2,0:T(8,128)}, f32[2,144,16]{1,2,0:T(8,128)S(1)}, u32[]{:S(2)}) copy-start(f32[2,144,16]{1,2,0:T(8,128)S(1)} %fusion.52) | copy-start | bytes 55300
  281.6 58.8 %copy-start.66 = (f32[2,144]{1,0:T(2,128)}, f32[2,144]{1,0:T(2,128)S(1)}, u32[]{:S(2)}) copy-start(f32[2,144]{1,0:T(2,128)S(1)} %mul.272) | copy-start | bytes 3460
  313.9 26.4 %copy-start.55 = (f32[256]{0:T(256)S(1)}, f32[256]{0:T(256)}, u32[]{:S(2)}) copy-start(f32[256]{0:T(256)} %copy-done.54) | copy-start | bytes 3076
  313.9 26.4 %copy-start.59 = (s32[256]{0:T(256)S(1)}, s32[256]{0:T(256)}, u32[]{:S(2)}) copy-start(s32[256]{0:T(256)} %copy-done.57) | copy-start | bytes 3076
  314.7 26.8 %copy-start.39 = (bf16[1,256,768]{2,1,0:T(8,128)(2,1)S(1)}, bf16[1,256,768]{2,1,0:T(8,128)(2,1)}, u32[]{:S(2)}) copy-start(bf16[1,256,768]{2,1,0:T(8,128)(2,1)} %param.36) | copy-start | bytes 1179652
  314.7 26.8 %copy-start.71 = (f32[256]{0:T(256)S(1)}, f32[256]{0:T(256)}, u32[]{:S(2)}) copy-start(f32[256]{0:T(256)} %get-tuple-element.122) | copy-start | bytes 3076
  342.8 158.9 %reduce-scatter.11.cloned.1.call-start = ((), (), s32[]{:S(2)}) async-start(), calls=%async_computation.17 | async-start | bytes 1474560 | tf_op jit(solution)/shard_map/reduce_scatter | solution.py:605
  344.8 42.2 %copy-start.51 = (f32[256]{0:T(256)}, f32[256]{0:T(256)S(1)}, u32[]{:S(2)}) copy-start(f32[256]{0:T(256)S(1)} %get-tuple-element.121) | copy-start | bytes 3076
  352.8 34.2 %copy-start.24 = (bf16[1,256,768]{2,1,0:T(8,128)(2,1)S(1)}, bf16[1,256,768]{2,1,0:T(8,128)(2,1)}, u32[]{:S(2)}) copy-start(bf16[1,256,768]{2,1,0:T(8,128)(2,1)} %param.23) | copy-start | bytes 1179652
  388.7 113.1 %reduce-scatter.17.cloned.1.call-start = ((), (), s32[]{:S(2)}) async-start(), calls=%async_computation.20 | async-start | bytes 1474560 | tf_op jit(solution)/shard_map/reduce_scatter | solution.py:605
  391.4 110.3 %reduce-scatter.13.cloned.1.call-start = ((), (), s32[]{:S(2)}) async-start(), calls=%async_computation.18 | async-start | bytes 1474560 | tf_op jit(solution)/shard_map/reduce_scatter | solution.py:605
  398.9 34.3 %copy-start.76 = (pred[18]{0:T(512)(128)(4,1)S(1)}, pred[18]{0:T(512)(128)(4,1)}, u32[]{:S(2)}) copy-start(pred[18]{0:T(512)(128)(4,1)} %get-tuple-element.108) | copy-start | bytes 58
  440.5 24.2 %copy-start.25 = (bf16[1,256,768]{2,1,0:T(8,128)(2,1)S(1)}, bf16[1,256,768]{2,1,0:T(8,128)(2,1)}, u32[]{:S(2)}) copy-start(bf16[1,256,768]{2,1,0:T(8,128)(2,1)} %param.23) | copy-start | bytes 1179652
  440.5 24.2 %copy-start.52 = (f32[256]{0:T(256)S(1)}, f32[256]{0:T(256)}, u32[]{:S(2)}) copy-start(f32[256]{0:T(256)} %copy-done.51) | copy-start | bytes 3076
  469.0 28.1 %all-to-all-start.1 = ((bf16[8,64,768]{2,1,0:T(8,128)(2,1)}), bf16[8,64,768]{2,1,0:T(8,128)(2,1)}, u32[]{:S(2)}, u32[]{:S(2)}) async-start(bf16[8,64,768]{2,1,0:T(8,128)(2,1)} %bitcast.29), calls=%async_computation.2 | async-start | bytes 1572864 | tf_op jit(solution)/shard_map/all_to_all | solution.py:503
  473.2 45.4 %reduce-scatter.15.cloned.1.call-start = ((), (), s32[]{:S(2)}) async-start(), calls=%async_computation.19 | async-start | bytes 1474560 | tf_op jit(solution)/shard_map/reduce_scatter | solution.py:605
  474.9 128.8 %all-reduce.11.cloned.1.call-start = ((), (), s32[]{:S(2)}) async-start(), calls=%async_computation.24 | async-start | bytes 2359296 | tf_op jit(solution)/shard_map/psum | solution.py:606
  500.3 18.3 %copy-start.10 = (bf16[768,768]{1,0:T(8,128)(2,1)S(1)}, bf16[768,768]{1,0:T(8,128)(2,1)}, u32[]{:S(2)}) copy-start(bf16[768,768]{1,0:T(8,128)(2,1)} %all-gather.19.cloned.1.call-done.wv_ref) | copy-start | bytes 3538948
  500.3 18.3 %copy-start.26 = (bf16[1,256,768]{2,1,0:T(8,128)(2,1)S(1)}, bf16[1,256,768]{2,1,0:T(8,128)(2,1)}, u32[]{:S(2)}) copy-start(bf16[1,256,768]{2,1,0:T(8,128)(2,1)} %param.23) | copy-start | bytes 1179652
  500.4 18.3 %copy-start.53 = (f32[256]{0:T(256)S(1)}, f32[256]{0:T(256)}, u32[]{:S(2)}) copy-start(f32[256]{0:T(256)} %copy-done.51) | copy-start | bytes 3076
  518.6 46.1 %copy-start.70 = (f32[256]{0:T(256)S(1)}, f32[256]{0:T(256)}, u32[]{:S(2)}) copy-start(f32[256]{0:T(256)} %get-tuple-element.120) | copy-start | bytes 3076
  564.7 45.3 %copy-start.1 = (bf16[2,768,768]{2,1,0:T(8,128)(2,1)S(1)}, bf16[2,768,768]{2,1,0:T(8,128)(2,1)}, u32[]{:S(2)}) copy-start(bf16[2,768,768]{2,1,0:T(8,128)(2,1)} %param.32) | copy-start | bytes 7077892
  (56 other events, 282.2 us)
Sparse Core Ops, SparseCore 0:
  9.7 20.4 all-gather.14
  31.7 17.5 all-gather.16
  50.8 17.4 all-gather.18
  70.3 60.4 all-gather.24
  132.2 16.0 all-gather.20
  150.3 20.8 all-gather.28
  213.7 19.7 all-gather.26
  250.9 29.3 reduce-scatter.6
  283.1 29.3 reduce-scatter.8
  343.0 58.7 all-gather.22
  404.3 24.1 reduce-scatter.10
  431.1 25.7 reduce-scatter.16
  466.5 23.7 reduce-scatter.12
  492.9 25.7 reduce-scatter.14
  522.3 81.3 all-reduce.10

commit v2 on v1

v2 whole, which is shorter than its diff:
```python
import functools
import math

import jax
import jax.numpy as jnp
import numpy as np
from jax import lax
from jax.experimental import pallas as pl
from jax.experimental.pallas import tpu as pltpu
from jax.sharding import PartitionSpec as P

HEADS = 12
HEAD_DIM = 64
BLOCK = 128
PAIRS = HEADS // 2
NEAR = 2 * BLOCK
SPAN = 3 * BLOCK
epsilon = 1e-06
MASKED = -1e30
bucket_edges = [math.ceil(16 * 8 ** (marker / 16)) for marker in range(1, 16)]
F32 = jnp.float32
BF16 = jnp.bfloat16
HIGH = lax.Precision.HIGHEST


def bucket_of(distance):
    gap = np.maximum(distance, 0)
    count = np.full(gap.shape, 16, np.int32)
    for edge in bucket_edges:
        count = count + (gap >= edge)
    return np.where(gap < 16, gap, count)


def wrapped_lanes():
    lanes = np.arange(SPAN)
    return np.where(lanes < NEAR, lanes, lanes - SPAN)


def onehot_of(distance, buckets):
    return (bucket_of(distance)[:, None] == np.arange(buckets)[None, :]).astype(np.float32)


def dot(left, right, left_dim=1, right_dim=0):
    return lax.dot_general(
        left, right, (((left_dim,), (right_dim,)), ((), ())), preferred_element_type=F32
    )


def lane_ids(rows, lanes):
    return lax.broadcasted_iota(jnp.int32, (rows, lanes), 1)


def stack_heads(rows):
    first = lane_ids(rows.shape[0], BLOCK) < HEAD_DIM
    zero = jnp.zeros_like(rows)
    return jnp.concatenate([jnp.where(first, rows, zero), jnp.where(first, zero, rows)], axis=0)


def merge_heads(stacked):
    half = stacked.shape[0] // 2
    first = lane_ids(half, BLOCK) < HEAD_DIM
    return jnp.where(first, stacked[:half], stacked[half:])


def fold_lanes(tile, combine):
    return combine(tile[:, :BLOCK], tile[:, BLOCK:])


def near_bias(base_ref):
    tiles = []
    for head in range(2):
        row = jnp.broadcast_to(base_ref[0, head : head + 1, :], (BLOCK, SPAN))
        tiles.append(pltpu.roll(row, 0, 1, stride=1, stride_axis=0)[:, :NEAR])
    return jnp.concatenate(tiles, axis=0)


def rows_at(block):
    return pl.ds(pl.multiple_of(block * BLOCK, BLOCK), BLOCK)


def two_tiles(ref, source_ref, tile):
    return jnp.concatenate(
        [ref[rows_at(source_ref[tile]), :], ref[rows_at(source_ref[tile + 1]), :]], axis=0
    )


class LineGather:
    def __init__(self, axis, lines, across, views, own, sems):
        self.axis, self.lines, self.across = axis, lines, across
        self.views, self.own, self.sems = views, own, sems
        self.me = lax.axis_index(axis)
        self.line, self.column = self.me // across, self.me % across

    def copy(self, part, block, peer, kind, place, own=False):
        send, recv = self.sems
        view = self.views[part](block)
        return pltpu.make_async_remote_copy(
            src_ref=self.own[part] if own else view,
            dst_ref=view,
            send_sem=send.at[part, kind, place],
            recv_sem=recv.at[part, kind, place],
            device_id={self.axis: peer},
            device_id_type=pl.DeviceIdType.MESH,
        )

    def line_send(self, part, way, step):
        place = self.line - way * step
        ahead = self.line + way
        there = (place >= 0) & (place < self.lines) & (ahead >= 0) & (ahead < self.lines)
        copy = self.copy(
            part,
            place * self.across + self.column,
            ahead * self.across + self.column,
            (1 - way) // 2,
            step,
            own=step == 0,
        )
        return there, copy

    def line_recv(self, part, way, step):
        place = self.line - way * (step + 1)
        there = (place >= 0) & (place < self.lines)
        block = place * self.across + self.column
        return there, block, self.copy(part, block, self.me, (1 - way) // 2, step)

    def cross_send(self, part, block, ahead, own=False):
        peer = self.line * self.across + (self.column + ahead) % self.across
        return self.copy(part, block, peer, 1 + ahead, block // self.across, own)

    def cross_recv(self, part, line, ahead):
        block = line * self.across + (self.column + self.across - ahead) % self.across
        return self.copy(part, block, self.me, 1 + ahead, line)

    def begin(self, part):
        for way in (1, -1):
            there, copy = self.line_send(part, way, 0)
            pl.when(there)(copy.start)
        for ahead in range(1, self.across):
            self.cross_send(part, self.me, ahead, own=True).start()

    def advance(self, part, step):
        for way in (1, -1):
            there, block, arrived = self.line_recv(part, way, step)

            @pl.when(there)
            def _():
                arrived.wait_recv()
                for ahead in range(1, self.across):
                    self.cross_send(part, block, ahead).start()

            if step + 2 < self.lines:
                there, copy = self.line_send(part, way, step + 1)
                pl.when(there)(copy.start)

    def wait_cross(self, part):
        for ahead in range(1, self.across):
            for line in range(self.lines):
                self.cross_recv(part, line, ahead).wait_recv()

    def finish(self):
        for part in range(len(self.views)):
            for step in range(self.lines - 1):
                for way in (1, -1):
                    there, copy = self.line_send(part, way, step)
                    pl.when(there)(copy.wait_send)
            for ahead in range(1, self.across):
                for line in range(self.lines):
                    self.cross_send(part, line * self.across + self.column, ahead).wait_send()


def gather_sems(parts, lines, across):
    return [pltpu.SemaphoreType.DMA((parts, 1 + across, lines))] * 2


def greet(counts):
    barrier = pltpu.get_barrier_semaphore()
    for axis, count in zip(("ctx", "wsh"), counts):
        me = lax.axis_index(axis)
        for ahead in range(1, count):
            pl.semaphore_signal(
                barrier,
                inc=1,
                device_id={axis: (me + ahead) % count},
                device_id_type=pl.DeviceIdType.MESH,
            )
    pl.semaphore_wait(barrier, sum(counts) - 2)


class Exchange:
    def __init__(self, count, experts, most, sems, source, target):
        self.count, self.experts, self.most = count, experts, most
        self.send, self.recv = sems
        self.source, self.target = source, target
        self.me = lax.axis_index("ctx")

    def rows(self, place):
        return pl.ds(pl.multiple_of(place * self.most, self.most), self.most)

    def copy(self, expert, ahead, outward):
        peer = (self.me + ahead) % self.count if outward else (self.me + self.count - ahead) % self.count
        return pltpu.make_async_remote_copy(
            src_ref=self.source(expert, peer),
            dst_ref=self.target(expert, self.me),
            send_sem=self.send.at[expert, ahead - 1],
            recv_sem=self.recv.at[expert, ahead - 1],
            device_id={"ctx": peer},
            device_id_type=pl.DeviceIdType.MESH,
        )

    def start(self, expert):
        for ahead in range(1, self.count):
            self.copy(expert, ahead, True).start()
        self.target(expert, self.me)[...] = self.source(expert, self.me)[...]

    def wait(self, expert):
        for ahead in range(1, self.count):
            peer = (self.me + self.count - ahead) % self.count
            pltpu.make_async_remote_copy(
                src_ref=self.source(expert, peer),
                dst_ref=self.target(expert, peer),
                send_sem=self.send.at[expert, ahead - 1],
                recv_sem=self.recv.at[expert, ahead - 1],
                device_id={"ctx": peer},
                device_id_type=pl.DeviceIdType.MESH,
            ).wait_recv()

    def finish(self, expert):
        for ahead in range(1, self.count):
            self.copy(expert, ahead, True).wait_send()


def exchange_sems(count, experts):
    return [pltpu.SemaphoreType.DMA((experts, count - 1))] * 2


def cap_map(target_ref, expert, capacity):
    slots = target_ref.shape[1]
    rows = lax.broadcasted_iota(jnp.int32, (capacity, slots), 0)
    return (rows == jnp.broadcast_to(target_ref[expert : expert + 1, :], rows.shape)).astype(F32).astype(BF16)


def placement_of(slot_ref, slots):
    rows = lax.broadcasted_iota(jnp.int32, (slots, slot_ref.shape[1]), 0)
    return (rows == jnp.broadcast_to(slot_ref[0:1, :], rows.shape)).astype(F32).astype(BF16)


def grid_of(count):
    lines = 4 if count % 4 == 0 else 1
    return lines, count // lines


def route_slots(routes_ref, chosen_ref, most):
    experts, tokens = chosen_ref.shape
    ids = lax.broadcasted_iota(jnp.int32, (experts, tokens), 0)
    routes = jnp.broadcast_to(routes_ref[0:1, :], ids.shape)
    chosen = (ids == routes).astype(F32)
    chosen_ref[...] = chosen
    earlier = lax.broadcasted_iota(jnp.int32, (tokens, tokens), 0) < lax.broadcasted_iota(
        jnp.int32, (tokens, tokens), 1
    )
    before = dot(chosen.astype(BF16), earlier.astype(F32).astype(BF16))
    rank = jnp.sum(chosen * before, axis=0, keepdims=True).astype(jnp.int32)
    return routes_ref[0:1, :] * most + rank, jnp.sum(chosen, axis=1, keepdims=True)


def project_kernel(
    counts,
    capacity,
    rows_ref,
    wq_ref,
    wk_ref,
    wv_ref,
    wo_ref,
    small_ref,
    routes_ref,
    grad_ref,
    qkv_out,
    weights_out,
    small_out,
    slot_out,
    target_out,
    own_out,
    held,
    weights,
    smalls,
    gain,
    ready,
    chosen,
    tallies,
    grad_rows,
    outgoing,
    incoming,
    row_send,
    row_recv,
    weight_send,
    weight_recv,
    grad_send,
    grad_recv,
    tally_send,
    tally_recv,
    out_sems,
    local_sems,
):
    ctx_count, wsh_count = counts
    experts = chosen.shape[0]
    exp_dev = experts // ctx_count
    lanes = experts
    tokens, width = rows_ref.shape
    share = wq_ref.shape[0]
    lines, across = grid_of(ctx_count)
    pairs = wsh_count // 2

    def shard(block):
        return pl.ds(pl.multiple_of(block * share, 16), share)

    def weight_view(place):
        return lambda block: weights.at[place, shard(block), :]

    rows = LineGather(
        "ctx", lines, across, [lambda block: held.at[block]], [rows_ref], (row_send, row_recv)
    )
    mats = LineGather(
        "wsh",
        pairs,
        2,
        [lambda block: smalls.at[shard(block), :]] + [weight_view(place) for place in range(4)],
        [small_ref, wq_ref, wk_ref, wv_ref, wo_ref],
        (weight_send, weight_recv),
    )
    own_copies = [
        pltpu.make_async_copy(ref, view(index), local_sems.at[2 + place])
        for place, (ref, view, index) in enumerate(
            zip(
                [rows_ref] + mats.own,
                rows.views + mats.views,
                [rows.me] + [mats.me] * 5,
            )
        )
    ]
    grad_copy = pltpu.make_async_copy(grad_ref, grad_rows, local_sems.at[8])
    grad_copy.start()
    for copy in own_copies:
        copy.start()
    greet(counts)
    rows.begin(0)
    for part in range(5):
        mats.begin(part)
    most = incoming.shape[1] // ctx_count
    slot, tally = route_slots(routes_ref, chosen, most)
    slot_out[...] = jnp.broadcast_to(slot, slot_out.shape)
    tallies[rows.me] = jnp.broadcast_to(tally, (experts, BLOCK))
    counted = Exchange(
        ctx_count,
        1,
        most,
        (tally_send, tally_recv),
        lambda expert, peer: tallies.at[rows.me],
        lambda expert, peer: tallies.at[peer],
    )
    for ahead in range(1, ctx_count):
        counted.copy(0, ahead, True).start()
    grad_copy.wait()
    outgoing[...] = dot(placement_of(slot_out, experts * most), grad_rows[...]).astype(BF16)
    grads = Exchange(
        ctx_count,
        exp_dev,
        most,
        (grad_send, grad_recv),
        lambda expert, peer: outgoing.at[grads.rows(peer * exp_dev + expert), :],
        lambda expert, peer: incoming.at[expert, grads.rows(peer), :],
    )
    for copy in own_copies:
        copy.wait()
    for step in range(max(lines, pairs) - 1):
        if step < lines - 1:
            rows.advance(0, step)
        if step == 0:
            for expert in range(exp_dev):
                grads.start(expert)
        if step >= lines - 2 or step < pairs - 1:
            for part in range(5):
                if step < pairs - 1:
                    mats.advance(part, step)
    for part in range(5):
        mats.wait_cross(part)
    weights_copy = pltpu.make_async_copy(weights, weights_out, local_sems.at[0])
    weights_copy.start()
    small_copy = pltpu.make_async_copy(smalls, small_out, local_sems.at[1])
    small_copy.start()
    gain[...] = jnp.transpose(smalls[...].astype(F32))[lanes : lanes + 8, :]
    upper = rows.line // max(lines // 2, 1)

    def put(slot, block):
        place = pl.ds(pl.multiple_of(block * tokens, tokens), tokens)
        return pltpu.make_async_copy(ready.at[slot], qkv_out.at[place, :], out_sems.at[slot])

    def order(step):
        ahead, line = step // lines, step % lines
        line = line + upper * (lines - 1 - 2 * line)
        return line, ahead, line * across + (rows.column + across - ahead) % across

    def step_body(step, carry):
        line, ahead, block = order(step)
        slot = step % 2
        for skip in range(1, across):

            @pl.when(ahead == skip)
            def _():
                rows.cross_recv(0, line, skip).wait_recv()

        @pl.when(step >= 2)
        def _():
            put(slot, order(step - 2)[2]).wait()

        values = held[block].astype(F32)
        inv = lax.rsqrt(jnp.mean(values * values, axis=-1, keepdims=True) + epsilon)
        normed = (values * inv * gain[0:1, :]).astype(BF16)
        for place in range(3):
            ready[slot, :, place * width : (place + 1) * width] = dot(
                normed, weights[place]
            ).astype(BF16)
        put(slot, block).start()
        return carry

    lax.fori_loop(0, ctx_count, step_body, 0)
    for step in (ctx_count - 2, ctx_count - 1):
        put(step % 2, order(step)[2]).wait()
    counted.wait(0)
    lane = lane_ids(1, ctx_count * most)
    for expert in range(exp_dev):
        offset = jnp.zeros((1, 1), F32)
        target = jnp.full((1, ctx_count * most), capacity, jnp.int32)
        for source in range(ctx_count):
            count = tallies[source, pl.ds(rows.me * exp_dev + expert, 1), 0:1]
            inside = (lane >= source * most) & (
                lane < source * most + jnp.broadcast_to(count.astype(jnp.int32), lane.shape)
            )
            place = lane - source * most + jnp.broadcast_to(offset.astype(jnp.int32), lane.shape)
            target = jnp.where(inside, place, target)
            offset = offset + count
        target_out[expert : expert + 1, :] = target
    target_out[exp_dev:, :] = jnp.zeros_like(target_out[exp_dev:, :])
    for expert in range(exp_dev):
        grads.wait(expert)
        own_out[expert] = dot(cap_map(target_out, expert, capacity), incoming[expert]).astype(BF16)
    weights_copy.wait()
    small_copy.wait()
    counted.finish(0)
    for expert in range(exp_dev):
        grads.finish(expert)
    rows.finish()
    mats.finish()


def project(counts, capacity, experts, most, rows, weights, small, routes, grad):
    tokens, width = rows.shape
    ctx_count, wsh_count = counts
    exp_dev = experts // ctx_count
    length = tokens * ctx_count
    lines, across = grid_of(ctx_count)
    vmem = pl.BlockSpec(memory_space=pltpu.VMEM)
    anywhere = pl.BlockSpec(memory_space=pl.ANY)
    return pl.pallas_call(
        functools.partial(project_kernel, counts, capacity),
        in_specs=[anywhere] * 6 + [vmem, anywhere],
        out_specs=[anywhere] * 3 + [vmem] * 3,
        out_shape=[
            jax.ShapeDtypeStruct((length, 3 * width), BF16),
            jax.ShapeDtypeStruct((4, width, width), BF16),
            jax.ShapeDtypeStruct((width, small.shape[1]), BF16),
            jax.ShapeDtypeStruct((8, tokens), jnp.int32),
            jax.ShapeDtypeStruct((8, ctx_count * most), jnp.int32),
            jax.ShapeDtypeStruct((exp_dev, capacity, width), BF16),
        ],
        scratch_shapes=[
            pltpu.VMEM((ctx_count, tokens, width), BF16),
            pltpu.VMEM((4, width, width), BF16),
            pltpu.VMEM((width, small.shape[1]), BF16),
            pltpu.VMEM((8, width), F32),
            pltpu.VMEM((2, tokens, 3 * width), BF16),
            pltpu.VMEM((experts, tokens), F32),
            pltpu.VMEM((ctx_count, experts, BLOCK), F32),
            pltpu.VMEM((tokens, width), BF16),
            pltpu.VMEM((experts * most, width), BF16),
            pltpu.VMEM((exp_dev, ctx_count * most, width), BF16),
            *gather_sems(1, lines, across),
            *gather_sems(5, wsh_count // 2, 2),
            *exchange_sems(ctx_count, exp_dev),
            *exchange_sems(ctx_count, 1),
            pltpu.SemaphoreType.DMA((2,)),
            pltpu.SemaphoreType.DMA((9,)),
        ],
        compiler_params=pltpu.CompilerParams(
            collective_id=0, has_side_effects=True, vmem_limit_bytes=40 << 20
        ),
        name="project",
    )(rows, *weights, small, routes, grad)


def gelu_parts(values):
    slope, cubic = math.sqrt(2 / math.pi), 0.044715
    square = values * values
    bent = jnp.tanh(slope * (values + cubic * values * square))
    outer = 0.5 * (1.0 + bent)
    derivative = outer + 0.5 * values * (1.0 - bent * bent) * slope * (1.0 + 3 * cubic * square)
    return values * outer, derivative


def choose(rows, router, experts, expert):
    logits = dot(rows, router)
    lanes = lane_ids(rows.shape[0], router.shape[1])
    logits = jnp.where(lanes < experts, logits, MASKED)
    weights = jnp.exp(logits - jnp.max(logits, axis=-1, keepdims=True))
    probs = weights / jnp.sum(weights, axis=-1, keepdims=True)
    hot = (lanes == expert).astype(F32)
    return probs, hot, jnp.sum(probs * hot, axis=-1, keepdims=True)


def middle_kernel(
    counts,
    experts,
    spread_here,
    attn_ref,
    exact_ref,
    hidden_ref,
    grad_ref,
    weights_ref,
    w_in_ref,
    w_out_ref,
    own_g_ref,
    small_ref,
    slot_ref,
    target_ref,
    lse_ref,
    routes_ref,
    output_out,
    grad_mid_out,
    grad_heads_out,
    heads_all_out,
    stats_out,
    grad_wo_out,
    grad_router_out,
    grad_gain_out,
    grad_in_out,
    grad_out_out,
    attn,
    exact,
    hidden,
    grad,
    wo,
    w_in,
    w_out,
    resid,
    incoming,
    own_x,
    all_x,
    all_g,
    hid,
    du,
    parts,
    from_mate,
    from_far,
    returning,
    home,
    branch,
    stats,
    stage_in,
    stage_out,
    heads_stage,
    fetch_sems,
    out_sems,
    heads_sems,
    x_send,
    x_recv,
    g_send,
    g_recv,
    go_send,
    go_recv,
    back_send,
    back_recv,
    mate_send,
    mate_recv,
    far_send,
    far_recv,
    branch_send,
    branch_recv,
):
    ctx_count, wsh_count = counts
    tokens, width = hidden.shape
    exp_dev, capacity = own_x.shape[:2]
    most = incoming.shape[1] // ctx_count
    lines, across = grid_of(ctx_count)
    pairs = wsh_count // 2
    me = lax.axis_index("ctx")
    home_row = me if spread_here else 0
    sources = (
        (attn_ref, attn),
        (weights_ref.at[3], wo),
        (hidden_ref, hidden),
        (grad_ref, grad),
        (w_in_ref, w_in),
        (w_out_ref, w_out),
        (exact_ref, exact),
    )
    fetches = [
        pltpu.make_async_copy(src, dst, fetch_sems.at[place])
        for place, (src, dst) in enumerate(sources)
    ]
    for fetch in fetches:
        fetch.start()
    views = [
        (lambda buffer, expert: lambda block: buffer.at[expert, block])(buffer, expert)
        for buffer in (all_g, all_x)
        for expert in range(exp_dev)
    ]
    gather_g = LineGather(
        "wsh",
        pairs,
        2,
        views[:exp_dev],
        [own_g_ref.at[expert] for expert in range(exp_dev)],
        (g_send, g_recv),
    )
    gather_x = LineGather(
        "wsh",
        pairs,
        2,
        views[exp_dev:],
        [own_x.at[expert] for expert in range(exp_dev)],
        (x_send, x_recv),
    )
    wsh_me, my_line, my_core = gather_x.me, gather_x.line, gather_x.column
    greet(counts)
    for expert in range(exp_dev):
        gather_g.begin(expert)
        all_g[expert, wsh_me] = own_g_ref[expert]

    small_t = jnp.transpose(small_ref[...].astype(F32))[experts : experts + 8, :]
    gain_two = small_t[1:2, :]
    router = jnp.where(
        lane_ids(width, small_ref.shape[1]) < experts, small_ref[...], jnp.zeros_like(small_ref)
    )
    for fetch in fetches[:3]:
        fetch.wait()
    resid[...] = hidden[...].astype(F32) + dot(attn[...], wo[...])
    inv_two = lax.rsqrt(jnp.mean(resid[...] * resid[...], axis=-1, keepdims=True) + epsilon)
    normed_two = (resid[...] * inv_two * gain_two).astype(BF16)
    placement = placement_of(slot_ref, experts * most)
    returning[0] = dot(placement, normed_two).astype(BF16)
    forth = Exchange(
        ctx_count,
        exp_dev,
        most,
        (go_send, go_recv),
        lambda expert, peer: returning.at[0, forth.rows(peer * exp_dev + expert), :],
        lambda expert, peer: incoming.at[expert, forth.rows(peer), :],
    )
    for expert in range(exp_dev):
        forth.start(expert)
    gate = choose(normed_two, router, experts, routes_ref[...])[2]
    for expert in range(exp_dev):
        for step in range(pairs - 1):
            gather_g.advance(expert, step)
    gather_g.finish()
    for fetch in fetches[3:]:
        fetch.wait()

    def mate_copy(array, expert, line):
        mine = line * 2 + 1 - my_core
        return pltpu.make_async_remote_copy(
            src_ref=parts.at[array, expert, mine],
            dst_ref=from_mate.at[array, expert, line],
            send_sem=mate_send.at[array, expert, line],
            recv_sem=mate_recv.at[array, expert, line],
            device_id={"wsh": my_line * 2 + 1 - my_core},
            device_id_type=pl.DeviceIdType.MESH,
        )

    def far_copy(array, expert, ahead):
        line = (my_line + ahead) % pairs
        return pltpu.make_async_remote_copy(
            src_ref=parts.at[array, expert, line * 2 + my_core],
            dst_ref=from_far.at[array, expert, ahead - 1],
            send_sem=far_send.at[array, expert, ahead - 1],
            recv_sem=far_recv.at[array, expert, ahead - 1],
            device_id={"wsh": line * 2 + my_core},
            device_id_type=pl.DeviceIdType.MESH,
        )

    def work(expert, step):
        line = (my_line + step // 2) % pairs
        core = (my_core + step % 2) % 2
        block = line * 2 + core

        @pl.when(step % 2 == 1)
        def _():
            gather_x.cross_recv(expert, line, 1).wait_recv()
            gather_g.cross_recv(expert, line, 1).wait_recv()

        rows = all_x[expert, block]
        active, slope = gelu_parts(dot(rows, w_in[expert]))
        active = active.astype(BF16)
        hid[expert, block] = active
        parts[0, expert, block] = dot(active, w_out[expert]).astype(BF16)
        share = choose(rows, router, experts, exp_dev * me + expert)[2]
        grads = (share * all_g[expert, block].astype(F32)).astype(BF16)
        all_g[expert, block] = grads
        grad_u = (dot(grads, w_out[expert], 1, 1) * slope).astype(BF16)
        du[expert, block] = grad_u
        parts[1, expert, block] = dot(grad_u, w_in[expert], 1, 1).astype(BF16)

        @pl.when(step % 2 == 1)
        def _():
            mate_copy(0, expert, line).start()
            mate_copy(1, expert, line).start()

    def fold(expert, ahead):
        line = (my_line + ahead) % pairs
        for array in range(2):
            mate_copy(array, expert, line).wait_recv()
            if ahead > 0:
                both = parts[array, expert, line * 2 + my_core].astype(F32) + from_mate[
                    array, expert, line
                ].astype(F32)
                parts[array, expert, line * 2 + my_core] = both.astype(BF16)
                far_copy(array, expert, ahead).start()

    for expert in range(exp_dev):
        forth.wait(expert)
        own_x[expert] = dot(cap_map(target_ref, expert, capacity), incoming[expert]).astype(BF16)
        gather_x.begin(expert)
        all_x[expert, wsh_me] = own_x[expert]
        lax.fori_loop(0, 2, lambda step, carry: (work(expert, step), carry)[1], 0)
        for step in range(pairs - 1):
            gather_x.advance(expert, step)
        lax.fori_loop(2, wsh_count, lambda step, carry: (work(expert, step), carry)[1], 0)
        for ahead in range(1, pairs):
            fold(expert, ahead)

    back = [
        Exchange(
            ctx_count,
            exp_dev,
            most,
            (back_send.at[array], back_recv.at[array]),
            (
                lambda array: lambda expert, peer: returning.at[
                    array, forth.rows(expert * ctx_count + peer), :
                ]
            )(array),
            (
                lambda array: lambda expert, peer: home.at[
                    array, forth.rows(peer * exp_dev + expert), :
                ]
            )(array),
        )
        for array in range(2)
    ]
    for expert in range(exp_dev):
        forth.finish(expert)
    for expert in range(exp_dev):
        expert_rows = pl.ds(expert * ctx_count * most, ctx_count * most)
        fold(expert, 0)
        sums = []
        for array in range(2):
            line = my_line * 2 + my_core
            total = parts[array, expert, line].astype(F32) + from_mate[
                array, expert, my_line
            ].astype(F32)
            for ahead in range(1, pairs):
                far_copy(array, expert, ahead).wait_recv()
                total = total + from_far[array, expert, ahead - 1].astype(F32)
            sums.append(total)
        out_rows = sums[0].astype(BF16)
        rows = own_x[expert]
        probs, hot, share = choose(rows, router, experts, exp_dev * me + expert)
        slot_g = own_g_ref[expert].astype(F32)
        grad_gate = jnp.sum(slot_g * out_rows.astype(F32), axis=-1, keepdims=True)
        grad_logits = (share * grad_gate * (hot - probs)).astype(BF16)
        grad_rows = sums[1].astype(BF16).astype(F32) + dot(grad_logits, router, 1, 1)
        spread = cap_map(target_ref, expert, capacity)
        returning[1, expert_rows] = dot(spread, grad_rows.astype(BF16), 0, 0).astype(BF16)
        back[1].start(expert)
        returning[0, expert_rows] = dot(spread, out_rows, 0, 0).astype(BF16)
        router_part = dot(grad_logits, rows, 0, 0)[:experts]
        if expert == 0:
            grad_router_out[...] = router_part
        else:
            grad_router_out[...] += router_part
    for expert in range(exp_dev):
        back[0].start(expert)
    grad_up = grad[...].astype(F32)
    for expert in range(exp_dev):
        back[1].wait(expert)
    grad_normed = dot(placement_of(slot_ref, experts * most), home[1], 0, 0)
    scaled = grad_normed * gain_two
    mean = jnp.mean(scaled * resid[...], axis=-1, keepdims=True)
    gain_part = jnp.sum(grad_normed * resid[...] * inv_two, axis=0, keepdims=True)
    grad_gain_out[...] = jnp.broadcast_to(gain_part, grad_gain_out.shape)
    grad_mid = grad_up + inv_two * scaled - resid[...] * inv_two * inv_two * inv_two * mean
    grad_mid_out[...] = grad_mid
    branch[home_row] = grad_mid.astype(BF16)

    gather_d = LineGather(
        "ctx",
        lines,
        across,
        [lambda block: branch.at[block], lambda block: stats.at[block]],
        [branch.at[me], stats.at[me]],
        (branch_send, branch_recv),
    )
    if spread_here:
        gather_d.begin(0)
    grad_heads = dot(branch[home_row], wo[...], 1, 1).astype(BF16)
    grad_heads_out[...] = grad_heads
    product = grad_heads.astype(F32) * exact[...]
    heads = lax.broadcasted_iota(jnp.int32, (width, BLOCK), 0) // HEAD_DIM
    head_hot = (heads == lane_ids(width, BLOCK)).astype(F32)
    delta = jnp.transpose(
        lax.dot_general(
            product, head_hot, (((1,), (0,)), ((), ())), precision=HIGH, preferred_element_type=F32
        )
    )
    for pair in range(PAIRS):
        stats[home_row, pair] = lse_ref[pair]
        stats[home_row, pair, 2:4, :] = delta[2 * pair : 2 * pair + 2, :]
    if spread_here:
        gather_d.begin(1)

    def in_copy(expert):
        return pltpu.make_async_copy(stage_in, grad_in_out.at[expert], out_sems.at[1])

    def out_copy(expert):
        return pltpu.make_async_copy(stage_out, grad_out_out.at[expert], out_sems.at[0])

    group = min(wsh_count, 4)

    def slot_sum(stage, left, right, expert):
        def part(turn):
            blocks = pl.ds(turn * group, group)
            return dot(
                left[expert, blocks].reshape(group * capacity, left.shape[3]),
                right[expert, blocks].reshape(group * capacity, right.shape[3]),
                0,
                0,
            )

        stage[...] = part(0)
        if wsh_count > group:

            def add(turn, carry):
                stage[...] += part(turn)
                return carry

            lax.fori_loop(1, wsh_count // group, add, 0)

    def grads_of(expert):
        if expert:
            out_copy(expert - 1).wait()
        slot_sum(stage_out, hid, all_g, expert)
        out_copy(expert).start()
        if expert:
            in_copy(expert - 1).wait()
        slot_sum(stage_in, all_x, du, expert)
        in_copy(expert).start()

    grad_wo_out[...] = dot(attn[...], branch[home_row], 0, 0).astype(BF16)
    for step in range(lines - 1):
        if spread_here:
            for part in range(2):
                gather_d.advance(part, step)
        if step < exp_dev:
            grads_of(step)
    for expert in range(min(lines - 1, exp_dev), exp_dev):
        grads_of(expert)
    for expert in range(exp_dev):
        back[0].wait(expert)
    token_out = dot(placement_of(slot_ref, experts * most), home[0], 0, 0)
    output_out[...] = (resid[...] + gate * token_out).astype(BF16)
    upper = gather_d.line // max(lines // 2, 1)

    def order(step):
        ahead, line = step // lines, step % lines
        line = line + upper * (lines - 1 - 2 * line)
        return line, ahead, line * across + (gather_d.column + across - ahead) % across

    def put(slot, block):
        place = pl.ds(pl.multiple_of(block * tokens, tokens), tokens)
        return pltpu.make_async_copy(
            heads_stage.at[slot], heads_all_out.at[place, :], heads_sems.at[slot]
        )

    def heads_step(step, carry):
        line, ahead, block = order(step)
        slot = step % 2
        for skip in range(1, across):

            @pl.when(ahead == skip)
            def _():
                gather_d.cross_recv(0, line, skip).wait_recv()
                gather_d.cross_recv(1, line, skip).wait_recv()

        @pl.when(step >= 2)
        def _():
            put(slot, order(step - 2)[2]).wait()

        heads_stage[slot] = dot(branch[block], wo[...], 1, 1).astype(BF16)
        put(slot, block).start()
        return carry

    if spread_here:
        lax.fori_loop(0, ctx_count, heads_step, 0)
    stats_copy = pltpu.make_async_copy(stats, stats_out, fetch_sems.at[0])
    stats_copy.start()
    if spread_here:
        for step in (ctx_count - 2, ctx_count - 1):
            put(step % 2, order(step)[2]).wait()
    else:
        heads_stage[0] = branch[0]
        own_branch = pltpu.make_async_copy(heads_stage.at[0], heads_all_out, heads_sems.at[0])
        own_branch.start()
        own_branch.wait()
    out_copy(exp_dev - 1).wait()
    in_copy(exp_dev - 1).wait()
    stats_copy.wait()
    for expert in range(exp_dev):
        for array in range(2):
            back[array].finish(expert)
            for line in range(pairs):
                mate_copy(array, expert, line).wait_send()
            for ahead in range(1, pairs):
                far_copy(array, expert, ahead).wait_send()
    gather_x.finish()
    if spread_here:
        gather_d.finish()


def middle(
    counts,
    experts,
    attn,
    exact,
    hidden,
    grad,
    weights,
    w_in,
    w_out,
    own_g,
    small,
    slots,
    targets,
    lse_rows,
    routes,
):
    ctx_count, wsh_count = counts
    tokens, width = hidden.shape
    exp_dev, capacity = own_g.shape[:2]
    units = w_in.shape[2]
    slot_count = targets.shape[1]
    all_slots = experts * (slot_count // ctx_count)
    lines, across = grid_of(ctx_count)
    pairs = wsh_count // 2
    vmem = pl.BlockSpec(memory_space=pltpu.VMEM)
    anywhere = pl.BlockSpec(memory_space=pl.ANY)
    slot_rows = (exp_dev, wsh_count, capacity)
    spread_here = wsh_count <= 4
    held = ctx_count if spread_here else 1
    return pl.pallas_call(
        functools.partial(middle_kernel, counts, experts, spread_here),
        in_specs=[anywhere] * 7 + [vmem] * 6,
        out_specs=[vmem] * 3 + [anywhere] * 2 + [vmem] * 3 + [anywhere] * 2,
        out_shape=[
            jax.ShapeDtypeStruct((tokens, width), BF16),
            jax.ShapeDtypeStruct((tokens, width), F32),
            jax.ShapeDtypeStruct((tokens, width), BF16),
            jax.ShapeDtypeStruct((tokens * held, width), BF16),
            jax.ShapeDtypeStruct((held, PAIRS, 8, tokens), F32),
            jax.ShapeDtypeStruct((width, width), BF16),
            jax.ShapeDtypeStruct((experts, width), F32),
            jax.ShapeDtypeStruct((8, width), F32),
            jax.ShapeDtypeStruct((exp_dev, width, units), F32),
            jax.ShapeDtypeStruct((exp_dev, units, width), F32),
        ],
        scratch_shapes=[
            pltpu.VMEM((tokens, width), BF16),
            pltpu.VMEM((tokens, width), F32),
            pltpu.VMEM((tokens, width), BF16),
            pltpu.VMEM((tokens, width), BF16),
            pltpu.VMEM((width, width), BF16),
            pltpu.VMEM(w_in.shape, BF16),
            pltpu.VMEM(w_out.shape, BF16),
            pltpu.VMEM((tokens, width), F32),
            pltpu.VMEM((exp_dev, slot_count, width), BF16),
            pltpu.VMEM((exp_dev, capacity, width), BF16),
            pltpu.VMEM((*slot_rows, width), BF16),
            pltpu.VMEM((*slot_rows, width), BF16),
            pltpu.VMEM((*slot_rows, units), BF16),
            pltpu.VMEM((*slot_rows, units), BF16),
            pltpu.VMEM((2, *slot_rows, width), BF16),
            pltpu.VMEM((2, exp_dev, pairs, capacity, width), BF16),
            pltpu.VMEM((2, exp_dev, max(pairs - 1, 1), capacity, width), BF16),
            pltpu.VMEM((2, all_slots, width), BF16),
            pltpu.VMEM((2, all_slots, width), BF16),
            pltpu.VMEM((held, tokens, width), BF16),
            pltpu.VMEM((held, PAIRS, 8, tokens), F32),
            pltpu.VMEM((width, units), F32),
            pltpu.VMEM((units, width), F32),
            pltpu.VMEM((2, tokens, width), BF16),
            pltpu.SemaphoreType.DMA((7,)),
            pltpu.SemaphoreType.DMA((2,)),
            pltpu.SemaphoreType.DMA((2,)),
            *gather_sems(exp_dev, pairs, 2),
            *gather_sems(exp_dev, pairs, 2),
            *exchange_sems(ctx_count, exp_dev),
            pltpu.SemaphoreType.DMA((2, exp_dev, ctx_count - 1)),
            pltpu.SemaphoreType.DMA((2, exp_dev, ctx_count - 1)),
            pltpu.SemaphoreType.DMA((2, exp_dev, pairs)),
            pltpu.SemaphoreType.DMA((2, exp_dev, pairs)),
            pltpu.SemaphoreType.DMA((2, exp_dev, max(pairs - 1, 1))),
            pltpu.SemaphoreType.DMA((2, exp_dev, max(pairs - 1, 1))),
            *gather_sems(2, lines, across),
        ],
        compiler_params=pltpu.CompilerParams(
            collective_id=1, has_side_effects=True, vmem_limit_bytes=(56 if spread_here else 62) << 20
        ),
        name="middle",
    )(
        attn,
        exact,
        hidden,
        grad,
        weights,
        w_in,
        w_out,
        own_g,
        small,
        slots,
        targets,
        lse_rows,
        routes,
    )


def forward_kernel(place_ref, source_ref, q_ref, k_ref, v_ref, base_ref, out_ref, exact_ref, lse_ref, row_ref, scores_ref, bias_ref):
    bias_ref[...] = near_bias(base_ref)
    lanes = lane_ids(2 * BLOCK, NEAR)
    for own in range(2):
        block = place_ref[own]
        stacked = stack_heads(q_ref[rows_at(source_ref[block + 1]), :])
        scores = dot(stacked, two_tiles(k_ref, source_ref, block), 1, 1) + bias_ref[...]
        scores = jnp.where(lanes + block * BLOCK < BLOCK, MASKED, scores)
        scores_ref[0] = scores
        chunks = jnp.maximum(block, 1) // 2

        def score_step(chunk, best):
            start = block - 2 * chunk
            part = dot(stacked, two_tiles(k_ref, source_ref, start), 1, 1)
            part = jnp.where(lanes + start * BLOCK < BLOCK, MASKED, part)
            scores_ref[chunk] = part
            return jnp.maximum(best, fold_lanes(part, jnp.maximum))

        best = lax.fori_loop(1, chunks + 1, score_step, fold_lanes(scores, jnp.maximum))
        top = jnp.max(best, axis=-1, keepdims=True)

        def value_step(chunk, carry):
            total, summed = carry
            weights = jnp.exp(scores_ref[chunk] - top)
            high = weights.astype(BF16)
            low = (weights - high.astype(F32)).astype(BF16)
            values = two_tiles(v_ref, source_ref, block - 2 * chunk)
            summed = summed + dot(jnp.concatenate([high, low], axis=0), values)
            return (total + fold_lanes(weights, jnp.add), summed)

        total, summed = lax.fori_loop(
            0,
            chunks + 1,
            value_step,
            (jnp.zeros((2 * BLOCK, BLOCK), F32), jnp.zeros((4 * BLOCK, BLOCK), F32)),
        )
        total = jnp.sum(total, axis=-1, keepdims=True)
        main = summed[: 2 * BLOCK] / total
        exact = main + summed[2 * BLOCK :] / total
        rows = pl.ds(own * BLOCK, BLOCK)
        out_ref[rows, :] = merge_heads(main).astype(BF16)
        exact_ref[rows, :] = merge_heads(exact)
        lse = jnp.broadcast_to(top + jnp.log(total), (2 * BLOCK, BLOCK))
        lse_ref[0, own] = lse
        lse = jnp.transpose(lse)
        for head in range(2):
            row_ref[0, head : head + 1, own * BLOCK : (own + 1) * BLOCK] = lse[
                :1, head * BLOCK : (head + 1) * BLOCK
            ]
    row_ref[0, 2:8, :] = jnp.zeros((6, NEAR), F32)


def pair_specs(rows, width):
    pairs = width // BLOCK

    def column(offset):
        return pl.BlockSpec((rows, BLOCK), lambda pair, place, source: (0, offset + pair))

    return [column(0), column(pairs), column(2 * pairs)]


def attend_forward(places, source, qkv, base, width):
    rows = qkv.shape[0]
    chunks = rows // NEAR
    own = pl.BlockSpec((NEAR, BLOCK), lambda pair, place, source: (0, pair))
    return pl.pallas_call(
        forward_kernel,
        grid_spec=pltpu.PrefetchScalarGridSpec(
            num_scalar_prefetch=2,
            grid=(PAIRS,),
            in_specs=pair_specs(rows, width)
            + [pl.BlockSpec((1, 8, SPAN), lambda pair, place, source: (pair, 0, 0))],
            out_specs=[
                own,
                own,
                pl.BlockSpec((1, 2, NEAR, BLOCK), lambda pair, place, source: (pair, 0, 0, 0)),
                pl.BlockSpec((1, 8, NEAR), lambda pair, place, source: (pair, 0, 0)),
            ],
            scratch_shapes=[
                pltpu.VMEM((chunks, NEAR, NEAR), F32),
                pltpu.VMEM((NEAR, NEAR), F32),
            ],
        ),
        out_shape=[
            jax.ShapeDtypeStruct((NEAR, width), BF16),
            jax.ShapeDtypeStruct((NEAR, width), F32),
            jax.ShapeDtypeStruct((PAIRS, 2, NEAR, BLOCK), F32),
            jax.ShapeDtypeStruct((PAIRS, 8, NEAR), F32),
        ],
        compiler_params=pltpu.CompilerParams(vmem_limit_bytes=40 << 20),
        name="attend_forward",
    )(places, source, qkv, qkv, qkv, base)


def query_kernel(
    place_ref, source_ref, q_ref, k_ref, v_ref, base_ref, do_ref, exact_ref, lse_ref, dq_ref, sums_ref, bias_ref, near_ref
):
    bias_ref[...] = near_bias(base_ref)
    lanes = lane_ids(2 * BLOCK, NEAR)
    far = jnp.zeros((2 * BLOCK, BLOCK), F32)
    for own in range(2):
        block = place_ref[own]
        rows = pl.ds(own * BLOCK, BLOCK)
        stacked = stack_heads(q_ref[rows_at(source_ref[block + 1]), :])
        grads = stack_heads(do_ref[rows, :])
        exact = exact_ref[rows, :]
        product = grads.astype(F32) * jnp.concatenate([exact, exact], axis=0)
        delta = jnp.sum(product, axis=-1, keepdims=True)
        lse = lse_ref[0, own][:, :1]

        def grad_scores(scores, start):
            weights = jnp.exp(scores - lse)
            return weights * (dot(grads, two_tiles(v_ref, source_ref, start), 1, 1) - delta)

        scores = dot(stacked, two_tiles(k_ref, source_ref, block), 1, 1) + bias_ref[...]
        scores = jnp.where(lanes + block * BLOCK < BLOCK, MASKED, scores)
        near = grad_scores(scores, block)
        if own == 0:
            near_ref[...] = near
        else:
            near_ref[...] += near

        def step(chunk, carry):
            grad_q, far = carry
            start = block - 2 * chunk
            keys = two_tiles(k_ref, source_ref, start)
            part = dot(stacked, keys, 1, 1)
            part = jnp.where(lanes + start * BLOCK < BLOCK, MASKED, part)
            grad_s = grad_scores(part, start)
            return (grad_q + dot(grad_s.astype(BF16), keys), far + fold_lanes(grad_s, jnp.add))

        grad_q, far = lax.fori_loop(
            1,
            jnp.maximum(block, 1) // 2 + 1,
            step,
            (dot(near.astype(BF16), two_tiles(k_ref, source_ref, block)), far),
        )
        dq_ref[rows, :] = merge_heads(grad_q).astype(BF16)
    row_ids = lax.broadcasted_iota(jnp.int32, (BLOCK, SPAN), 0)
    for head in range(2):
        part = near_ref[head * BLOCK : (head + 1) * BLOCK, :]
        part = jnp.concatenate([part, jnp.zeros((BLOCK, BLOCK), F32)], axis=1)
        for bit in range(BLOCK.bit_length() - 1):
            moved = pltpu.roll(part, SPAN - (1 << bit), 1)
            part = jnp.where((row_ids >> bit) & 1 == 1, moved, part)
        sums_ref[0, head : head + 1, :] = jnp.sum(part, axis=0, keepdims=True)
        far_part = jnp.sum(far[head * BLOCK : (head + 1) * BLOCK], axis=0, keepdims=True)
        sums_ref[0, 2 + head : 3 + head, :] = jnp.concatenate(
            [far_part, jnp.zeros((1, NEAR), F32)], axis=1
        )
    sums_ref[0, 4:8, :] = jnp.zeros((4, SPAN), F32)


def attend_queries(places, source, qkv, base, grad_out, exact, lse):
    rows, width = qkv.shape[0], grad_out.shape[1]
    own = pl.BlockSpec((NEAR, BLOCK), lambda pair, place, source: (0, pair))
    row_spec = pl.BlockSpec((1, 8, SPAN), lambda pair, place, source: (pair, 0, 0))
    return pl.pallas_call(
        query_kernel,
        grid_spec=pltpu.PrefetchScalarGridSpec(
            num_scalar_prefetch=2,
            grid=(PAIRS,),
            in_specs=pair_specs(rows, width)
            + [
                row_spec,
                own,
                own,
                pl.BlockSpec((1, 2, NEAR, BLOCK), lambda pair, place, source: (pair, 0, 0, 0)),
            ],
            out_specs=[own, row_spec],
            scratch_shapes=[pltpu.VMEM((NEAR, NEAR), F32), pltpu.VMEM((NEAR, NEAR), F32)],
        ),
        out_shape=[
            jax.ShapeDtypeStruct((NEAR, width), BF16),
            jax.ShapeDtypeStruct((PAIRS, 8, SPAN), F32),
        ],
        compiler_params=pltpu.CompilerParams(vmem_limit_bytes=40 << 20),
        name="attend_queries",
    )(places, source, qkv, qkv, qkv, base, grad_out, exact, lse)


def key_kernel(place_ref, source_ref, q_ref, k_ref, v_ref, base_ref, do_ref, stats_ref, dk_ref, dv_ref, bias_ref):
    bias_ref[...] = near_bias(base_ref)
    blocks = q_ref.shape[0] // BLOCK
    lanes = lane_ids(2 * BLOCK, NEAR)

    def spread(row, start):
        window = jnp.concatenate(
            [
                stats_ref[source_ref[tile] // 2, 0, row : row + 2, rows_at(source_ref[tile] % 2)]
                for tile in (start, start + 1)
            ],
            axis=1,
        )
        return jnp.concatenate(
            [
                jnp.broadcast_to(window[:1], (BLOCK, NEAR)),
                jnp.broadcast_to(window[1:], (BLOCK, NEAR)),
            ],
            axis=0,
        )

    for own in range(2):
        block = place_ref[own]
        rows = pl.ds(own * BLOCK, BLOCK)
        keys = stack_heads(k_ref[rows_at(source_ref[block + 1]), :])
        values = stack_heads(v_ref[rows_at(source_ref[block + 1]), :])

        def grads(scores, start):
            queries, grad_out = two_tiles(q_ref, source_ref, start), two_tiles(do_ref, source_ref, start)
            scores = jnp.where((start == blocks) & (lanes >= BLOCK), MASKED, scores)
            weights = jnp.exp(scores - spread(0, start))
            grad_s = weights * (dot(values, grad_out, 1, 1) - spread(2, start))
            return dot(grad_s.astype(BF16), queries), dot(weights.astype(BF16), grad_out)

        def step(chunk, carry):
            start = block + 1 + 2 * chunk
            more_k, more_v = grads(dot(keys, two_tiles(q_ref, source_ref, start), 1, 1), start)
            return (carry[0] + more_k, carry[1] + more_v)

        near = dot(keys, two_tiles(q_ref, source_ref, block + 1), 1, 1) + bias_ref[...]
        chunks = jnp.maximum(blocks - 1 - block, 0) // 2
        grad_k, grad_v = lax.fori_loop(1, chunks + 1, step, grads(near, block + 1))
        dk_ref[rows, :] = merge_heads(grad_k).astype(BF16)
        dv_ref[rows, :] = merge_heads(grad_v).astype(BF16)


def attend_keys(places, source, qkv, base, grad_out, stats):
    rows, width = grad_out.shape
    own = pl.BlockSpec((NEAR, BLOCK), lambda pair, place, source: (0, pair))
    return pl.pallas_call(
        key_kernel,
        grid_spec=pltpu.PrefetchScalarGridSpec(
            num_scalar_prefetch=2,
            grid=(PAIRS,),
            in_specs=pair_specs(rows, width)
            + [
                pl.BlockSpec((1, 8, SPAN), lambda pair, place, source: (pair, 0, 0)),
                pl.BlockSpec((rows, BLOCK), lambda pair, place, source: (0, pair)),
                pl.BlockSpec(
                    (rows // NEAR, 1, 8, NEAR), lambda pair, place, source: (0, pair, 0, 0)
                ),
            ],
            out_specs=[own, own],
            scratch_shapes=[pltpu.VMEM((NEAR, NEAR), F32)],
        ),
        out_shape=[jax.ShapeDtypeStruct((NEAR, width), BF16)] * 2,
        compiler_params=pltpu.CompilerParams(vmem_limit_bytes=40 << 20),
        name="attend_keys",
    )(places, source, qkv, qkv, qkv, base, grad_out, stats)


BITS = {"core": ("wsh", 1), "x": ("wsh", 2), "y": ("ctx", 1), "near": ("ctx", 2), "far": ("ctx", 4)}
ORDERS = (
    ("core", "x", "near", "y", "far"),
    ("core", "x", "y", "near", "far"),
    ("core", "y", "near", "x", "far"),
    ("core", "near", "y", "x", "far"),
)


def halved_shapes(order, share, width):
    shapes, blocks, rows, columns = [], 4, share, width
    for name in order:
        if name in ("core", "x"):
            blocks //= 2
        elif name == "y":
            columns //= 2
        else:
            rows //= 2
        shapes.append((blocks, rows, columns))
    return shapes


def partner(name):
    axis, bit = BITS[name]
    me = lax.axis_index(axis)
    side = (me // bit) % 2
    return axis, me + bit * (1 - 2 * side), side


def tail_kernel(
    experts,
    dq_ref,
    dk_ref,
    dv_ref,
    hidden_ref,
    grad_mid_ref,
    weights_ref,
    grad_wo_ref,
    small_ref,
    router_ref,
    gain_ref,
    sums_ref,
    hot_ref,
    input_grad_out,
    wq_out,
    wk_out,
    wv_out,
    wo_out,
    router_out,
    gains_out,
    table_out,
    weights,
    hidden,
    grad_mid,
    grad_wo,
    total,
    gathered,
    pack,
    pack_recv,
    *rest,
):
    steps = len(BITS)
    sends = [rest[matrix * steps : (matrix + 1) * steps] for matrix in range(4)]
    rest = rest[4 * steps :]
    recvs = [rest[matrix * steps : (matrix + 1) * steps] for matrix in range(4)]
    fetch_sems, half_send, half_recv, whole_send, whole_recv, pack_send, pack_sem = rest[4 * steps :]
    tokens, width = dq_ref.shape
    share = total.shape[2]
    sources = (
        (hidden_ref, hidden),
        (grad_wo_ref, grad_wo),
        (weights_ref.at[pl.ds(0, 3)], weights),
        (grad_mid_ref, grad_mid),
    )
    fetches = [
        pltpu.make_async_copy(src, dst, fetch_sems.at[place])
        for place, (src, dst) in enumerate(sources)
    ]
    for fetch in fetches:
        fetch.start()
    barrier = pltpu.get_barrier_semaphore()
    for name in BITS:
        axis, peer, side = partner(name)
        pl.semaphore_signal(
            barrier, inc=1, device_id={axis: peer}, device_id_type=pl.DeviceIdType.MESH
        )
    pl.semaphore_wait(barrier, steps)

    def remote(source, target, send, recv, name):
        axis, peer, side = partner(name)
        return pltpu.make_async_remote_copy(
            src_ref=source,
            dst_ref=target,
            send_sem=send,
            recv_sem=recv,
            device_id={axis: peer},
            device_id_type=pl.DeviceIdType.MESH,
        )

    regions = []
    for order in ORDERS:
        blocks, row, column, kept = [0, 1, 2, 3], 0, 0, []
        rows, columns = share, width
        for name in order:
            side = partner(name)[2]
            if name == "core":
                pair = [(line * 2 + side, line * 2 + 1 - side) for line in range(2)]
                keep = ([a for a, b in pair], row, column)
                sent = ([b for a, b in pair], row, column)
            elif name == "x":
                core = partner("core")[2]
                keep = ([side * 2 + core], row, column)
                sent = ([(1 - side) * 2 + core], row, column)
            elif name == "y":
                columns //= 2
                keep = (blocks, row, column + side * columns)
                sent = (blocks, row, column + (1 - side) * columns)
            else:
                rows //= 2
                keep = (blocks, row + side * rows, column)
                sent = (blocks, row + (1 - side) * rows, column)
            blocks, row, column = keep
            kept.append((keep, sent))
        regions.append(kept)

    def spans(matrix, step, region):
        shape = sends[matrix][step].shape
        blocks, row, column = region
        row_part = pl.ds(row if isinstance(row, int) else pl.multiple_of(row, 16), shape[1])
        column_part = pl.ds(
            column if isinstance(column, int) else pl.multiple_of(column, BLOCK), shape[2]
        )
        return blocks, row_part, column_part

    def half_copy(matrix, step):
        return remote(
            sends[matrix][step],
            recvs[matrix][step],
            half_send.at[matrix, step],
            half_recv.at[matrix, step],
            ORDERS[matrix][step],
        )

    def give(matrix, step):
        blocks, row_part, column_part = spans(matrix, step, regions[matrix][step][1])
        for place, block in enumerate(blocks):
            sends[matrix][step][place] = total[matrix, block, row_part, column_part].astype(BF16)
        half_copy(matrix, step).start()

    def take(matrix, step):
        half_copy(matrix, step).wait_recv()
        blocks, row_part, column_part = spans(matrix, step, regions[matrix][step][0])
        for place, block in enumerate(blocks):
            total[matrix, block, row_part, column_part] += recvs[matrix][step][place].astype(F32)

    def whole_view(matrix, step):
        keep = regions[matrix][step][0]
        blocks, row_part, column_part = spans(matrix, step, keep)
        return gathered.at[matrix, row_part, column_part]

    wholes = [[name for name in order if BITS[name][0] == "ctx"] for order in ORDERS]

    def whole_copy(matrix, back):
        name = wholes[matrix][2 - back]
        step = ORDERS[matrix].index(name)
        blocks, row, column = regions[matrix][step][0]
        shape = sends[matrix][step].shape
        row_part = pl.ds(row if isinstance(row, int) else pl.multiple_of(row, 16), shape[1])
        column_part = pl.ds(
            column if isinstance(column, int) else pl.multiple_of(column, BLOCK), shape[2]
        )
        view = gathered.at[matrix, row_part, column_part]
        return remote(view, view, whole_send.at[matrix, back], whole_recv.at[matrix, back], name)

    fetches[0].wait()
    resid = hidden[...].astype(F32)
    inv = lax.rsqrt(jnp.mean(resid * resid, axis=-1, keepdims=True) + epsilon)
    gain = jnp.transpose(small_ref[...].astype(F32))[experts : experts + 1, :]
    normed = (resid * inv * gain).astype(BF16)
    for matrix, ref in ((1, dq_ref), (2, dk_ref), (3, dv_ref)):
        part = dot(normed, ref[...], 0, 0)
        for block in range(4):
            total[matrix, block] = part[block * share : (block + 1) * share]
        give(matrix, 0)
    fetches[1].wait()
    for block in range(4):
        total[0, block] = grad_wo[block * share : (block + 1) * share, :].astype(F32)
    give(0, 0)
    fetches[2].wait()
    grad_normed = dot(dq_ref[...], weights[0], 1, 1)
    grad_normed = grad_normed + dot(dk_ref[...], weights[1], 1, 1)
    grad_normed = grad_normed + dot(dv_ref[...], weights[2], 1, 1)
    pack[...] = jnp.zeros_like(pack)
    pack[:experts, :] = router_ref[...]
    pack[experts : experts + 1, :] = jnp.sum(grad_normed * resid * inv, axis=0, keepdims=True)
    pack[experts + 1 : experts + 2, :] = gain_ref[0:1, :]
    last = lane_ids(2, BLOCK) == hot_ref.shape[1] - 1
    for pair in range(PAIRS):
        near = lax.dot_general(
            sums_ref[pair, 0:2, :],
            hot_ref[...],
            (((1,), (0,)), ((), ())),
            precision=HIGH,
            preferred_element_type=F32,
        )
        near = jnp.concatenate([near, jnp.zeros((2, BLOCK - near.shape[1]), F32)], axis=1)
        distant = jnp.sum(sums_ref[pair, 2:4, :], axis=1, keepdims=True)
        place = experts + 8 + 2 * pair
        pack[place : place + 2, :BLOCK] = near + jnp.where(last, distant, 0.0)

    def pack_copy(step):
        return remote(
            pack_recv.at[0, step],
            pack_recv.at[1, step],
            pack_send.at[step],
            pack_sem.at[step],
            list(BITS)[step],
        )

    for step in range(steps):
        pack_recv[0, step] = pack[...]
        pack_copy(step).start()
        for matrix in (1, 2, 3, 0):
            take(matrix, step)
            if step + 1 < steps:
                give(matrix, step + 1)
        if step == 0:
            fetches[3].wait()
            scaled = grad_normed * gain
            mean = jnp.mean(scaled * resid, axis=-1, keepdims=True)
            grad_in = grad_mid[...] + inv * scaled - resid * inv * inv * inv * mean
            input_grad_out[...] = grad_in.astype(BF16)
        pack_copy(step).wait_recv()
        pack[...] += pack_recv[1, step]

    outs = (wo_out, wq_out, wk_out, wv_out)
    mine = lax.axis_index("wsh")
    for matrix in range(4):
        keep = regions[matrix][steps - 1][0]
        blocks, row_part, column_part = spans(matrix, steps - 1, keep)
        gathered[matrix, row_part, column_part] = total[
            matrix, blocks[0], row_part, column_part
        ].astype(BF16)
        whole_copy(matrix, 0).start()
    for back in range(3):
        for matrix in range(4):
            whole_copy(matrix, back).wait_recv()
            if back < 2:
                whole_copy(matrix, back + 1).start()
            else:
                outs[matrix][...] = gathered[matrix].astype(F32)
        if back == 0:
            buckets = table_out.shape[0]
            for block in range(4):

                @pl.when(mine == block)
                def _():
                    rows = pack[: experts + 8, block * share : (block + 1) * share]
                    turned = jnp.transpose(rows)
                    router_out[...] = turned[:, :experts]
                    gains_out[...] = rows[experts : experts + 8]
                    table = jnp.transpose(pack[experts + 8 :, :BLOCK])
                    table_out[...] = table[block * buckets : (block + 1) * buckets, :HEADS]

    for step in range(steps):
        pack_copy(step).wait_send()
        for matrix in range(4):
            half_copy(matrix, step).wait_send()
    for back in range(3):
        for matrix in range(4):
            whole_copy(matrix, back).wait_send()


def tail(experts, dq, dk, dv, hidden, grad_mid, weights, grad_wo, small, router, gains, sums, hot, share, buckets):
    tokens, width = dq.shape
    vmem = pl.BlockSpec(memory_space=pltpu.VMEM)
    anywhere = pl.BlockSpec(memory_space=pl.ANY)
    steps = len(BITS)
    pieces = [shape for order in ORDERS for shape in halved_shapes(order, share, width)]
    buffers = [pltpu.VMEM(shape, BF16) for shape in pieces]
    rows = experts + 8 + 16
    dma = pltpu.SemaphoreType.DMA
    return pl.pallas_call(
        functools.partial(tail_kernel, experts),
        in_specs=[vmem] * 3 + [anywhere] * 4 + [vmem] * 5,
        out_specs=[vmem] * 8,
        out_shape=[
            jax.ShapeDtypeStruct((tokens, width), BF16),
            *[jax.ShapeDtypeStruct((share, width), F32)] * 4,
            jax.ShapeDtypeStruct((share, experts), F32),
            jax.ShapeDtypeStruct((8, share), F32),
            jax.ShapeDtypeStruct((buckets, HEADS), F32),
        ],
        scratch_shapes=[
            pltpu.VMEM((3, width, width), BF16),
            pltpu.VMEM((tokens, width), BF16),
            pltpu.VMEM((tokens, width), F32),
            pltpu.VMEM((width, width), BF16),
            pltpu.VMEM((4, 4, share, width), F32),
            pltpu.VMEM((4, share, width), BF16),
            pltpu.VMEM((rows, width), F32),
            pltpu.VMEM((2, steps, rows, width), F32),
            *buffers,
            *buffers,
            dma((4,)),
            dma((4, steps)),
            dma((4, steps)),
            dma((4, 3)),
            dma((4, 3)),
            dma((steps,)),
            dma((steps,)),
        ],
        compiler_params=pltpu.CompilerParams(
            collective_id=2, has_side_effects=True, vmem_limit_bytes=56 << 20
        ),
        name="tail",
    )(dq, dk, dv, hidden, grad_mid, weights, grad_wo, small, router, gains, sums, hot)


def rms_forward(values, gain_vec):
    inv_rms = lax.rsqrt(jnp.mean(values * values, axis=-1, keepdims=True) + epsilon)
    return (values * inv_rms * gain_vec, inv_rms)


def rms_backward(values, inv_rms, gain_vec, upstream):
    grad_gain = jnp.sum(upstream * values * inv_rms, axis=0)
    scaled = upstream * gain_vec
    grad_values = inv_rms * scaled - values * inv_rms**3 * jnp.mean(
        scaled * values, axis=-1, keepdims=True
    )
    return (grad_values, grad_gain)


def per_device(
    hidden_in,
    w_query,
    w_key,
    w_value,
    w_output,
    w_router,
    gain_attn,
    gain_moe,
    rel_bias,
    w_in,
    w_out,
    routes,
    block_pairs,
    cotangent,
):
    tokens, width = hidden_in.shape[1:]
    ctx_count, wsh_count = lax.axis_size("ctx"), lax.axis_size("wsh")
    ctx_rank, wsh_rank = lax.axis_index("ctx"), lax.axis_index("wsh")
    length = tokens * ctx_count
    blocks = length // BLOCK
    experts, exp_dev = w_router.shape[1], w_in.shape[0]
    slot_most = 2 * tokens // experts
    capacity = (9 * length // (8 * experts) + 7) // 8 * 8

    def over(axis, array, dim=0):
        return lax.all_gather(array, axis, axis=dim, tiled=True)

    share = width // wsh_count
    small = jnp.concatenate(
        [
            w_router,
            gain_attn[:, None],
            gain_moe[:, None],
            jnp.pad(rel_bias, ((0, share - rel_bias.shape[0]), (0, 0))),
        ],
        axis=1,
    )
    small = jnp.pad(small, ((0, 0), (0, BLOCK - small.shape[1])))
    qkv, weights, small, slot_rows, targets, own_g = project(
        (ctx_count, wsh_count),
        capacity,
        experts,
        slot_most,
        hidden_in[0],
        (w_query, w_key, w_value, w_output),
        small,
        routes.reshape(1, tokens),
        cotangent[0],
    )
    full_query, full_key, full_value, full_output = (weights[place] for place in range(4))
    full_router = small[:, :experts]
    gain_one = small[:, experts].astype(F32)
    gain_two = small[:, experts + 1].astype(F32)
    full_bias = small.reshape(wsh_count, share, BLOCK)[
        :, : rel_bias.shape[0], experts + 2 : experts + 2 + HEADS
    ].reshape(-1, HEADS)

    order = block_pairs.reshape(-1)
    places = lax.dynamic_slice_in_dim(order, 2 * ctx_rank, 2)
    ids = jnp.arange(blocks, dtype=jnp.int32)
    inverse = jnp.sum(jnp.where(order[None, :] == ids[:, None], ids[None, :], 0), axis=1)
    source = jnp.pad(inverse, (1, 1))

    buckets = full_bias.shape[0]
    lanes = wrapped_lanes()
    query_hot = onehot_of(BLOCK - lanes, buckets)
    key_hot = onehot_of(lanes, buckets)

    def base_rows(hot, distance):
        table = dot(full_bias, jnp.asarray(hot, BF16), 0, 1)
        table = table - full_bias[buckets - 1].astype(F32)[:, None]
        table = jnp.where(jnp.asarray(distance >= 0)[None, :], table, MASKED)
        return jnp.pad(table.reshape(PAIRS, 2, SPAN), ((0, 0), (0, 6), (0, 0)))

    query_base = base_rows(query_hot, BLOCK - lanes)
    key_base = base_rows(key_hot, lanes)

    attn_low, attn_exact, lse, lse_rows = attend_forward(places, source, qkv, query_base, width)
    (
        output_rows,
        grad_mid,
        grad_heads,
        heads_all,
        stats,
        grad_wo,
        grad_router,
        grad_gain_m,
        grad_w_in,
        grad_w_out,
    ) = middle(
        (ctx_count, wsh_count),
        experts,
        attn_low,
        attn_exact,
        hidden_in[0],
        cotangent[0],
        weights,
        w_in,
        w_out,
        own_g,
        small,
        slot_rows,
        targets,
        lse_rows,
        routes.reshape(tokens, 1),
    )

    if heads_all.shape[0] == tokens:
        heads_all = dot(over("ctx", heads_all), full_output, 1, 1).astype(BF16)
        stats = over("ctx", stats)

    grad_q, sums = attend_queries(places, source, qkv, query_base, grad_heads, attn_exact, lse)
    grad_k, grad_v = attend_keys(places, source, qkv, key_base, heads_all, stats)

    bucket_share = buckets // wsh_count
    if ctx_count == 8 and wsh_count == 4 and share % 64 == 0:
        grad_input, grad_a, grad_b, grad_c, grad_d, own_router, own_gains, own_table = tail(
            experts,
            grad_q,
            grad_k,
            grad_v,
            hidden_in[0],
            grad_mid,
            weights,
            grad_wo,
            small,
            grad_router,
            grad_gain_m,
            sums,
            jnp.asarray(query_hot),
            share,
            bucket_share,
        )
        return (
            output_rows[None],
            grad_input[None],
            grad_a,
            grad_b,
            grad_c,
            grad_d,
            own_router,
            own_gains[0],
            own_gains[1],
            own_table,
            grad_w_in,
            grad_w_out,
        )

    near_sums = sums[:, :2].reshape(HEADS, SPAN)
    far_sums = jnp.sum(sums[:, 2:4].reshape(HEADS, SPAN), axis=1)
    grad_table = jnp.dot(jnp.asarray(query_hot.T), near_sums.T, precision=HIGH)
    grad_table = grad_table.at[buckets - 1].add(far_sums)

    resid_in = hidden_in[0].astype(F32)
    normed_one, inv_one = rms_forward(resid_in, gain_one)
    normed_one = normed_one.astype(BF16)
    grad_normed_one = dot(grad_q, full_query, 1, 1)
    grad_normed_one = grad_normed_one + dot(grad_k, full_key, 1, 1)
    grad_normed_one = grad_normed_one + dot(grad_v, full_value, 1, 1)
    grad_in_norm, grad_gain_a = rms_backward(resid_in, inv_one, gain_one, grad_normed_one)
    grad_input = (grad_mid + grad_in_norm).astype(BF16)

    def reduce_weight(grad):
        part = lax.psum_scatter(grad.astype(BF16), "wsh", scatter_dimension=0, tiled=True)
        return lax.psum(part, "ctx").astype(F32)

    grad_wq = dot(normed_one, grad_q, 0, 0)
    grad_wk = dot(normed_one, grad_k, 0, 0)
    grad_wv = dot(normed_one, grad_v, 0, 0)
    shares = [reduce_weight(grad) for grad in (grad_wq, grad_wk, grad_wv, grad_wo)]
    columns = jnp.concatenate(
        [grad_router.T, grad_gain_a[:, None], grad_gain_m[0][:, None]], axis=1
    )
    table = jnp.pad(grad_table, ((0, 0), (0, columns.shape[1] - HEADS)))
    summed = lax.psum(jnp.concatenate([columns, table], axis=0), ("ctx", "wsh"))
    own_columns = lax.dynamic_slice_in_dim(summed[:width], wsh_rank * share, share, 0)
    own_table = lax.dynamic_slice_in_dim(
        summed[width:, :HEADS], wsh_rank * bucket_share, bucket_share, 0
    )
    return (
        output_rows.astype(BF16)[None],
        grad_input[None],
        *shares,
        own_columns[:, :experts],
        own_columns[:, experts],
        own_columns[:, experts + 1],
        own_table,
        grad_w_in,
        grad_w_out,
    )


def solution(mesh):
    in_specs = (
        P("wsh", "ctx", None),
        P("wsh", None),
        P("wsh", None),
        P("wsh", None),
        P("wsh", None),
        P("wsh", None),
        P("wsh"),
        P("wsh"),
        P("wsh", None),
        P("ctx", None, "wsh"),
        P("ctx", "wsh", None),
        P("wsh", "ctx", None),
        P(),
        P("wsh", "ctx", None),
    )
    out_specs = (
        P("wsh", "ctx", None),
        P("wsh", "ctx", None),
        P("wsh", None),
        P("wsh", None),
        P("wsh", None),
        P("wsh", None),
        P("wsh", None),
        P("wsh"),
        P("wsh"),
        P("wsh", None),
        P("ctx", None, "wsh"),
        P("ctx", "wsh", None),
    )
    return jax.shard_map(
        per_device, mesh=mesh, in_specs=in_specs, out_specs=out_specs, check_vma=False
    )
```

time: 618 us -> 395 us (0.64)
  Pallas kernels: 105 us -> 341 us
  waiting for transfers between devices: 211 us -> 0 us
  blocking collectives: 138 us -> 0 us
  matrix products: 57.9 us -> 2.05 us
  other arithmetic: 27.8 us -> 0.83 us
  between operations: 15.7 us -> 0.9 us
  starting transfers between devices: 12.8 us -> 0 us
    pallas_call x2 -> x3, Pallas kernels: 17.7 us -> 253 us  [the longest x1 131 us: middle(): pl.pallas_call(functools.partial(middle_kernel, counts, experts, spread_h...]
    all_gather x8 -> x0, waiting for transfers between devices: 98.6 us -> none  [the longest x6 83.5 us: over(): return lax.all_gather(array, axis, axis=dim, tiled=True)]
    reduce_scatter x6 -> x0, waiting for transfers between devices: 72.3 us -> none  [the longest x2 55.4 us: sum_slots(): lax.psum_scatter(jnp.swapaxes(parts, 0, 1), 'wsh', scatter_dimension=0, t...]
    all_to_all x2 -> x0, blocking collectives: 48.8 us -> none  [the longest x1 25.6 us: bring_back(): lax.all_to_all(returning, 'ctx', split_axis=0, concat_axis=0, tiled=True)]
    psum x1 -> x0, blocking collectives: 41.3 us -> none  [per_device(): summed = lax.psum(jnp.concatenate([columns, table], axis=0), ('ctx', 'wsh'))]
    psum x1 -> x0, waiting for transfers between devices: 36.5 us -> none  [reduce_weight(): return lax.psum(part, 'ctx').astype(F32)]
    all_gather x2 -> x0, blocking collectives: 36.1 us -> none  [the longest x1 30.6 us: over(): return lax.all_gather(array, axis, axis=dim, tiled=True)]
    dot_general x11 -> x0, matrix products: 27.8 us -> none  [the longest x1 7.3 us: per_device(): jnp.einsum('ecf,ecd->efd', hidden_act, grad_slots, preferred_element_type...]
  transfers between devices with their start and end apart: 17 -> 0, of which waited for: 8 -> 0; matrix products, arithmetic and copies ran while one was open for 13% -> 0% of each run, Pallas kernels for 17% -> 0%
where the time goes in v2:
time: 395 us; the launch traced here: 394 us
  Pallas kernels  341 us (86%)
  local copies, waits for them, and re-layouts  48.5 us (12%)
    pallas_call x1, Pallas kernels, middle(): pl.pallas_call(functools.partial(middle_kernel, counts, experts, spread_h...  131 us
    pallas_call x1, Pallas kernels, project(): pl.pallas_call(functools.partial(project_kernel, counts, capacity), in_sp...  62.1 us
    pallas_call x1, Pallas kernels, tail(): pl.pallas_call(functools.partial(tail_kernel, experts), in_specs=[vmem] *...  59.5 us
    unnamed x78, local copies, waits for them, and re-layouts  44.4 us
    pallas_call x1, Pallas kernels, attend_queries(): pl.pallas_call(query_kernel, grid_spec=pltpu.PrefetchScalarGridSpec(num_s...  33.7 us
    pallas_call x1, Pallas kernels, attend_forward(): pl.pallas_call(forward_kernel, grid_spec=pltpu.PrefetchScalarGridSpec(num...  29.9 us
    pallas_call x1, Pallas kernels, attend_keys(): pl.pallas_call(key_kernel, grid_spec=pltpu.PrefetchScalarGridSpec(num_sca...  24.9 us

profile of v2, /device:TPU:0, one launch (start us, length us, event | category | flops | bytes accessed | tf_op | source)
XLA Modules:
  0.0 393.6 jit_solution(7068061612837620186)
XLA Ops:
  0.6 0.8 copy.46
  1.4 0.7 broadcast_in_dim.50
  2.1 0.7 broadcast_in_dim.51
  2.7 0.7 fusion.3
  3.4 0.1 copy.47
  3.6 1.0 copy-done.3
  4.6 1.0 copy-done.7
  5.6 1.0 copy-done.16
  6.5 1.0 copy-done.17
  7.5 1.0 copy-done.18
  8.5 1.0 copy-done.19
  9.4 0.7 copy-done.24
  10.1 62.1 %project.1 = (bf16[2048,2304]{1,0:T(8,128)(2,1)}, bf16[4,768,768]{2,1,0:T(8,128)(2,1)S(1)}, bf16[768,128]{1,0:T(8,128)(2,1)S(1)}, s32[8,256]{1,0:T(8,128)S(1)}, ...) custom-call(bf16[256,768]{1,0:T(8,128)(2,1)S(1)} %bitcast.22, bf16[192,768]{1,0:T(8,128)(2,1)S(1)} %copy-done.16, ...), custom_call_target="tpu_custom_call" | custom-call | tf_op jit(solution)/shard_map/project/pallas_call | solution.py:463
  72.3 2.2 copy-done.2
  74.4 0.8 copy-done.9
  75.2 0.6 copy-done.22
  75.8 0.6 copy-done.23
  76.5 1.1 fusion.1
  77.7 0.8 copy.45
  78.4 0.1 reshape.55
  78.6 0.1 select_reduce_fusion
  78.8 3.7 copy-done
  82.5 29.9 %attend_forward.1 = (bf16[256,768]{1,0:T(8,128)(2,1)S(1)}, f32[256,768]{1,0:T(8,128)S(1)}, f32[6,2,256,128]{3,2,1,0:T(8,128)S(1)}, f32[6,8,256]{2,1,0:T(8,128)S(1)}) custom-call(s32[2]{0:T(128)S(1)} %dynamic_slice.3.place_ref, s32[18]{0:T(128)S(1)} %pad.19.source_ref, bf16[2048,2304]{1,0:T(8,128)(2,1)S(1)} %copy-done, bf16[2048,2304]{1,0:T(8,128)(2,1)S(1)} %copy-done, ...), custom_call_target="tpu_custom_call" | custom-call | tf_op jit(solution)/shard_map/attend_forward/pallas_call | solution.py:1109
  112.4 0.9 copy-done.4
  113.3 0.7 copy-done.15
  114.0 0.6 copy-done.21
  114.6 0.8 copy.48.routes_ref
  115.4 131.3 %middle.1 = (bf16[256,768]{1,0:T(8,128)(2,1)}, f32[256,768]{1,0:T(8,128)}, bf16[256,768]{1,0:T(8,128)(2,1)}, bf16[2048,768]{1,0:T(8,128)(2,1)}, f32[8,6,8,256]{3...) custom-call(bf16[256,768]{1,0:T(8,128)(2,1)} %copy-done.15, ...), custom_call_target="tpu_custom_call" | custom-call | tf_op jit(solution)/shard_map/middle/pallas_call | solution.py:968
  246.8 0.9 fusion
  247.8 3.7 copy-done.1
  251.5 1.9 copy-done.6
  253.4 1.0 copy-done.11
  254.4 24.9 %attend_keys.1 = (bf16[256,768]{1,0:T(8,128)(2,1)S(1)}, bf16[256,768]{1,0:T(8,128)(2,1)S(1)}) custom-call(s32[2]{0:T(128)S(1)} %dynamic_slice.3.place_ref, s32[18]{0:T(128)S(1)} %pad.19.source_ref, bf16[2048,2304]{1,0:T(8,128)(2,1)S(1)} %copy-done.1, bf16[2048,2304]{1,0:T(8,128)(2,1)S(1)} %copy-done.1, bf16[2048,2304]{1,0:T(8,128)(2,1)S(1)} %copy-done.1, ...), custom_call_target="tpu_custom_call" | custom-call | tf_op jit(solution)/shard_map/attend_keys/pallas_call | solution.py:1274
  279.3 33.7 %attend_queries.1 = (bf16[256,768]{1,0:T(8,128)(2,1)S(1)}, f32[6,8,384]{2,1,0:T(8,128)S(1)}) custom-call(s32[2]{0:T(128)S(1)} %dynamic_slice.3.place_ref, s32[18]{0:T(128)S(1)} %pad.19.source_ref, bf16[2048,2304]{1,0:T(8,128)(2,1)S(1)} %copy-done.1, bf16[2048,2304]{1,0:T(8,128)(2,1)S(1)} %copy-done.1, bf16[2048,2304]{1,0:T(8,128)(2,1)S(1)} %copy-done.1, ...), custom_call_target="tpu_custom_call" | custom-call | tf_op jit(solution)/shard_map/attend_queries/pallas_call | solution.py:1201
  313.0 0.7 copy-done.14
  313.8 0.6 copy-done.20
  314.4 59.5 %tail.1 = (bf16[256,768]{1,0:T(8,128)(2,1)}, f32[192,768]{1,0:T(8,128)}, f32[192,768]{1,0:T(8,128)}, f32[192,768]{1,0:T(8,128)}, f32[192,768]{1,0:T(8,128)}, /*i...) custom-call(bf16[256,768]{1,0:T(8,128)(2,1)} %copy-done.14, bf16[256,768]{1,0:T(8,128)(2,1)} %copy-done.12, ...), custom_call_target="tpu_custom_call" | custom-call | tf_op jit(solution)/shard_map/tail/pallas_call | solution.py:1578
  373.9 1.6 copy.49
  375.5 1.3 fusion.5
  376.9 0.7 copy.59
  377.6 1.8 copy.60
  379.4 1.9 copy.61
  381.3 1.9 copy.62
  383.2 1.9 copy.63
  385.1 0.8 copy.64
  386.0 0.6 copy.65
  386.6 4.9 %copy.66 = f32[2,768,768]{2,1,0:T(8,128)} copy(f32[2,768,768]{2,1,0:T(8,128)} %get-tuple-element.148) | data formatting | bytes 9437184
  391.5 2.2 copy.67
  (56 shorter events, 0.5 us)
Async XLA Ops:
  3.6 1.0 copy-start.3
  4.6 1.0 copy-start.7
  5.6 1.0 copy-start.16
  6.5 1.0 copy-start.17
  7.5 1.0 copy-start.18
  8.5 1.0 copy-start.19
  9.4 0.7 copy-start.24
  72.3 2.2 copy-start.2
  74.4 0.8 copy-start.9
  75.2 0.6 copy-start.22
  75.8 0.6 copy-start.23
  76.4 36.0 %copy-start.8 = (bf16[768,128]{1,0:T(8,128)(2,1)}, bf16[768,128]{1,0:T(8,128)(2,1)S(1)}, u32[]{:S(2)}) copy-start(bf16[768,128]{1,0:T(8,128)(2,1)S(1)} %get-tuple-element.45.small_ref) | copy-start | bytes 589828
  78.8 3.7 copy-start
  82.5 32.2 %copy-start.25 = (s32[1,256,1]{1,2,0:T(1,128)S(1)}, s32[1,256,1]{1,2,0:T(1,128)}, u32[]{:S(2)}) copy-start(s32[1,256,1]{1,2,0:T(1,128)} %param.30) | copy-start | bytes 3076
  112.4 0.9 copy-start.4
  113.3 0.7 copy-start.15
  114.0 0.6 copy-start.21
  115.4 131.3 %copy-start.29 = (bf16[384,32]{1,0:T(8,128)(2,1)S(1)}, bf16[384,32]{1,0:T(8,128)(2,1)}, u32[]{:S(2)}) copy-start(bf16[384,32]{1,0:T(8,128)(2,1)} %constant.30.clone) | copy-start | bytes 73732
  115.4 131.3 %copy-start.30 = (pred[384]{0:T(512)(128)(4,1)S(1)}, pred[384]{0:T(512)(128)(4,1)}, u32[]{:S(2)}) copy-start(pred[384]{0:T(512)(128)(4,1)} %constant.31.clone) | copy-start | bytes 1156
  247.8 3.7 copy-start.1
  251.5 1.9 copy-start.6
  253.4 1.0 copy-start.11
  254.4 24.9 %copy-start.5 = (f32[256,768]{1,0:T(8,128)S(1)}, f32[256,768]{1,0:T(8,128)}, u32[]{:S(2)}) copy-start(f32[256,768]{1,0:T(8,128)} %copy-done.4) | copy-start | bytes 2359300
  254.4 24.9 %copy-start.10 = (bf16[256,768]{1,0:T(8,128)(2,1)S(1)}, bf16[256,768]{1,0:T(8,128)(2,1)}, u32[]{:S(2)}) copy-start(bf16[256,768]{1,0:T(8,128)(2,1)} %get-tuple-element.54.do_ref) | copy-start | bytes 1179652
  279.2 33.8 %copy-start.12 = (bf16[256,768]{1,0:T(8,128)(2,1)}, bf16[256,768]{1,0:T(8,128)(2,1)S(1)}, u32[]{:S(2)}) copy-start(bf16[256,768]{1,0:T(8,128)(2,1)S(1)} %get-tuple-element.59.dk_ref) | copy-start | bytes 1179652
  279.3 33.8 %copy-start.13 = (bf16[256,768]{1,0:T(8,128)(2,1)}, bf16[256,768]{1,0:T(8,128)(2,1)S(1)}, u32[]{:S(2)}) copy-start(bf16[256,768]{1,0:T(8,128)(2,1)S(1)} %get-tuple-element.60.dv_ref) | copy-start | bytes 1179652
  313.0 0.7 copy-start.14
  313.8 0.6 copy-start.20
  314.4 62.5 %copy-start.27 = (bf16[256,768]{1,0:T(8,128)(2,1)S(1)}, bf16[256,768]{1,0:T(8,128)(2,1)}, u32[]{:S(2)}) copy-start(bf16[256,768]{1,0:T(8,128)(2,1)} %get-tuple-element.53) | copy-start | bytes 1179652
  373.9 11.3 %copy-start.26 = (f32[192,768]{1,0:T(8,128)S(1)}, f32[192,768]{1,0:T(8,128)}, u32[]{:S(2)}) copy-start(f32[192,768]{1,0:T(8,128)} %get-tuple-element.143) | copy-start | bytes 1769476
  373.9 12.1 %copy-start.28 = (f32[8,12]{1,0:T(8,128)S(1)}, f32[8,12]{1,0:T(8,128)}, u32[]{:S(2)}) copy-start(f32[8,12]{1,0:T(8,128)} %get-tuple-element.147) | copy-start | bytes 1156
  385.1 6.3 %slice-start = ((s8[4718592]{0:T(1024)(128)(4,1)}), s8[4194304]{0:T(1024)(128)(4,1)S(1)}, s32[]{:S(2)}) async-start(s8[4718592]{0:T(1024)(128)(4,1)} %bitcast.30), calls=%async_computation | async-start | bytes 8388608
  386.6 4.9 %slice-start.1 = ((s8[4718592]{0:T(1024)(128)(4,1)}), s8[524288]{0:T(1024)(128)(4,1)S(1)}, s32[]{:S(2)}) async-start(s8[4718592]{0:T(1024)(128)(4,1)} %bitcast.30), calls=%async_computation.1 | async-start | bytes 1048576

commit v3 on v2

--- a/solution.py
+++ b/solution.py
@@ -66,10 +66,10 @@
     return combine(tile[:, :BLOCK], tile[:, BLOCK:])
 
 
-def near_bias(base_ref):
+def near_bias(base_ref, place=0):
     tiles = []
     for head in range(2):
-        row = jnp.broadcast_to(base_ref[0, head : head + 1, :], (BLOCK, SPAN))
+        row = jnp.broadcast_to(base_ref[place, head : head + 1, :], (BLOCK, SPAN))
         tiles.append(pltpu.roll(row, 0, 1, stride=1, stride_axis=0)[:, :NEAR])
     return jnp.concatenate(tiles, axis=0)
 
@@ -78,9 +78,10 @@
     return pl.ds(pl.multiple_of(block * BLOCK, BLOCK), BLOCK)
 
 
-def two_tiles(ref, source_ref, tile):
+def two_tiles(ref, plan_ref, tile):
+    tile = SOURCE + tile
     return jnp.concatenate(
-        [ref[rows_at(source_ref[tile]), :], ref[rows_at(source_ref[tile + 1]), :]], axis=0
+        [ref[rows_at(plan_ref[tile]), :], ref[rows_at(plan_ref[tile + 1]), :]], axis=0
     )
 
 
@@ -263,6 +264,54 @@
     return routes_ref[0:1, :] * most + rank, jnp.sum(chosen, axis=1, keepdims=True)
 
 
+SOURCE = 2
+
+
+def plan_start(blocks):
+    return SOURCE + blocks + 2
+
+
+def plan_size(blocks):
+    return plan_start(blocks) + 4 + 3 * (blocks + 1)
+
+
+def write_plan(pairs_ref, plan, me):
+    blocks = 2 * pairs_ref.shape[0]
+    half = blocks // 2
+    own = [pairs_ref[me, side] for side in range(2)]
+    plan[0], plan[1] = own[0], own[1]
+    plan[SOURCE] = jnp.int32(0)
+    plan[SOURCE + blocks + 1] = jnp.int32(0)
+
+    def place(position, carry):
+        found = jnp.int32(0)
+        for row in range(blocks):
+            found = found + jnp.where(pairs_ref[row // 2, row % 2] == position, row, 0)
+        plan[SOURCE + 1 + position] = found
+        return carry
+
+    lax.fori_loop(0, blocks, place, 0)
+    early, late = jnp.minimum(own[0], own[1]), jnp.maximum(own[0], own[1])
+    first = jnp.where(own[0] < own[1], 0, 1).astype(jnp.int32)
+    start = plan_start(blocks)
+    plan[start], plan[start + 1] = first, 1 - first
+    plan[start + 2], plan[start + 3] = early, late
+    start = start + 4
+    for step in range(blocks + 1):
+        rest = step - (half + 2)
+        if step <= half:
+            tile, owner = late - step, jnp.int32(1)
+        elif step == half + 1:
+            tile, owner = early, jnp.int32(0)
+        else:
+            tile = jnp.where(rest < early, early - 1 - rest, late - half - 1 - (rest - early))
+            owner = jnp.where(rest < early, 0, 1).astype(jnp.int32)
+        tile = jnp.minimum(jnp.maximum(tile, 0), blocks - 1)
+        plan[start + step] = plan[SOURCE + 1 + tile]
+        plan[start + blocks + 1 + step] = owner
+        plan[start + 2 * blocks + 2 + step] = plan[SOURCE + blocks - tile]
+
+
 def project_kernel(
     counts,
     capacity,
@@ -273,6 +322,9 @@
     wo_ref,
     small_ref,
     routes_ref,
+    pairs_ref,
+    query_hot_ref,
+    key_hot_ref,
     grad_ref,
     qkv_out,
     weights_out,
@@ -280,6 +332,9 @@
     slot_out,
     target_out,
     own_out,
+    plan_out,
+    query_base_out,
+    key_base_out,
     held,
     weights,
     smalls,
@@ -425,6 +480,22 @@
     lax.fori_loop(0, ctx_count, step_body, 0)
     for step in (ctx_count - 2, ctx_count - 1):
         put(step % 2, order(step)[2]).wait()
+    write_plan(pairs_ref, plan_out, rows.me)
+    turned = jnp.transpose(smalls[...].astype(F32))
+    for hot_ref, base_out, sign in (
+        (query_hot_ref, query_base_out, -1),
+        (key_hot_ref, key_base_out, 1),
+    ):
+        table = dot(turned.astype(BF16), hot_ref[...])
+        lane = lane_ids(BLOCK, SPAN)
+        lane = jnp.where(lane < NEAR, lane, lane - SPAN)
+        gap = lane if sign > 0 else BLOCK - lane
+        last = jnp.max(jnp.where(gap == NEAR - 1, table, -jnp.inf), axis=1, keepdims=True)
+        table = jnp.where(gap >= 0, table - last, MASKED)
+        for pair in range(PAIRS):
+            start = experts + 2 + 2 * pair
+            base_out[pair] = jnp.zeros((8, SPAN), F32)
+            base_out[pair, 0:2, :] = table[start : start + 2]
     counted.wait(0)
     lane = lane_ids(1, ctx_count * most)
     for expert in range(exp_dev):
@@ -452,7 +523,9 @@
     mats.finish()
 
 
-def project(counts, capacity, experts, most, rows, weights, small, routes, grad):
+def project(
+    counts, capacity, experts, most, rows, weights, small, routes, pairs, query_hot, key_hot, grad
+):
     tokens, width = rows.shape
     ctx_count, wsh_count = counts
     exp_dev = experts // ctx_count
@@ -460,10 +533,11 @@
     lines, across = grid_of(ctx_count)
     vmem = pl.BlockSpec(memory_space=pltpu.VMEM)
     anywhere = pl.BlockSpec(memory_space=pl.ANY)
+    smem = pl.BlockSpec(memory_space=pltpu.SMEM)
     return pl.pallas_call(
         functools.partial(project_kernel, counts, capacity),
-        in_specs=[anywhere] * 6 + [vmem, anywhere],
-        out_specs=[anywhere] * 3 + [vmem] * 3,
+        in_specs=[anywhere] * 6 + [vmem, smem, vmem, vmem, anywhere],
+        out_specs=[anywhere] * 3 + [vmem] * 3 + [smem] + [vmem] * 2,
         out_shape=[
             jax.ShapeDtypeStruct((length, 3 * width), BF16),
             jax.ShapeDtypeStruct((4, width, width), BF16),
@@ -471,6 +545,9 @@
             jax.ShapeDtypeStruct((8, tokens), jnp.int32),
             jax.ShapeDtypeStruct((8, ctx_count * most), jnp.int32),
             jax.ShapeDtypeStruct((exp_dev, capacity, width), BF16),
+            jax.ShapeDtypeStruct((plan_size(2 * ctx_count),), jnp.int32),
+            jax.ShapeDtypeStruct((PAIRS, 8, SPAN), F32),
+            jax.ShapeDtypeStruct((PAIRS, 8, SPAN), F32),
         ],
         scratch_shapes=[
             pltpu.VMEM((ctx_count, tokens, width), BF16),
@@ -491,10 +568,10 @@
             pltpu.SemaphoreType.DMA((9,)),
         ],
         compiler_params=pltpu.CompilerParams(
-            collective_id=0, has_side_effects=True, vmem_limit_bytes=40 << 20
+            collective_id=0, has_side_effects=True, vmem_limit_bytes=60 << 20
         ),
         name="project",
-    )(rows, *weights, small, routes, grad)
+    )(rows, *weights, small, routes, pairs, query_hot, key_hot, grad)
 
 
 def gelu_parts(values):
@@ -533,6 +610,10 @@
     target_ref,
     lse_ref,
     routes_ref,
+    base_ref,
+    plan_ref,
+    qkv_ref,
+    lse_all_ref,
     output_out,
     grad_mid_out,
     grad_heads_out,
@@ -541,10 +622,22 @@
     grad_wo_out,
     grad_router_out,
     grad_gain_out,
+    dq_out,
+    sums_out,
     grad_in_out,
     grad_out_out,
+    qkv,
+    lse_all,
+    stacked_q,
+    stacked_g,
+    lse_rep,
+    delta_rep,
+    bias,
+    near,
     attn,
     exact,
+    heads,
+    exact_blocks,
     hidden,
     grad,
     wo,
@@ -602,6 +695,8 @@
         (w_out_ref, w_out),
         (exact_ref, exact),
     )
+    if spread_here:
+        sources = sources + ((qkv_ref, qkv), (lse_all_ref, lse_all))
     fetches = [
         pltpu.make_async_copy(src, dst, fetch_sems.at[place])
         for place, (src, dst) in enumerate(sources)
@@ -645,6 +740,7 @@
     resid[...] = hidden[...].astype(F32) + dot(attn[...], wo[...])
     inv_two = lax.rsqrt(jnp.mean(resid[...] * resid[...], axis=-1, keepdims=True) + epsilon)
     normed_two = (resid[...] * inv_two * gain_two).astype(BF16)
+    units = w_in.shape[2]
     placement = placement_of(slot_ref, experts * most)
     returning[0] = dot(placement, normed_two).astype(BF16)
     forth = Exchange(
@@ -655,8 +751,7 @@
         lambda expert, peer: returning.at[0, forth.rows(peer * exp_dev + expert), :],
         lambda expert, peer: incoming.at[expert, forth.rows(peer), :],
     )
-    for expert in range(exp_dev):
-        forth.start(expert)
+    forth.start(0)
     gate = choose(normed_two, router, experts, routes_ref[...])[2]
     for expert in range(exp_dev):
         for step in range(pairs - 1):
@@ -687,32 +782,27 @@
             device_id_type=pl.DeviceIdType.MESH,
         )
 
-    def work(expert, step):
-        line = (my_line + step // 2) % pairs
-        core = (my_core + step % 2) % 2
-        block = line * 2 + core
-
-        @pl.when(step % 2 == 1)
-        def _():
-            gather_x.cross_recv(expert, line, 1).wait_recv()
-            gather_g.cross_recv(expert, line, 1).wait_recv()
-
-        rows = all_x[expert, block]
+    def work(expert, ahead):
+        line = (my_line + ahead) % pairs
+        both = pl.ds(line * 2, 2)
+        gather_x.cross_recv(expert, line, 1).wait_recv()
+        gather_g.cross_recv(expert, line, 1).wait_recv()
+        rows = all_x[expert, both].reshape(2 * capacity, width)
         active, slope = gelu_parts(dot(rows, w_in[expert]))
         active = active.astype(BF16)
-        hid[expert, block] = active
-        parts[0, expert, block] = dot(active, w_out[expert]).astype(BF16)
+        hid[expert, both] = active.reshape(2, capacity, units)
+        part = dot(active, w_out[expert]).astype(BF16)
+        parts[0, expert, both] = part.reshape(2, capacity, width)
+        mate_copy(0, expert, line).start()
         share = choose(rows, router, experts, exp_dev * me + expert)[2]
-        grads = (share * all_g[expert, block].astype(F32)).astype(BF16)
-        all_g[expert, block] = grads
+        grads = all_g[expert, both].reshape(2 * capacity, width).astype(F32)
+        grads = (share * grads).astype(BF16)
+        all_g[expert, both] = grads.reshape(2, capacity, width)
         grad_u = (dot(grads, w_out[expert], 1, 1) * slope).astype(BF16)
-        du[expert, block] = grad_u
-        parts[1, expert, block] = dot(grad_u, w_in[expert], 1, 1).astype(BF16)
-
-        @pl.when(step % 2 == 1)
-        def _():
-            mate_copy(0, expert, line).start()
-            mate_copy(1, expert, line).start()
+        du[expert, both] = grad_u.reshape(2, capacity, units)
+        part = dot(grad_u, w_in[expert], 1, 1).astype(BF16)
+        parts[1, expert, both] = part.reshape(2, capacity, width)
+        mate_copy(1, expert, line).start()
 
     def fold(expert, ahead):
         line = (my_line + ahead) % pairs
@@ -727,13 +817,23 @@
 
     for expert in range(exp_dev):
         forth.wait(expert)
+        if expert + 1 < exp_dev:
+            forth.start(expert + 1)
         own_x[expert] = dot(cap_map(target_ref, expert, capacity), incoming[expert]).astype(BF16)
         gather_x.begin(expert)
         all_x[expert, wsh_me] = own_x[expert]
-        lax.fori_loop(0, 2, lambda step, carry: (work(expert, step), carry)[1], 0)
+        work(expert, 0)
         for step in range(pairs - 1):
             gather_x.advance(expert, step)
-        lax.fori_loop(2, wsh_count, lambda step, carry: (work(expert, step), carry)[1], 0)
+
+        def others(ahead, carry):
+            work(expert, ahead)
+            return carry
+
+        if pairs == 2:
+            work(expert, 1)
+        else:
+            lax.fori_loop(1, pairs, others, 0)
         for ahead in range(1, pairs):
             fold(expert, ahead)
 
@@ -782,51 +882,13 @@
         returning[1, expert_rows] = dot(spread, grad_rows.astype(BF16), 0, 0).astype(BF16)
         back[1].start(expert)
         returning[0, expert_rows] = dot(spread, out_rows, 0, 0).astype(BF16)
+        if expert + 1 < exp_dev:
+            back[0].start(expert)
         router_part = dot(grad_logits, rows, 0, 0)[:experts]
         if expert == 0:
             grad_router_out[...] = router_part
         else:
             grad_router_out[...] += router_part
-    for expert in range(exp_dev):
-        back[0].start(expert)
-    grad_up = grad[...].astype(F32)
-    for expert in range(exp_dev):
-        back[1].wait(expert)
-    grad_normed = dot(placement_of(slot_ref, experts * most), home[1], 0, 0)
-    scaled = grad_normed * gain_two
-    mean = jnp.mean(scaled * resid[...], axis=-1, keepdims=True)
-    gain_part = jnp.sum(grad_normed * resid[...] * inv_two, axis=0, keepdims=True)
-    grad_gain_out[...] = jnp.broadcast_to(gain_part, grad_gain_out.shape)
-    grad_mid = grad_up + inv_two * scaled - resid[...] * inv_two * inv_two * inv_two * mean
-    grad_mid_out[...] = grad_mid
-    branch[home_row] = grad_mid.astype(BF16)
-
-    gather_d = LineGather(
-        "ctx",
-        lines,
-        across,
-        [lambda block: branch.at[block], lambda block: stats.at[block]],
-        [branch.at[me], stats.at[me]],
-        (branch_send, branch_recv),
-    )
-    if spread_here:
-        gather_d.begin(0)
-    grad_heads = dot(branch[home_row], wo[...], 1, 1).astype(BF16)
-    grad_heads_out[...] = grad_heads
-    product = grad_heads.astype(F32) * exact[...]
-    heads = lax.broadcasted_iota(jnp.int32, (width, BLOCK), 0) // HEAD_DIM
-    head_hot = (heads == lane_ids(width, BLOCK)).astype(F32)
-    delta = jnp.transpose(
-        lax.dot_general(
-            product, head_hot, (((1,), (0,)), ((), ())), precision=HIGH, preferred_element_type=F32
-        )
-    )
-    for pair in range(PAIRS):
-        stats[home_row, pair] = lse_ref[pair]
-        stats[home_row, pair, 2:4, :] = delta[2 * pair : 2 * pair + 2, :]
-    if spread_here:
-        gather_d.begin(1)
-
     def in_copy(expert):
         return pltpu.make_async_copy(stage_in, grad_in_out.at[expert], out_sems.at[1])
 
@@ -864,15 +926,127 @@
         slot_sum(stage_in, all_x, du, expert)
         in_copy(expert).start()
 
+    for expert in range(exp_dev):
+        grads_of(expert)
+    grad_up = grad[...].astype(F32)
+    for expert in range(exp_dev):
+        back[1].wait(expert)
+    back[0].start(exp_dev - 1)
+    grad_normed = dot(placement_of(slot_ref, experts * most), home[1], 0, 0)
+    scaled = grad_normed * gain_two
+    mean = jnp.mean(scaled * resid[...], axis=-1, keepdims=True)
+    gain_part = jnp.sum(grad_normed * resid[...] * inv_two, axis=0, keepdims=True)
+    grad_gain_out[...] = jnp.broadcast_to(gain_part, grad_gain_out.shape)
+    grad_mid = grad_up + inv_two * scaled - resid[...] * inv_two * inv_two * inv_two * mean
+    grad_mid_out[...] = grad_mid
+    branch[home_row] = grad_mid.astype(BF16)
+
+    gather_d = LineGather(
+        "ctx",
+        lines,
+        across,
+        [lambda block: branch.at[block], lambda block: stats.at[block]],
+        [branch.at[me], stats.at[me]],
+        (branch_send, branch_recv),
+    )
+    if spread_here:
+        gather_d.begin(0)
+    grad_heads = dot(branch[home_row], wo[...], 1, 1).astype(BF16)
+    grad_heads_out[...] = grad_heads
+    if spread_here:
+        for own in range(2):
+            heads[own] = grad_heads[own * BLOCK : (own + 1) * BLOCK]
+            exact_blocks[own] = exact[own * BLOCK : (own + 1) * BLOCK, :]
+    product = grad_heads.astype(F32) * exact[...]
+    head_of = lax.broadcasted_iota(jnp.int32, (width, BLOCK), 0) // HEAD_DIM
+    head_hot = (head_of == lane_ids(width, BLOCK)).astype(F32)
+    delta = jnp.transpose(
+        lax.dot_general(
+            product, head_hot, (((1,), (0,)), ((), ())), precision=HIGH, preferred_element_type=F32
+        )
+    )
+    for pair in range(PAIRS):
+        stats[home_row, pair] = lse_ref[pair]
+        stats[home_row, pair, 2:4, :] = delta[2 * pair : 2 * pair + 2, :]
+    if spread_here:
+        gather_d.begin(1)
+
     grad_wo_out[...] = dot(attn[...], branch[home_row], 0, 0).astype(BF16)
+
+    plan_from = plan_start(2 * ctx_count)
+    half = ctx_count
+
+    def query_pair(pair, carry):
+        pair_lanes = pl.ds(pl.multiple_of(pair * BLOCK, BLOCK), BLOCK)
+
+        def tile(part, step):
+            lanes = pl.ds(pl.multiple_of(part * width + pair * BLOCK, BLOCK), BLOCK)
+            return qkv[plan_ref[plan_from + 4 + step], :, lanes]
+
+        bias[...] = near_bias(base_ref, pair)
+        for place in range(2):
+            own = plan_ref[plan_from + place]
+            stacked_q[place] = stack_heads(tile(0, 0 if place else half + 1))
+            grads = stack_heads(heads[own, :, pair_lanes])
+            stacked_g[place] = grads
+            own_exact = exact_blocks[own, :, pair_lanes]
+            product = grads.astype(F32) * jnp.concatenate([own_exact, own_exact], axis=0)
+            delta_rep[place] = jnp.broadcast_to(
+                jnp.sum(product, axis=-1, keepdims=True), (2 * BLOCK, BLOCK)
+            )
+            lse_rep[place] = lse_all[pair, own]
+
+        def score_grads(place, step, extra):
+            keys = tile(1, step)
+            scores = dot(stacked_q[place], keys, 1, 1)
+            if extra is not None:
+                scores = scores + extra
+            weights = jnp.exp(scores - lse_rep[place])
+            grad_s = weights * (dot(stacked_g[place], tile(2, step), 1, 1) - delta_rep[place])
+            return grad_s, dot(grad_s.astype(BF16), keys)
+
+        diagonal, big = score_grads(1, 0, bias[:, BLOCK:])
+        beside, more = score_grads(1, 1, bias[:, :BLOCK])
+        big = big + more
+        far = jnp.zeros((2 * BLOCK, BLOCK), F32)
+        for step in range(2, half + 1):
+            grad_s, more = score_grads(1, step, None)
+            far, big = far + grad_s, big + more
+        grad_s, small_part = score_grads(0, half + 1, bias[:, BLOCK:])
+        near[:, BLOCK:] = diagonal + grad_s
+        for step in range(half + 2, 2 * half + 1):
+            place = plan_ref[plan_from + 4 + 2 * half + 1 + step]
+            later = place.astype(F32)
+            sooner = 1.0 - later
+            extra = None
+            if step == half + 2:
+                extra = bias[:, :BLOCK] * sooner
+            grad_s, more = score_grads(place, step, extra)
+            if step == half + 2:
+                near[:, :BLOCK] = beside + grad_s * sooner
+                far = far + grad_s * later
+            else:
+                far = far + grad_s
+            big = big + more * later
+            small_part = small_part + more * sooner
+        second = plan_ref[plan_from].astype(F32)
+        small_part, big = merge_heads(small_part), merge_heads(big)
+        first = 1.0 - second
+        dq_out[:BLOCK, pair_lanes] = (small_part * first + big * second).astype(BF16)
+        dq_out[BLOCK:, pair_lanes] = (big * first + small_part * second).astype(BF16)
+        put_sums(sums_out, pair, near, far)
+        return carry
+
+    def query_pairs(turn):
+        share = PAIRS // (lines - 1)
+        lax.fori_loop(turn * share, (turn + 1) * share, query_pair, 0)
+
     for step in range(lines - 1):
         if spread_here:
             for part in range(2):
                 gather_d.advance(part, step)
-        if step < exp_dev:
-            grads_of(step)
-    for expert in range(min(lines - 1, exp_dev), exp_dev):
-        grads_of(expert)
+        if spread_here:
+            query_pairs(step)
     for expert in range(exp_dev):
         back[0].wait(expert)
     token_out = dot(placement_of(slot_ref, experts * most), home[0], 0, 0)
@@ -951,6 +1125,10 @@
     targets,
     lse_rows,
     routes,
+    base,
+    plan,
+    qkv,
+    lse,
 ):
     ctx_count, wsh_count = counts
     tokens, width = hidden.shape
@@ -965,10 +1143,14 @@
     slot_rows = (exp_dev, wsh_count, capacity)
     spread_here = wsh_count <= 4
     held = ctx_count if spread_here else 1
+    score_rows = NEAR if spread_here else 16
     return pl.pallas_call(
         functools.partial(middle_kernel, counts, experts, spread_here),
-        in_specs=[anywhere] * 7 + [vmem] * 6,
-        out_specs=[vmem] * 3 + [anywhere] * 2 + [vmem] * 3 + [anywhere] * 2,
+        in_specs=[anywhere] * 7
+        + [vmem] * 7
+        + [pl.BlockSpec(memory_space=pltpu.SMEM)]
+        + [anywhere] * 2,
+        out_specs=[vmem] * 3 + [anywhere] * 2 + [vmem] * 5 + [anywhere] * 2,
         out_shape=[
             jax.ShapeDtypeStruct((tokens, width), BF16),
             jax.ShapeDtypeStruct((tokens, width), F32),
@@ -978,12 +1160,24 @@
             jax.ShapeDtypeStruct((width, width), BF16),
             jax.ShapeDtypeStruct((experts, width), F32),
             jax.ShapeDtypeStruct((8, width), F32),
+            jax.ShapeDtypeStruct((tokens if spread_here else 16, width), BF16),
+            jax.ShapeDtypeStruct((PAIRS, 8, SPAN), F32),
             jax.ShapeDtypeStruct((exp_dev, width, units), F32),
             jax.ShapeDtypeStruct((exp_dev, units, width), F32),
         ],
         scratch_shapes=[
+            pltpu.VMEM(qkv.shape if spread_here else (1, 16, BLOCK), BF16),
+            pltpu.VMEM(lse.shape if spread_here else (1, 2, 8, BLOCK), F32),
+            pltpu.VMEM((2, score_rows, BLOCK), BF16),
+            pltpu.VMEM((2, score_rows, BLOCK), BF16),
+            pltpu.VMEM((2, score_rows, BLOCK), F32),
+            pltpu.VMEM((2, score_rows, BLOCK), F32),
+            pltpu.VMEM((score_rows, NEAR), F32),
+            pltpu.VMEM((score_rows, NEAR), F32),
             pltpu.VMEM((tokens, width), BF16),
             pltpu.VMEM((tokens, width), F32),
+            pltpu.VMEM((2, BLOCK if spread_here else 16, width), BF16),
+            pltpu.VMEM((2, BLOCK if spread_here else 8, width), F32),
             pltpu.VMEM((tokens, width), BF16),
             pltpu.VMEM((tokens, width), BF16),
             pltpu.VMEM((width, width), BF16),
@@ -1006,7 +1200,7 @@
             pltpu.VMEM((width, units), F32),
             pltpu.VMEM((units, width), F32),
             pltpu.VMEM((2, tokens, width), BF16),
-            pltpu.SemaphoreType.DMA((7,)),
+            pltpu.SemaphoreType.DMA((9,)),
             pltpu.SemaphoreType.DMA((2,)),
             pltpu.SemaphoreType.DMA((2,)),
             *gather_sems(exp_dev, pairs, 2),
@@ -1021,7 +1215,7 @@
             *gather_sems(2, lines, across),
         ],
         compiler_params=pltpu.CompilerParams(
-            collective_id=1, has_side_effects=True, vmem_limit_bytes=(56 if spread_here else 62) << 20
+            collective_id=1, has_side_effects=True, vmem_limit_bytes=(60 if spread_here else 62) << 20
         ),
         name="middle",
     )(
@@ -1038,91 +1232,194 @@
         targets,
         lse_rows,
         routes,
-    )
-
-
-def forward_kernel(place_ref, source_ref, q_ref, k_ref, v_ref, base_ref, out_ref, exact_ref, lse_ref, row_ref, scores_ref, bias_ref):
-    bias_ref[...] = near_bias(base_ref)
-    lanes = lane_ids(2 * BLOCK, NEAR)
+        base,
+        plan,
+        qkv,
+        lse,
+    )
+
+
+class Tiles:
+    def __init__(self, plan_ref, blocks, keys):
+        self.plan, self.blocks, self.half = plan_ref, blocks, blocks // 2
+        self.start = plan_start(blocks)
+        self.rows_from = self.start + 4 + (2 * (blocks + 1) if keys else 0)
+        self.keys = keys
+        self.count = blocks + 1
+
+    def own(self, place):
+        return self.plan[self.start + (1 - place if self.keys else place)]
+
+    def row(self, step):
+        return self.plan[self.rows_from + step]
+
+    def place(self, step):
+        if step <= self.half:
+            return 1
+        if step == self.half + 1:
+            return 0
+        return self.plan[self.start + 4 + self.blocks + 1 + step]
+
+    def groups(self):
+        found, step = [], 0
+        while step <= self.half:
+            size = 2 if step + 1 <= self.half else 1
+            found.append((step, size))
+            step += size
+        return found + [(step, 1) for step in range(self.half + 1, self.count)]
+
+
+def span(step, size=1):
+    return slice(step * BLOCK, (step + size) * BLOCK)
+
+
+def only(place, wanted, value):
+    if isinstance(place, int):
+        return value if place == wanted else jnp.zeros_like(value)
+    return jnp.where(place == wanted, value, jnp.zeros_like(value))
+
+
+def order_bias(bias, step, size, place, half):
+    if step == 0:
+        return bias[:, : size * BLOCK]
+    if step == half + 1:
+        return bias[:, :BLOCK]
+    if step == half + 2:
+        return jnp.where(place == 0, bias[:, BLOCK:], 0.0)
+    return None
+
+
+def forward_pair(tiles, load, bias, stacked, keys, scores, tops, totals, weights, values, others):
+    half, count = tiles.half, tiles.count
+    lowest = jnp.full((NEAR, BLOCK), MASKED, F32)
+    for place in range(2):
+        stacked[place] = stack_heads(load(0, None, tiles.own(place)))
+    for step in range(count):
+        row = tiles.row(step)
+        keys[span(step), :] = load(1, row, None)
+        tile, place = load(2, row, None), tiles.place(step)
+        values[span(step), :] = only(place, 1, tile)
+        if step > half:
+            others[span(step - half - 1), :] = only(place, 0, tile)
+    best = [lowest, lowest]
+    for step, size in tiles.groups():
+        place = tiles.place(step)
+        part = dot(stacked[place], keys[span(step, size), :], 1, 1)
+        extra = order_bias(bias, step, size, place, half)
+        if extra is not None:
+            part = part + extra
+        scores[:, span(step, size)] = part
+        part = fold_lanes(part, jnp.maximum) if size == 2 else part
+        for wanted in range(2):
+            if isinstance(place, int):
+                if place == wanted:
+                    best[wanted] = jnp.maximum(best[wanted], part)
+            else:
+                best[wanted] = jnp.maximum(best[wanted], jnp.where(place == wanted, part, MASKED))
+    for wanted in range(2):
+        top = jnp.max(best[wanted], axis=-1, keepdims=True)
+        tops[wanted] = jnp.broadcast_to(top, (NEAR, BLOCK))
+    total = [jnp.zeros((NEAR, BLOCK), F32)] * 2
+    for step in range(count):
+        place = tiles.place(step)
+        part = jnp.exp(scores[:, span(step)] - tops[place])
+        high = part.astype(BF16)
+        weights[:NEAR, span(step)] = high
+        weights[NEAR:, span(step)] = (part - high.astype(F32)).astype(BF16)
+        for wanted in range(2):
+            if not isinstance(place, int) or place == wanted:
+                total[wanted] = total[wanted] + only(place, wanted, part)
+    results = []
+    for wanted in range(2):
+        whole = jnp.sum(total[wanted], axis=-1, keepdims=True)
+        if wanted:
+            summed = dot(weights[...], values[...])
+        else:
+            summed = dot(weights[:, span(half + 1, count - half - 1)], others[...])
+        main = summed[:NEAR] / whole
+        exact = main + summed[NEAR:] / whole
+        totals[wanted] = tops[wanted] + jnp.log(jnp.broadcast_to(whole, (NEAR, BLOCK)))
+        results.append((merge_heads(main).astype(BF16), merge_heads(exact)))
+    return results
+
+
+def in_order(tiles, pair):
+    first = tiles.own(0) == 0
+    return jnp.where(first, pair[0], pair[1]), jnp.where(first, pair[1], pair[0])
+
+
+def forward_kernel(
+    plan_ref, q_ref, k_ref, v_ref, base_ref, out_ref, exact_ref, lse_ref, row_ref, bias, *scratch
+):
+    blocks = q_ref.shape[0] // BLOCK
+    tiles = Tiles(plan_ref, blocks, False)
+    refs = (q_ref, k_ref, v_ref)
+    me = lax.axis_index("ctx")
+    near = near_bias(base_ref)
+    bias[...] = jnp.concatenate([near[:, BLOCK:], near[:, :BLOCK]], axis=1)
+    totals = scratch[4]
+
+    def load(part, row, own):
+        return refs[part][rows_at(2 * me + own if row is None else row), :]
+
+    results = forward_pair(tiles, load, bias, *scratch)
+    main = in_order(tiles, [result[0] for result in results])
+    exact = in_order(tiles, [result[1] for result in results])
+    lse = in_order(tiles, [totals[0], totals[1]])
     for own in range(2):
-        block = place_ref[own]
-        stacked = stack_heads(q_ref[rows_at(source_ref[block + 1]), :])
-        scores = dot(stacked, two_tiles(k_ref, source_ref, block), 1, 1) + bias_ref[...]
-        scores = jnp.where(lanes + block * BLOCK < BLOCK, MASKED, scores)
-        scores_ref[0] = scores
-        chunks = jnp.maximum(block, 1) // 2
-
-        def score_step(chunk, best):
-            start = block - 2 * chunk
-            part = dot(stacked, two_tiles(k_ref, source_ref, start), 1, 1)
-            part = jnp.where(lanes + start * BLOCK < BLOCK, MASKED, part)
-            scores_ref[chunk] = part
-            return jnp.maximum(best, fold_lanes(part, jnp.maximum))
-
-        best = lax.fori_loop(1, chunks + 1, score_step, fold_lanes(scores, jnp.maximum))
-        top = jnp.max(best, axis=-1, keepdims=True)
-
-        def value_step(chunk, carry):
-            total, summed = carry
-            weights = jnp.exp(scores_ref[chunk] - top)
-            high = weights.astype(BF16)
-            low = (weights - high.astype(F32)).astype(BF16)
-            values = two_tiles(v_ref, source_ref, block - 2 * chunk)
-            summed = summed + dot(jnp.concatenate([high, low], axis=0), values)
-            return (total + fold_lanes(weights, jnp.add), summed)
-
-        total, summed = lax.fori_loop(
-            0,
-            chunks + 1,
-            value_step,
-            (jnp.zeros((2 * BLOCK, BLOCK), F32), jnp.zeros((4 * BLOCK, BLOCK), F32)),
-        )
-        total = jnp.sum(total, axis=-1, keepdims=True)
-        main = summed[: 2 * BLOCK] / total
-        exact = main + summed[2 * BLOCK :] / total
         rows = pl.ds(own * BLOCK, BLOCK)
-        out_ref[rows, :] = merge_heads(main).astype(BF16)
-        exact_ref[rows, :] = merge_heads(exact)
-        lse = jnp.broadcast_to(top + jnp.log(total), (2 * BLOCK, BLOCK))
-        lse_ref[0, own] = lse
-        lse = jnp.transpose(lse)
+        out_ref[rows, :] = main[own]
+        exact_ref[rows, :] = exact[own]
+        lse_ref[0, own] = lse[own]
+        turned = jnp.transpose(lse[own])
         for head in range(2):
-            row_ref[0, head : head + 1, own * BLOCK : (own + 1) * BLOCK] = lse[
+            row_ref[0, head : head + 1, own * BLOCK : (own + 1) * BLOCK] = turned[
                 :1, head * BLOCK : (head + 1) * BLOCK
             ]
     row_ref[0, 2:8, :] = jnp.zeros((6, NEAR), F32)
 
 
+def forward_scratch(blocks):
+    count = blocks + 1
+    rest = count - blocks // 2 - 1
+    return [
+        pltpu.VMEM((2, NEAR, BLOCK), BF16),
+        pltpu.VMEM((count * BLOCK, BLOCK), BF16),
+        pltpu.VMEM((NEAR, count * BLOCK), F32),
+        pltpu.VMEM((2, NEAR, BLOCK), F32),
+        pltpu.VMEM((2, NEAR, BLOCK), F32),
+        pltpu.VMEM((2 * NEAR, count * BLOCK), BF16),
+        pltpu.VMEM((count * BLOCK, BLOCK), BF16),
+        pltpu.VMEM((rest * BLOCK, BLOCK), BF16),
+    ]
+
+
 def pair_specs(rows, width):
     pairs = width // BLOCK
 
     def column(offset):
-        return pl.BlockSpec((rows, BLOCK), lambda pair, place, source: (0, offset + pair))
+        return pl.BlockSpec((rows, BLOCK), lambda pair, plan: (0, offset + pair))
 
     return [column(0), column(pairs), column(2 * pairs)]
 
 
-def attend_forward(places, source, qkv, base, width):
+def attend_forward(plan, qkv, base, width):
     rows = qkv.shape[0]
-    chunks = rows // NEAR
-    own = pl.BlockSpec((NEAR, BLOCK), lambda pair, place, source: (0, pair))
+    own = pl.BlockSpec((NEAR, BLOCK), lambda pair, plan: (0, pair))
     return pl.pallas_call(
         forward_kernel,
         grid_spec=pltpu.PrefetchScalarGridSpec(
-            num_scalar_prefetch=2,
+            num_scalar_prefetch=1,
             grid=(PAIRS,),
             in_specs=pair_specs(rows, width)
-            + [pl.BlockSpec((1, 8, SPAN), lambda pair, place, source: (pair, 0, 0))],
+            + [pl.BlockSpec((1, 8, SPAN), lambda pair, plan: (pair, 0, 0))],
             out_specs=[
                 own,
                 own,
-                pl.BlockSpec((1, 2, NEAR, BLOCK), lambda pair, place, source: (pair, 0, 0, 0)),
-                pl.BlockSpec((1, 8, NEAR), lambda pair, place, source: (pair, 0, 0)),
+                pl.BlockSpec((1, 2, NEAR, BLOCK), lambda pair, plan: (pair, 0, 0, 0)),
+                pl.BlockSpec((1, 8, NEAR), lambda pair, plan: (pair, 0, 0)),
             ],
-            scratch_shapes=[
-                pltpu.VMEM((chunks, NEAR, NEAR), F32),
-                pltpu.VMEM((NEAR, NEAR), F32),
-            ],
+            scratch_shapes=[pltpu.VMEM((NEAR, NEAR), F32), *forward_scratch(rows // BLOCK)],
         ),
         out_shape=[
             jax.ShapeDtypeStruct((NEAR, width), BF16),
@@ -1130,55 +1427,12 @@
             jax.ShapeDtypeStruct((PAIRS, 2, NEAR, BLOCK), F32),
             jax.ShapeDtypeStruct((PAIRS, 8, NEAR), F32),
         ],
-        compiler_params=pltpu.CompilerParams(vmem_limit_bytes=40 << 20),
+        compiler_params=pltpu.CompilerParams(vmem_limit_bytes=60 << 20),
         name="attend_forward",
-    )(places, source, qkv, qkv, qkv, base)
-
-
-def query_kernel(
-    place_ref, source_ref, q_ref, k_ref, v_ref, base_ref, do_ref, exact_ref, lse_ref, dq_ref, sums_ref, bias_ref, near_ref
-):
-    bias_ref[...] = near_bias(base_ref)
-    lanes = lane_ids(2 * BLOCK, NEAR)
-    far = jnp.zeros((2 * BLOCK, BLOCK), F32)
-    for own in range(2):
-        block = place_ref[own]
-        rows = pl.ds(own * BLOCK, BLOCK)
-        stacked = stack_heads(q_ref[rows_at(source_ref[block + 1]), :])
-        grads = stack_heads(do_ref[rows, :])
-        exact = exact_ref[rows, :]
-        product = grads.astype(F32) * jnp.concatenate([exact, exact], axis=0)
-        delta = jnp.sum(product, axis=-1, keepdims=True)
-        lse = lse_ref[0, own][:, :1]
-
-        def grad_scores(scores, start):
-            weights = jnp.exp(scores - lse)
-            return weights * (dot(grads, two_tiles(v_ref, source_ref, start), 1, 1) - delta)
-
-        scores = dot(stacked, two_tiles(k_ref, source_ref, block), 1, 1) + bias_ref[...]
-        scores = jnp.where(lanes + block * BLOCK < BLOCK, MASKED, scores)
-        near = grad_scores(scores, block)
-        if own == 0:
-            near_ref[...] = near
-        else:
-            near_ref[...] += near
-
-        def step(chunk, carry):
-            grad_q, far = carry
-            start = block - 2 * chunk
-            keys = two_tiles(k_ref, source_ref, start)
-            part = dot(stacked, keys, 1, 1)
-            part = jnp.where(lanes + start * BLOCK < BLOCK, MASKED, part)
-            grad_s = grad_scores(part, start)
-            return (grad_q + dot(grad_s.astype(BF16), keys), far + fold_lanes(grad_s, jnp.add))
-
-        grad_q, far = lax.fori_loop(
-            1,
-            jnp.maximum(block, 1) // 2 + 1,
-            step,
-            (dot(near.astype(BF16), two_tiles(k_ref, source_ref, block)), far),
-        )
-        dq_ref[rows, :] = merge_heads(grad_q).astype(BF16)
+    )(plan, qkv, qkv, qkv, base)
+
+
+def put_sums(sums_ref, place, near_ref, far):
     row_ids = lax.broadcasted_iota(jnp.int32, (BLOCK, SPAN), 0)
     for head in range(2):
         part = near_ref[head * BLOCK : (head + 1) * BLOCK, :]
@@ -1186,29 +1440,76 @@
         for bit in range(BLOCK.bit_length() - 1):
             moved = pltpu.roll(part, SPAN - (1 << bit), 1)
             part = jnp.where((row_ids >> bit) & 1 == 1, moved, part)
-        sums_ref[0, head : head + 1, :] = jnp.sum(part, axis=0, keepdims=True)
+        sums_ref[place, head : head + 1, :] = jnp.sum(part, axis=0, keepdims=True)
         far_part = jnp.sum(far[head * BLOCK : (head + 1) * BLOCK], axis=0, keepdims=True)
-        sums_ref[0, 2 + head : 3 + head, :] = jnp.concatenate(
+        sums_ref[place, 2 + head : 3 + head, :] = jnp.concatenate(
             [far_part, jnp.zeros((1, NEAR), F32)], axis=1
         )
-    sums_ref[0, 4:8, :] = jnp.zeros((4, SPAN), F32)
-
-
-def attend_queries(places, source, qkv, base, grad_out, exact, lse):
+    sums_ref[place, 4:8, :] = jnp.zeros((4, SPAN), F32)
+
+
+def query_kernel(
+    plan_ref, q_ref, k_ref, v_ref, base_ref, do_ref, exact_ref, lse_ref, dq_ref, sums_ref, bias_ref, near_ref
+):
+    bias_ref[...] = near_bias(base_ref)
+    lanes = lane_ids(2 * BLOCK, NEAR)
+    far = jnp.zeros((2 * BLOCK, BLOCK), F32)
+    for own in range(2):
+        block = plan_ref[own]
+        rows = pl.ds(own * BLOCK, BLOCK)
+        stacked = stack_heads(q_ref[rows_at(plan_ref[SOURCE + 1 + block]), :])
+        grads = stack_heads(do_ref[rows, :])
+        exact = exact_ref[rows, :]
+        product = grads.astype(F32) * jnp.concatenate([exact, exact], axis=0)
+        delta = jnp.sum(product, axis=-1, keepdims=True)
+        lse = lse_ref[0, own][:, :1]
+
+        def grad_scores(scores, start):
+            weights = jnp.exp(scores - lse)
+            return weights * (dot(grads, two_tiles(v_ref, plan_ref, start), 1, 1) - delta)
+
+        scores = dot(stacked, two_tiles(k_ref, plan_ref, block), 1, 1) + bias_ref[...]
+        scores = jnp.where(lanes + block * BLOCK < BLOCK, MASKED, scores)
+        near = grad_scores(scores, block)
+        if own == 0:
+            near_ref[...] = near
+        else:
+            near_ref[...] += near
+
+        def step(chunk, carry):
+            grad_q, far = carry
+            start = block - 2 * chunk
+            keys = two_tiles(k_ref, plan_ref, start)
+            part = dot(stacked, keys, 1, 1)
+            part = jnp.where(lanes + start * BLOCK < BLOCK, MASKED, part)
+            grad_s = grad_scores(part, start)
+            return (grad_q + dot(grad_s.astype(BF16), keys), far + fold_lanes(grad_s, jnp.add))
+
+        grad_q, far = lax.fori_loop(
+            1,
+            jnp.maximum(block, 1) // 2 + 1,
+            step,
+            (dot(near.astype(BF16), two_tiles(k_ref, plan_ref, block)), far),
+        )
+        dq_ref[rows, :] = merge_heads(grad_q).astype(BF16)
+    put_sums(sums_ref, 0, near_ref, far)
+
+
+def attend_queries(plan, qkv, base, grad_out, exact, lse):
     rows, width = qkv.shape[0], grad_out.shape[1]
-    own = pl.BlockSpec((NEAR, BLOCK), lambda pair, place, source: (0, pair))
-    row_spec = pl.BlockSpec((1, 8, SPAN), lambda pair, place, source: (pair, 0, 0))
+    own = pl.BlockSpec((NEAR, BLOCK), lambda pair, plan: (0, pair))
+    row_spec = pl.BlockSpec((1, 8, SPAN), lambda pair, plan: (pair, 0, 0))
     return pl.pallas_call(
         query_kernel,
         grid_spec=pltpu.PrefetchScalarGridSpec(
-            num_scalar_prefetch=2,
+            num_scalar_prefetch=1,
             grid=(PAIRS,),
             in_specs=pair_specs(rows, width)
             + [
                 row_spec,
                 own,
                 own,
-                pl.BlockSpec((1, 2, NEAR, BLOCK), lambda pair, place, source: (pair, 0, 0, 0)),
+                pl.BlockSpec((1, 2, NEAR, BLOCK), lambda pair, plan: (pair, 0, 0, 0)),
             ],
             out_specs=[own, row_spec],
             scratch_shapes=[pltpu.VMEM((NEAR, NEAR), F32), pltpu.VMEM((NEAR, NEAR), F32)],
@@ -1217,80 +1518,119 @@
             jax.ShapeDtypeStruct((NEAR, width), BF16),
             jax.ShapeDtypeStruct((PAIRS, 8, SPAN), F32),
         ],
-        compiler_params=pltpu.CompilerParams(vmem_limit_bytes=40 << 20),
+        compiler_params=pltpu.CompilerParams(vmem_limit_bytes=60 << 20),
         name="attend_queries",
-    )(places, source, qkv, qkv, qkv, base, grad_out, exact, lse)
-
-
-def key_kernel(place_ref, source_ref, q_ref, k_ref, v_ref, base_ref, do_ref, stats_ref, dk_ref, dv_ref, bias_ref):
-    bias_ref[...] = near_bias(base_ref)
+    )(plan, qkv, qkv, qkv, base, grad_out, exact, lse)
+
+
+def key_pair(tiles, load, stat, bias, mine, queries, grads, rest_q, rest_g, stats, grad_s, weights):
+    half, count = tiles.half, tiles.count
+    for place in range(2):
+        for part in range(2):
+            mine[part, place] = stack_heads(load(1 + part, None, tiles.own(place)))
+    for step in range(count):
+        row, place = tiles.row(step), tiles.place(step)
+        for part, whole, rest in ((0, queries, rest_q), (3, grads, rest_g)):
+            tile = load(part, row, None)
+            whole[0, span(step), :] = tile
+            whole[1, span(step), :] = only(place, 1, tile)
+            if step > half:
+                rest[span(step - half - 1), :] = only(place, 0, tile)
+        stats[:, span(step)] = stat(row)
+    for step, size in tiles.groups():
+        place = tiles.place(step)
+        scores = dot(mine[0, place], queries[0, span(step, size), :], 1, 1)
+        extra = order_bias(bias, step, size, place, half)
+        if extra is not None:
+            scores = scores + extra
+        push = dot(mine[1, place], grads[0, span(step, size), :], 1, 1)
+        for head in range(2):
+            rows = slice(head * BLOCK, (head + 1) * BLOCK)
+            part = jnp.exp(scores[rows] - stats[head : head + 1, span(step, size)])
+            weights[rows, span(step, size)] = part.astype(BF16)
+            part = part * (push[rows] - stats[2 + head : 3 + head, span(step, size)])
+            grad_s[rows, span(step, size)] = part.astype(BF16)
+    tail = span(half + 1, count - half - 1)
+    grad_k = (dot(grad_s[:, tail], rest_q[...]), dot(grad_s[...], queries[1]))
+    grad_v = (dot(weights[:, tail], rest_g[...]), dot(weights[...], grads[1]))
+    return [
+        [merge_heads(part).astype(BF16) for part in grad] for grad in (grad_k, grad_v)
+    ]
+
+
+def key_kernel(plan_ref, q_ref, k_ref, v_ref, base_ref, do_ref, stats_ref, *refs):
+    passed = (len(refs) - 11) // 2
+    passed_in, outs, passed_out = (
+        refs[:passed],
+        refs[passed : passed + 2],
+        refs[passed + 2 : 2 * passed + 2],
+    )
+    bias, *scratch = refs[2 * passed + 2 :]
+    for src, dst in zip(passed_in, passed_out):
+        dst[...] = src[...]
     blocks = q_ref.shape[0] // BLOCK
-    lanes = lane_ids(2 * BLOCK, NEAR)
-
-    def spread(row, start):
-        window = jnp.concatenate(
-            [
-                stats_ref[source_ref[tile] // 2, 0, row : row + 2, rows_at(source_ref[tile] % 2)]
-                for tile in (start, start + 1)
-            ],
-            axis=1,
+    tiles = Tiles(plan_ref, blocks, True)
+    tile_refs = (q_ref, k_ref, v_ref, do_ref)
+    me = lax.axis_index("ctx")
+    bias[...] = near_bias(base_ref)
+
+    def load(part, row, own):
+        return tile_refs[part][rows_at(2 * me + own if row is None else row), :]
+
+    def stat(row):
+        return stats_ref[row // 2, 0, :, rows_at(row % 2)]
+
+    for out, grad in zip(outs, key_pair(tiles, load, stat, bias, *scratch)):
+        for own, part in enumerate(in_order(tiles, grad)):
+            out[own * BLOCK : (own + 1) * BLOCK, :] = part
+
+
+def key_scratch(blocks):
+    count = blocks + 1
+    rest = count - blocks // 2 - 1
+    return [
+        pltpu.VMEM((2, 2, NEAR, BLOCK), BF16),
+        pltpu.VMEM((2, count * BLOCK, BLOCK), BF16),
+        pltpu.VMEM((2, count * BLOCK, BLOCK), BF16),
+        pltpu.VMEM((rest * BLOCK, BLOCK), BF16),
+        pltpu.VMEM((rest * BLOCK, BLOCK), BF16),
+        pltpu.VMEM((8, count * BLOCK), F32),
+        pltpu.VMEM((NEAR, count * BLOCK), BF16),
+        pltpu.VMEM((NEAR, count * BLOCK), BF16),
+    ]
+
+
+def attend_keys(plan, qkv, base, grad_out, stats, passed):
+    rows, width = grad_out.shape
+    own = pl.BlockSpec((NEAR, BLOCK), lambda pair, plan: (0, pair))
+    pieces = [own] + [
+        pl.BlockSpec(
+            (array.shape[0], array.shape[1] // PAIRS, array.shape[2]), lambda pair, plan: (0, pair, 0)
         )
-        return jnp.concatenate(
-            [
-                jnp.broadcast_to(window[:1], (BLOCK, NEAR)),
-                jnp.broadcast_to(window[1:], (BLOCK, NEAR)),
-            ],
-            axis=0,
-        )
-
-    for own in range(2):
-        block = place_ref[own]
-        rows = pl.ds(own * BLOCK, BLOCK)
-        keys = stack_heads(k_ref[rows_at(source_ref[block + 1]), :])
-        values = stack_heads(v_ref[rows_at(source_ref[block + 1]), :])
-
-        def grads(scores, start):
-            queries, grad_out = two_tiles(q_ref, source_ref, start), two_tiles(do_ref, source_ref, start)
-            scores = jnp.where((start == blocks) & (lanes >= BLOCK), MASKED, scores)
-            weights = jnp.exp(scores - spread(0, start))
-            grad_s = weights * (dot(values, grad_out, 1, 1) - spread(2, start))
-            return dot(grad_s.astype(BF16), queries), dot(weights.astype(BF16), grad_out)
-
-        def step(chunk, carry):
-            start = block + 1 + 2 * chunk
-            more_k, more_v = grads(dot(keys, two_tiles(q_ref, source_ref, start), 1, 1), start)
-            return (carry[0] + more_k, carry[1] + more_v)
-
-        near = dot(keys, two_tiles(q_ref, source_ref, block + 1), 1, 1) + bias_ref[...]
-        chunks = jnp.maximum(blocks - 1 - block, 0) // 2
-        grad_k, grad_v = lax.fori_loop(1, chunks + 1, step, grads(near, block + 1))
-        dk_ref[rows, :] = merge_heads(grad_k).astype(BF16)
-        dv_ref[rows, :] = merge_heads(grad_v).astype(BF16)
-
-
-def attend_keys(places, source, qkv, base, grad_out, stats):
-    rows, width = grad_out.shape
-    own = pl.BlockSpec((NEAR, BLOCK), lambda pair, place, source: (0, pair))
+        for array in passed[1:]
+    ]
     return pl.pallas_call(
         key_kernel,
         grid_spec=pltpu.PrefetchScalarGridSpec(
-            num_scalar_prefetch=2,
+            num_scalar_prefetch=1,
             grid=(PAIRS,),
             in_specs=pair_specs(rows, width)
             + [
-                pl.BlockSpec((1, 8, SPAN), lambda pair, place, source: (pair, 0, 0)),
-                pl.BlockSpec((rows, BLOCK), lambda pair, place, source: (0, pair)),
+                pl.BlockSpec((1, 8, SPAN), lambda pair, plan: (pair, 0, 0)),
+                pl.BlockSpec((rows, BLOCK), lambda pair, plan: (0, pair)),
                 pl.BlockSpec(
-                    (rows // NEAR, 1, 8, NEAR), lambda pair, place, source: (0, pair, 0, 0)
+                    (rows // NEAR, 1, 8, NEAR), lambda pair, plan: (0, pair, 0, 0)
                 ),
-            ],
-            out_specs=[own, own],
-            scratch_shapes=[pltpu.VMEM((NEAR, NEAR), F32)],
+            ]
+            + pieces,
+            out_specs=[own, own] + pieces,
+            scratch_shapes=[pltpu.VMEM((NEAR, NEAR), F32), *key_scratch(rows // BLOCK)],
         ),
-        out_shape=[jax.ShapeDtypeStruct((NEAR, width), BF16)] * 2,
-        compiler_params=pltpu.CompilerParams(vmem_limit_bytes=40 << 20),
+        out_shape=[jax.ShapeDtypeStruct((NEAR, width), BF16)] * 2
+        + [jax.ShapeDtypeStruct(array.shape, array.dtype) for array in passed],
+        compiler_params=pltpu.CompilerParams(vmem_limit_bytes=60 << 20),
         name="attend_keys",
-    )(places, source, qkv, qkv, qkv, base, grad_out, stats)
+    )(plan, qkv, qkv, qkv, base, grad_out, stats, *passed)
 
 
 BITS = {"core": ("wsh", 1), "x": ("wsh", 2), "y": ("ctx", 1), "near": ("ctx", 2), "far": ("ctx", 4)}
@@ -1337,10 +1677,7 @@
     sums_ref,
     hot_ref,
     input_grad_out,
-    wq_out,
-    wk_out,
-    wv_out,
-    wo_out,
+    shares_out,
     router_out,
     gains_out,
     table_out,
@@ -1528,7 +1865,6 @@
         pack_copy(step).wait_recv()
         pack[...] += pack_recv[1, step]
 
-    outs = (wo_out, wq_out, wk_out, wv_out)
     mine = lax.axis_index("wsh")
     for matrix in range(4):
         keep = regions[matrix][steps - 1][0]
@@ -1543,7 +1879,7 @@
             if back < 2:
                 whole_copy(matrix, back + 1).start()
             else:
-                outs[matrix][...] = gathered[matrix].astype(F32)
+                shares_out[matrix] = gathered[matrix]
         if back == 0:
             buckets = table_out.shape[0]
             for block in range(4):
@@ -1578,10 +1914,10 @@
     return pl.pallas_call(
         functools.partial(tail_kernel, experts),
         in_specs=[vmem] * 3 + [anywhere] * 4 + [vmem] * 5,
-        out_specs=[vmem] * 8,
+        out_specs=[vmem] * 5,
         out_shape=[
             jax.ShapeDtypeStruct((tokens, width), BF16),
-            *[jax.ShapeDtypeStruct((share, width), F32)] * 4,
+            jax.ShapeDtypeStruct((4, share, width), BF16),
             jax.ShapeDtypeStruct((share, experts), F32),
             jax.ShapeDtypeStruct((8, share), F32),
             jax.ShapeDtypeStruct((buckets, HEADS), F32),
@@ -1606,10 +1942,42 @@
             dma((steps,)),
         ],
         compiler_params=pltpu.CompilerParams(
-            collective_id=2, has_side_effects=True, vmem_limit_bytes=56 << 20
+            collective_id=2, has_side_effects=True, vmem_limit_bytes=60 << 20
         ),
         name="tail",
     )(dq, dk, dv, hidden, grad_mid, weights, grad_wo, small, router, gains, sums, hot)
+
+
+def finish_kernel(
+    input_ref, shares_ref, router_ref, gains_ref, table_ref, input_out, wq, wk, wv, wo, router, gain_a, gain_m, table
+):
+    input_out[...] = input_ref[...]
+    for place, out in enumerate((wo, wq, wk, wv)):
+        out[...] = shares_ref[place].astype(F32)
+    router[...] = router_ref[...]
+    gain_a[...] = gains_ref[0, :]
+    gain_m[...] = gains_ref[1, :]
+    table[...] = table_ref[...]
+
+
+def finish(grad_input, shares, router, gains, table):
+    share, width = shares.shape[1:]
+    vmem = pl.BlockSpec(memory_space=pltpu.VMEM)
+    return pl.pallas_call(
+        finish_kernel,
+        in_specs=[vmem] * 5,
+        out_specs=[vmem] * 9,
+        out_shape=[
+            jax.ShapeDtypeStruct(grad_input.shape, BF16),
+            *[jax.ShapeDtypeStruct((share, width), F32)] * 4,
+            jax.ShapeDtypeStruct(router.shape, F32),
+            jax.ShapeDtypeStruct((share,), F32),
+            jax.ShapeDtypeStruct((share,), F32),
+            jax.ShapeDtypeStruct(table.shape, F32),
+        ],
+        compiler_params=pltpu.CompilerParams(vmem_limit_bytes=60 << 20),
+        name="finish",
+    )(grad_input, shares, router, gains, table)
 
 
 def rms_forward(values, gain_vec):
@@ -1665,7 +2033,17 @@
         axis=1,
     )
     small = jnp.pad(small, ((0, 0), (0, BLOCK - small.shape[1])))
-    qkv, weights, small, slot_rows, targets, own_g = project(
+    lanes = wrapped_lanes()
+    buckets = rel_bias.shape[0] * wsh_count
+    query_hot = onehot_of(BLOCK - lanes, buckets)
+    key_hot = onehot_of(lanes, buckets)
+
+    def hot_rows(hot):
+        spread = np.zeros((wsh_count, share, SPAN), np.float32)
+        spread[:, : rel_bias.shape[0]] = hot.T.reshape(wsh_count, -1, SPAN)
+        return jnp.asarray(spread.reshape(width, SPAN), BF16)
+
+    qkv, weights, small, slot_rows, targets, own_g, plan, query_base, key_base = project(
         (ctx_count, wsh_count),
         capacity,
         experts,
@@ -1674,37 +2052,12 @@
         (w_query, w_key, w_value, w_output),
         small,
         routes.reshape(1, tokens),
+        block_pairs,
+        hot_rows(query_hot),
+        hot_rows(key_hot),
         cotangent[0],
     )
-    full_query, full_key, full_value, full_output = (weights[place] for place in range(4))
-    full_router = small[:, :experts]
-    gain_one = small[:, experts].astype(F32)
-    gain_two = small[:, experts + 1].astype(F32)
-    full_bias = small.reshape(wsh_count, share, BLOCK)[
-        :, : rel_bias.shape[0], experts + 2 : experts + 2 + HEADS
-    ].reshape(-1, HEADS)
-
-    order = block_pairs.reshape(-1)
-    places = lax.dynamic_slice_in_dim(order, 2 * ctx_rank, 2)
-    ids = jnp.arange(blocks, dtype=jnp.int32)
-    inverse = jnp.sum(jnp.where(order[None, :] == ids[:, None], ids[None, :], 0), axis=1)
-    source = jnp.pad(inverse, (1, 1))
-
-    buckets = full_bias.shape[0]
-    lanes = wrapped_lanes()
-    query_hot = onehot_of(BLOCK - lanes, buckets)
-    key_hot = onehot_of(lanes, buckets)
-
-    def base_rows(hot, distance):
-        table = dot(full_bias, jnp.asarray(hot, BF16), 0, 1)
-        table = table - full_bias[buckets - 1].astype(F32)[:, None]
-        table = jnp.where(jnp.asarray(distance >= 0)[None, :], table, MASKED)
-        return jnp.pad(table.reshape(PAIRS, 2, SPAN), ((0, 0), (0, 6), (0, 0)))
-
-    query_base = base_rows(query_hot, BLOCK - lanes)
-    key_base = base_rows(key_hot, lanes)
-
-    attn_low, attn_exact, lse, lse_rows = attend_forward(places, source, qkv, query_base, width)
+    attn_low, attn_exact, lse, lse_rows = attend_forward(plan, qkv, query_base, width)
     (
         output_rows,
         grad_mid,
@@ -1714,6 +2067,8 @@
         grad_wo,
         grad_router,
         grad_gain_m,
+        grad_q,
+        sums,
         grad_w_in,
         grad_w_out,
     ) = middle(
@@ -1732,18 +2087,25 @@
         targets,
         lse_rows,
         routes.reshape(tokens, 1),
+        query_base,
+        plan,
+        qkv.reshape(blocks, BLOCK, 3 * width),
+        lse,
     )
 
     if heads_all.shape[0] == tokens:
-        heads_all = dot(over("ctx", heads_all), full_output, 1, 1).astype(BF16)
+        heads_all = dot(over("ctx", heads_all), weights[3], 1, 1).astype(BF16)
         stats = over("ctx", stats)
-
-    grad_q, sums = attend_queries(places, source, qkv, query_base, grad_heads, attn_exact, lse)
-    grad_k, grad_v = attend_keys(places, source, qkv, key_base, heads_all, stats)
+        grad_q, sums = attend_queries(
+            plan, qkv, query_base, grad_heads, attn_exact, lse
+        )
+    grad_k, grad_v, output_rows, grad_w_in, grad_w_out = attend_keys(
+        plan, qkv, key_base, heads_all, stats, (output_rows, grad_w_in, grad_w_out)
+    )
 
     bucket_share = buckets // wsh_count
     if ctx_count == 8 and wsh_count == 4 and share % 64 == 0:
-        grad_input, grad_a, grad_b, grad_c, grad_d, own_router, own_gains, own_table = tail(
+        results = tail(
             experts,
             grad_q,
             grad_k,
@@ -1760,20 +2122,8 @@
             share,
             bucket_share,
         )
-        return (
-            output_rows[None],
-            grad_input[None],
-            grad_a,
-            grad_b,
-            grad_c,
-            grad_d,
-            own_router,
-            own_gains[0],
-            own_gains[1],
-            own_table,
-            grad_w_in,
-            grad_w_out,
-        )
+        grad_input, *shares = finish(*results)
+        return (output_rows[None], grad_input[None], *shares, grad_w_in, grad_w_out)
 
     near_sums = sums[:, :2].reshape(HEADS, SPAN)
     far_sums = jnp.sum(sums[:, 2:4].reshape(HEADS, SPAN), axis=1)
@@ -1781,6 +2131,8 @@
     grad_table = grad_table.at[buckets - 1].add(far_sums)
 
     resid_in = hidden_in[0].astype(F32)
+    full_query, full_key, full_value = (weights[place] for place in range(3))
+    gain_one = small[:, experts].astype(F32)
     normed_one, inv_one = rms_forward(resid_in, gain_one)
     normed_one = normed_one.astype(BF16)
     grad_normed_one = dot(grad_q, full_query, 1, 1)

time: 395 us -> 300 us (0.76)
  Pallas kernels: 341 us -> 286 us
  local copies, waits for them, and re-layouts: 48.5 us -> 7.24 us
    unnamed x78 -> x3, local copies, waits for them, and re-layouts: 44.4 us -> 3.68 us
    pallas_call x1, Pallas kernels: 33.7 us -> 3 us  [finish(): pl.pallas_call(finish_kernel, in_specs=[vmem] * 5, out_specs=[vmem] * 9,...]
    pallas_call x1, Pallas kernels: 29.9 us -> 17.2 us  [attend_forward(): pl.pallas_call(forward_kernel, grid_spec=pltpu.PrefetchScalarGridSpec(num...]
    pallas_call x1, Pallas kernels: 24.9 us -> 18.1 us  [attend_keys(): pl.pallas_call(key_kernel, grid_spec=pltpu.PrefetchScalarGridSpec(num_sca...]
    pallas_call x1, Pallas kernels: 131 us -> 125 us  [middle(): pl.pallas_call(functools.partial(middle_kernel, counts, experts, spread_h...]
where the time goes in v3:
time: 300 us; the launch traced here: 295 us
  Pallas kernels  286 us (95%)
  local copies, waits for them, and re-layouts  7.24 us (2%)
    pallas_call x1, Pallas kernels, middle(): pl.pallas_call(functools.partial(middle_kernel, counts, experts, spread_h...  125 us
    pallas_call x1, Pallas kernels, project(): pl.pallas_call(functools.partial(project_kernel, counts, capacity), in_sp...  64.3 us
    pallas_call x1, Pallas kernels, tail(): pl.pallas_call(functools.partial(tail_kernel, experts), in_specs=[vmem] *...  58.9 us
    pallas_call x1, Pallas kernels, attend_keys(): pl.pallas_call(key_kernel, grid_spec=pltpu.PrefetchScalarGridSpec(num_sca...  18.1 us
    pallas_call x1, Pallas kernels, attend_forward(): pl.pallas_call(forward_kernel, grid_spec=pltpu.PrefetchScalarGridSpec(num...  17.2 us

profile of v3, /device:TPU:0, one launch (start us, length us, event | category | flops | bytes accessed | tf_op | source)
XLA Modules:
  0.0 295.2 jit_solution(17440741499326743243)
XLA Ops:
  0.6 0.7 broadcast_in_dim.12
  1.3 0.7 broadcast_in_dim.13
  2.0 0.8 copy.38
  2.7 1.4 copy.40.pairs_ref
  4.1 0.7 fusion.1
  4.8 0.1 copy.39
  4.9 0.6 pad.9.small_ref
  5.5 1.5 copy.41.routes_ref
  7.0 64.3 %project.1 = (bf16[2048,2304]{1,0:T(8,128)(2,1)}, bf16[4,768,768]{2,1,0:T(8,128)(2,1)}, bf16[768,128]{1,0:T(8,128)(2,1)}, s32[8,256]{1,0:T(8,128)}, s32[8,256]{1...) custom-call(bf16[256,768]{1,0:T(8,128)(2,1)} %bitcast.8, ...), custom_call_target="tpu_custom_call" | custom-call | tf_op jit(solution)/shard_map/project/pallas_call | solution.py:537
  71.3 17.2 %attend_forward.1 = (bf16[256,768]{1,0:T(8,128)(2,1)}, f32[256,768]{1,0:T(8,128)}, f32[6,2,256,128]{3,2,1,0:T(8,128)}, f32[6,8,256]{2,1,0:T(8,128)}) custom-call(s32[75]{0:T(128)} %get-tuple-element.55.plan_ref, bf16[2048,2304]{1,0:T(8,128)(2,1)} %get-tuple-element.56.q_ref.k_ref.v_ref, bf16[2048,2304]{1,0:T(8,128)(2,1)} %get-tuple-element.56.q_ref.k_ref.v_ref, ...), custom_call_target="tpu_custom_call" | custom-call | tf_op jit(solution)/shard_map/attend_forward/pallas_call | solution.py:1409
  88.5 124.6 %middle.1 = (bf16[256,768]{1,0:T(8,128)(2,1)}, f32[256,768]{1,0:T(8,128)}, bf16[256,768]{1,0:T(8,128)(2,1)}, bf16[2048,768]{1,0:T(8,128)(2,1)}, f32[8,6,8,256]{3...) custom-call(bf16[256,768]{1,0:T(8,128)(2,1)} %get-tuple-element.59.a, ...), custom_call_target="tpu_custom_call" | custom-call | tf_op jit(solution)/shard_map/middle/pallas_call | solution.py:1147
  213.2 18.1 %attend_keys.1 = (bf16[256,768]{1,0:T(8,128)(2,1)}, bf16[256,768]{1,0:T(8,128)(2,1)}, bf16[256,768]{1,0:T(8,128)(2,1)}, f32[2,768,768]{2,1,0:T(8,128)}, f32[2,768,768]{2,1,0:T(8,128)}) custom-call(s32[75]{0:T(128)} %get-tuple-element.55.plan_ref, bf16[2048,2304]{1,0:T(8,128)(2,1)} %get-tuple-element.56.q_ref.k_ref.v_ref, ...), custom_call_target="tpu_custom_call" | custom-call | tf_op jit(solution)/shard_map/attend_keys/pallas_call | solution.py:1612
  231.3 58.9 %tail.1 = (bf16[256,768]{1,0:T(8,128)(2,1)}, bf16[4,192,768]{2,1,0:T(8,128)(2,1)}, f32[192,16]{1,0:T(8,128)}, f32[8,192]{1,0:T(8,128)}, f32[8,12]{1,0:T(8,128)}) custom-call(bf16[256,768]{1,0:T(8,128)(2,1)} %get-tuple-element.74.dq_ref, bf16[256,768]{1,0:T(8,128)(2,1)} %get-tuple-element.75.dk_ref, bf16[256,768]{1,0:T(8,128)(2,1)} %get-tuple-element.76.dv_ref, ...), custom_call_target="tpu_custom_call" | custom-call | tf_op jit(solution)/shard_map/tail/pallas_call | solution.py:1914
  290.2 3.0 %finish.1 = (bf16[256,768]{1,0:T(8,128)(2,1)}, f32[192,768]{1,0:T(8,128)}, f32[192,768]{1,0:T(8,128)}, f32[192,768]{1,0:T(8,128)}, f32[192,768]{1,0:T(8,128)}, /...) custom-call(bf16[256,768]{1,0:T(8,128)(2,1)} %get-tuple-element.82.input_ref, ...), custom_call_target="tpu_custom_call" | custom-call | tf_op jit(solution)/shard_map/finish/pallas_call | solution.py:1966
  293.2 1.6 copy.42

commit v4 on v3

--- a/solution.py
+++ b/solution.py
@@ -86,9 +86,10 @@
 
 
 class LineGather:
-    def __init__(self, axis, lines, across, views, own, sems):
+    def __init__(self, axis, lines, across, views, own, sems, crossing=None):
         self.axis, self.lines, self.across = axis, lines, across
         self.views, self.own, self.sems = views, own, sems
+        self.crossing = crossing or ["all"] * len(views)
         self.me = lax.axis_index(axis)
         self.line, self.column = self.me // across, self.me % across
 
@@ -136,22 +137,21 @@
         for way in (1, -1):
             there, copy = self.line_send(part, way, 0)
             pl.when(there)(copy.start)
-        for ahead in range(1, self.across):
-            self.cross_send(part, self.me, ahead, own=True).start()
+        if self.crossing[part] != "none":
+            for ahead in range(1, self.across):
+                self.cross_send(part, self.me, ahead, own=True).start()
 
     def advance(self, part, step):
         for way in (1, -1):
             there, block, arrived = self.line_recv(part, way, step)
 
-            @pl.when(there)
-            def _():
-                arrived.wait_recv()
+            pl.when(there)(arrived.wait_recv)
+            if step + 2 < self.lines:
+                onward, copy = self.line_send(part, way, step + 1)
+                pl.when(onward)(copy.start)
+            if self.crossing[part] == "all":
                 for ahead in range(1, self.across):
-                    self.cross_send(part, block, ahead).start()
-
-            if step + 2 < self.lines:
-                there, copy = self.line_send(part, way, step + 1)
-                pl.when(there)(copy.start)
+                    pl.when(there)(self.cross_send(part, block, ahead).start)
 
     def wait_cross(self, part):
         for ahead in range(1, self.across):
@@ -165,8 +165,64 @@
                     there, copy = self.line_send(part, way, step)
                     pl.when(there)(copy.wait_send)
             for ahead in range(1, self.across):
-                for line in range(self.lines):
-                    self.cross_send(part, line * self.across + self.column, ahead).wait_send()
+                if self.crossing[part] == "all":
+                    for line in range(self.lines):
+                        self.cross_send(part, line * self.across + self.column, ahead).wait_send()
+                elif self.crossing[part] == "own":
+                    self.cross_send(part, self.me, ahead).wait_send()
+
+
+class RowGather:
+    def __init__(self, counts, held, sems):
+        lines, across = grid_of(counts[0])
+        tokens = held.shape[1]
+        self.across, self.lines = across, lines
+        me = lax.axis_index("ctx")
+        self.me = me
+        self.balanced = across == 2 and tokens % 32 == 0
+        bulk = tokens * 13 // 16 if self.balanced else tokens
+        half = bulk // 32 * 16
+        cuts = [(0, half), (half, bulk - half)]
+
+        def view(start, rows, turn):
+            def of(block):
+                if turn:
+                    block = block + 1 - 2 * (block % 2)
+                return held.at[block, pl.ds(start, rows), :]
+
+            return of
+
+        views = [view(start, rows, False) for start, rows in cuts]
+        crossing = ["all", "all"]
+        if self.balanced:
+            views += [view(bulk, tokens - bulk, turn) for turn in (False, True)]
+            crossing += ["own", "none"]
+        self.parts = len(views)
+        self.gather = LineGather(
+            "ctx", lines, across, views, [of(me) for of in views], sems, crossing
+        )
+
+    def begin(self):
+        for part in range(min(self.parts, 3)):
+            self.gather.begin(part)
+
+    def advance(self, step):
+        if self.balanced and step == 0:
+            self.gather.cross_recv(2, self.gather.line, 1).wait_recv()
+            self.gather.begin(3)
+        for part in range(self.parts):
+            self.gather.advance(part, step)
+
+    def wait_cross(self, line, ahead):
+        for part in range(2):
+            self.gather.cross_recv(part, line, ahead).wait_recv()
+
+    def finish(self):
+        self.gather.finish()
+
+
+def row_parts(ctx_count, tokens):
+    return 4 if grid_of(ctx_count)[1] == 2 and tokens % 32 == 0 else 2
 
 
 def gather_sems(parts, lines, across):
@@ -325,13 +381,11 @@
     pairs_ref,
     query_hot_ref,
     key_hot_ref,
-    grad_ref,
     qkv_out,
     weights_out,
     small_out,
     slot_out,
     target_out,
-    own_out,
     plan_out,
     query_base_out,
     key_base_out,
@@ -342,15 +396,10 @@
     ready,
     chosen,
     tallies,
-    grad_rows,
-    outgoing,
-    incoming,
     row_send,
     row_recv,
     weight_send,
     weight_recv,
-    grad_send,
-    grad_recv,
     tally_send,
     tally_recv,
     out_sems,
@@ -371,36 +420,34 @@
     def weight_view(place):
         return lambda block: weights.at[place, shard(block), :]
 
-    rows = LineGather(
-        "ctx", lines, across, [lambda block: held.at[block]], [rows_ref], (row_send, row_recv)
-    )
+    rows = RowGather(counts, held, (row_send, row_recv))
     mats = LineGather(
         "wsh",
         pairs,
         2,
         [lambda block: smalls.at[shard(block), :]] + [weight_view(place) for place in range(4)],
-        [small_ref, wq_ref, wk_ref, wv_ref, wo_ref],
+        None,
         (weight_send, weight_recv),
     )
+    mats.own = [view(mats.me) for view in mats.views]
+    own_weights = (small_ref, wq_ref, wk_ref, wv_ref, wo_ref)
     own_copies = [
-        pltpu.make_async_copy(ref, view(index), local_sems.at[2 + place])
-        for place, (ref, view, index) in enumerate(
-            zip(
-                [rows_ref] + mats.own,
-                rows.views + mats.views,
-                [rows.me] + [mats.me] * 5,
-            )
+        pltpu.make_async_copy(ref, view, local_sems.at[2 + place])
+        for place, (ref, view) in enumerate(
+            [(rows_ref, held.at[rows.me])]
+            + list(zip(own_weights, mats.own))
         )
     ]
-    grad_copy = pltpu.make_async_copy(grad_ref, grad_rows, local_sems.at[8])
-    grad_copy.start()
     for copy in own_copies:
         copy.start()
     greet(counts)
-    rows.begin(0)
+    own_copies[0].wait()
+    rows.begin()
     for part in range(5):
-        mats.begin(part)
-    most = incoming.shape[1] // ctx_count
+        own_copies[1 + part].wait()
+        if part < 4:
+            mats.begin(part)
+    most = target_out.shape[1] // ctx_count
     slot, tally = route_slots(routes_ref, chosen, most)
     slot_out[...] = jnp.broadcast_to(slot, slot_out.shape)
     tallies[rows.me] = jnp.broadcast_to(tally, (experts, BLOCK))
@@ -414,74 +461,39 @@
     )
     for ahead in range(1, ctx_count):
         counted.copy(0, ahead, True).start()
-    grad_copy.wait()
-    outgoing[...] = dot(placement_of(slot_out, experts * most), grad_rows[...]).astype(BF16)
-    grads = Exchange(
-        ctx_count,
-        exp_dev,
-        most,
-        (grad_send, grad_recv),
-        lambda expert, peer: outgoing.at[grads.rows(peer * exp_dev + expert), :],
-        lambda expert, peer: incoming.at[expert, grads.rows(peer), :],
-    )
-    for copy in own_copies:
-        copy.wait()
-    for step in range(max(lines, pairs) - 1):
-        if step < lines - 1:
-            rows.advance(0, step)
+    write_plan(pairs_ref, plan_out, rows.me)
+
+    def place_targets():
+        counted.wait(0)
+        lane = lane_ids(1, ctx_count * most)
+        for expert in range(exp_dev):
+            offset = jnp.zeros((1, 1), F32)
+            target = jnp.full((1, ctx_count * most), capacity, jnp.int32)
+            for source in range(ctx_count):
+                count = tallies[source, pl.ds(rows.me * exp_dev + expert, 1), 0:1]
+                inside = (lane >= source * most) & (
+                    lane < source * most + jnp.broadcast_to(count.astype(jnp.int32), lane.shape)
+                )
+                place = lane - source * most + jnp.broadcast_to(offset.astype(jnp.int32), lane.shape)
+                target = jnp.where(inside, place, target)
+                offset = offset + count
+            target_out[expert : expert + 1, :] = target
+        target_out[exp_dev:, :] = jnp.zeros_like(target_out[exp_dev:, :])
+
+    for step in range(lines - 2):
+        rows.advance(step)
         if step == 0:
-            for expert in range(exp_dev):
-                grads.start(expert)
-        if step >= lines - 2 or step < pairs - 1:
-            for part in range(5):
-                if step < pairs - 1:
-                    mats.advance(part, step)
-    for part in range(5):
+            place_targets()
+    for step in range(pairs - 1):
+        for part in range(4):
+            mats.advance(part, step)
+    mats.begin(4)
+    for part in range(4):
         mats.wait_cross(part)
-    weights_copy = pltpu.make_async_copy(weights, weights_out, local_sems.at[0])
-    weights_copy.start()
     small_copy = pltpu.make_async_copy(smalls, small_out, local_sems.at[1])
     small_copy.start()
-    gain[...] = jnp.transpose(smalls[...].astype(F32))[lanes : lanes + 8, :]
-    upper = rows.line // max(lines // 2, 1)
-
-    def put(slot, block):
-        place = pl.ds(pl.multiple_of(block * tokens, tokens), tokens)
-        return pltpu.make_async_copy(ready.at[slot], qkv_out.at[place, :], out_sems.at[slot])
-
-    def order(step):
-        ahead, line = step // lines, step % lines
-        line = line + upper * (lines - 1 - 2 * line)
-        return line, ahead, line * across + (rows.column + across - ahead) % across
-
-    def step_body(step, carry):
-        line, ahead, block = order(step)
-        slot = step % 2
-        for skip in range(1, across):
-
-            @pl.when(ahead == skip)
-            def _():
-                rows.cross_recv(0, line, skip).wait_recv()
-
-        @pl.when(step >= 2)
-        def _():
-            put(slot, order(step - 2)[2]).wait()
-
-        values = held[block].astype(F32)
-        inv = lax.rsqrt(jnp.mean(values * values, axis=-1, keepdims=True) + epsilon)
-        normed = (values * inv * gain[0:1, :]).astype(BF16)
-        for place in range(3):
-            ready[slot, :, place * width : (place + 1) * width] = dot(
-                normed, weights[place]
-            ).astype(BF16)
-        put(slot, block).start()
-        return carry
-
-    lax.fori_loop(0, ctx_count, step_body, 0)
-    for step in (ctx_count - 2, ctx_count - 1):
-        put(step % 2, order(step)[2]).wait()
-    write_plan(pairs_ref, plan_out, rows.me)
     turned = jnp.transpose(smalls[...].astype(F32))
+    gain[...] = turned[lanes : lanes + 8, :]
     for hot_ref, base_out, sign in (
         (query_hot_ref, query_base_out, -1),
         (key_hot_ref, key_base_out, 1),
@@ -496,39 +508,63 @@
             start = experts + 2 + 2 * pair
             base_out[pair] = jnp.zeros((8, SPAN), F32)
             base_out[pair, 0:2, :] = table[start : start + 2]
-    counted.wait(0)
-    lane = lane_ids(1, ctx_count * most)
-    for expert in range(exp_dev):
-        offset = jnp.zeros((1, 1), F32)
-        target = jnp.full((1, ctx_count * most), capacity, jnp.int32)
-        for source in range(ctx_count):
-            count = tallies[source, pl.ds(rows.me * exp_dev + expert, 1), 0:1]
-            inside = (lane >= source * most) & (
-                lane < source * most + jnp.broadcast_to(count.astype(jnp.int32), lane.shape)
-            )
-            place = lane - source * most + jnp.broadcast_to(offset.astype(jnp.int32), lane.shape)
-            target = jnp.where(inside, place, target)
-            offset = offset + count
-        target_out[expert : expert + 1, :] = target
-    target_out[exp_dev:, :] = jnp.zeros_like(target_out[exp_dev:, :])
-    for expert in range(exp_dev):
-        grads.wait(expert)
-        own_out[expert] = dot(cap_map(target_out, expert, capacity), incoming[expert]).astype(BF16)
+    rows.advance(lines - 2)
+    column = rows.me % across
+    upper = rows.me // across // max(lines // 2, 1)
+
+    def put(slot, block):
+        place = pl.ds(pl.multiple_of(block * tokens, tokens), tokens)
+        return pltpu.make_async_copy(ready.at[slot], qkv_out.at[place, :], out_sems.at[slot])
+
+    def order(step):
+        ahead, line = step // lines, step % lines
+        line = line + upper * (lines - 1 - 2 * line)
+        return line, ahead, line * across + (column + across - ahead) % across
+
+    def step_body(step, carry):
+        line, ahead, block = order(step)
+        slot = step % 2
+        for skip in range(1, across):
+
+            @pl.when(ahead == skip)
+            def _():
+                rows.wait_cross(line, skip)
+
+        @pl.when(step >= 2)
+        def _():
+            put(slot, order(step - 2)[2]).wait()
+
+        values = held[block].astype(F32)
+        inv = lax.rsqrt(jnp.mean(values * values, axis=-1, keepdims=True) + epsilon)
+        normed = (values * inv * gain[0:1, :]).astype(BF16)
+        for place in range(3):
+            ready[slot, :, place * width : (place + 1) * width] = dot(
+                normed, weights[place]
+            ).astype(BF16)
+        put(slot, block).start()
+        return carry
+
+    lax.fori_loop(0, ctx_count // 2, step_body, 0)
+    for step in range(pairs - 1):
+        mats.advance(4, step)
+    lax.fori_loop(ctx_count // 2, ctx_count, step_body, 0)
+    mats.wait_cross(4)
+    weights_copy = pltpu.make_async_copy(weights, weights_out, local_sems.at[0])
+    weights_copy.start()
+    for step in (ctx_count - 2, ctx_count - 1):
+        put(step % 2, order(step)[2]).wait()
     weights_copy.wait()
     small_copy.wait()
     counted.finish(0)
-    for expert in range(exp_dev):
-        grads.finish(expert)
     rows.finish()
     mats.finish()
 
 
 def project(
-    counts, capacity, experts, most, rows, weights, small, routes, pairs, query_hot, key_hot, grad
+    counts, capacity, experts, most, rows, weights, small, routes, pairs, query_hot, key_hot
 ):
     tokens, width = rows.shape
     ctx_count, wsh_count = counts
-    exp_dev = experts // ctx_count
     length = tokens * ctx_count
     lines, across = grid_of(ctx_count)
     vmem = pl.BlockSpec(memory_space=pltpu.VMEM)
@@ -536,15 +572,14 @@
     smem = pl.BlockSpec(memory_space=pltpu.SMEM)
     return pl.pallas_call(
         functools.partial(project_kernel, counts, capacity),
-        in_specs=[anywhere] * 6 + [vmem, smem, vmem, vmem, anywhere],
-        out_specs=[anywhere] * 3 + [vmem] * 3 + [smem] + [vmem] * 2,
+        in_specs=[anywhere] * 6 + [vmem, smem, vmem, vmem],
+        out_specs=[anywhere] * 3 + [vmem] * 2 + [smem] + [vmem] * 2,
         out_shape=[
             jax.ShapeDtypeStruct((length, 3 * width), BF16),
             jax.ShapeDtypeStruct((4, width, width), BF16),
             jax.ShapeDtypeStruct((width, small.shape[1]), BF16),
             jax.ShapeDtypeStruct((8, tokens), jnp.int32),
             jax.ShapeDtypeStruct((8, ctx_count * most), jnp.int32),
-            jax.ShapeDtypeStruct((exp_dev, capacity, width), BF16),
             jax.ShapeDtypeStruct((plan_size(2 * ctx_count),), jnp.int32),
             jax.ShapeDtypeStruct((PAIRS, 8, SPAN), F32),
             jax.ShapeDtypeStruct((PAIRS, 8, SPAN), F32),
@@ -557,21 +592,17 @@
             pltpu.VMEM((2, tokens, 3 * width), BF16),
             pltpu.VMEM((experts, tokens), F32),
             pltpu.VMEM((ctx_count, experts, BLOCK), F32),
-            pltpu.VMEM((tokens, width), BF16),
-            pltpu.VMEM((experts * most, width), BF16),
-            pltpu.VMEM((exp_dev, ctx_count * most, width), BF16),
-            *gather_sems(1, lines, across),
+            *gather_sems(row_parts(ctx_count, tokens), lines, across),
             *gather_sems(5, wsh_count // 2, 2),
-            *exchange_sems(ctx_count, exp_dev),
             *exchange_sems(ctx_count, 1),
             pltpu.SemaphoreType.DMA((2,)),
-            pltpu.SemaphoreType.DMA((9,)),
+            pltpu.SemaphoreType.DMA((8,)),
         ],
         compiler_params=pltpu.CompilerParams(
             collective_id=0, has_side_effects=True, vmem_limit_bytes=60 << 20
         ),
         name="project",
-    )(rows, *weights, small, routes, pairs, query_hot, key_hot, grad)
+    )(rows, *weights, small, routes, pairs, query_hot, key_hot)
 
 
 def gelu_parts(values):
@@ -604,7 +635,6 @@
     weights_ref,
     w_in_ref,
     w_out_ref,
-    own_g_ref,
     small_ref,
     slot_ref,
     target_ref,
@@ -613,7 +643,6 @@
     base_ref,
     plan_ref,
     qkv_ref,
-    lse_all_ref,
     output_out,
     grad_mid_out,
     grad_heads_out,
@@ -630,12 +659,19 @@
     lse_all,
     stacked_q,
     stacked_g,
-    lse_rep,
     delta_rep,
     bias,
     near,
+    tile_keys,
+    scores,
+    tops,
+    tile_weights,
+    tile_values,
+    other_values,
+    lse_rows,
+    own_g,
+    early_in,
     attn,
-    exact,
     heads,
     exact_blocks,
     hidden,
@@ -653,6 +689,9 @@
     parts,
     from_mate,
     from_far,
+    shares,
+    mate_shares,
+    far_shares,
     returning,
     home,
     branch,
@@ -667,6 +706,8 @@
     x_recv,
     g_send,
     g_recv,
+    early_send,
+    early_recv,
     go_send,
     go_recv,
     back_send,
@@ -677,6 +718,8 @@
     far_recv,
     branch_send,
     branch_recv,
+    stat_send,
+    stat_recv,
 ):
     ctx_count, wsh_count = counts
     tokens, width = hidden.shape
@@ -686,17 +729,17 @@
     pairs = wsh_count // 2
     me = lax.axis_index("ctx")
     home_row = me if spread_here else 0
-    sources = (
-        (attn_ref, attn),
+    sources = [
+        (grad_ref, grad),
         (weights_ref.at[3], wo),
         (hidden_ref, hidden),
-        (grad_ref, grad),
         (w_in_ref, w_in),
         (w_out_ref, w_out),
-        (exact_ref, exact),
-    )
+    ]
     if spread_here:
-        sources = sources + ((qkv_ref, qkv), (lse_all_ref, lse_all))
+        sources.insert(1, (qkv_ref, qkv))
+    else:
+        sources += [(attn_ref, attn), (exact_ref, exact_blocks)]
     fetches = [
         pltpu.make_async_copy(src, dst, fetch_sems.at[place])
         for place, (src, dst) in enumerate(sources)
@@ -713,7 +756,7 @@
         pairs,
         2,
         views[:exp_dev],
-        [own_g_ref.at[expert] for expert in range(exp_dev)],
+        [own_g.at[expert] for expert in range(exp_dev)],
         (g_send, g_recv),
     )
     gather_x = LineGather(
@@ -726,16 +769,83 @@
     )
     wsh_me, my_line, my_core = gather_x.me, gather_x.line, gather_x.column
     greet(counts)
+    fetches[0].wait()
+    returning[1] = dot(placement_of(slot_ref, experts * most), grad[...]).astype(BF16)
+    early = Exchange(
+        ctx_count,
+        exp_dev,
+        most,
+        (early_send, early_recv),
+        lambda expert, peer: returning.at[1, early.rows(peer * exp_dev + expert), :],
+        lambda expert, peer: early_in.at[expert, early.rows(peer), :],
+    )
     for expert in range(exp_dev):
-        gather_g.begin(expert)
-        all_g[expert, wsh_me] = own_g_ref[expert]
+        early.start(expert)
+
+    def pass_on():
+        for expert in range(exp_dev):
+            early.wait(expert)
+            own_g[expert] = dot(cap_map(target_ref, expert, capacity), early_in[expert]).astype(BF16)
+            gather_g.begin(expert)
+            all_g[expert, wsh_me] = own_g[expert]
+
+    if spread_here:
+        tiles = Tiles(plan_ref, 2 * ctx_count, False)
+        fetches[1].wait()
+
+        def attend(pair, carry):
+            pair_lanes = pl.ds(pl.multiple_of(pair * BLOCK, BLOCK), BLOCK)
+
+            def load(part, row):
+                lanes = pl.ds(pl.multiple_of(part * width + pair * BLOCK, BLOCK), BLOCK)
+                return qkv[row, :, lanes]
+
+            near_tiles = near_bias(base_ref, pair)
+            bias[...] = jnp.concatenate(
+                [near_tiles[:, BLOCK:], near_tiles[:, :BLOCK]], axis=1
+            )
+            totals = lse_all.at[pair]
+            results = forward_pair(
+                tiles,
+                load,
+                bias,
+                stacked_q,
+                tile_keys,
+                scores,
+                tops,
+                totals,
+                tile_weights,
+                tile_values,
+                other_values,
+            )
+            main = in_order(tiles, [result[0] for result in results])
+            whole = in_order(tiles, [result[1] for result in results])
+            lse = in_order(tiles, [totals[0], totals[1]])
+            for own in range(2):
+                rows = pl.ds(own * BLOCK, BLOCK)
+                attn[rows, pair_lanes] = main[own]
+                exact_blocks[own, :, pair_lanes] = whole[own]
+                turned = jnp.transpose(lse[own])
+                for head in range(2):
+                    lse_rows[pair, head : head + 1, own * BLOCK : (own + 1) * BLOCK] = turned[
+                        :1, head * BLOCK : (head + 1) * BLOCK
+                    ]
+            lse_rows[pair, 2:8, :] = jnp.zeros((6, 2 * BLOCK), F32)
+            return carry
+
+        lax.fori_loop(0, PAIRS - 1, attend, 0)
+        pass_on()
+        lax.fori_loop(PAIRS - 1, PAIRS, attend, 0)
+    else:
+        lse_rows[...] = lse_ref[...]
+        pass_on()
 
     small_t = jnp.transpose(small_ref[...].astype(F32))[experts : experts + 8, :]
     gain_two = small_t[1:2, :]
     router = jnp.where(
         lane_ids(width, small_ref.shape[1]) < experts, small_ref[...], jnp.zeros_like(small_ref)
     )
-    for fetch in fetches[:3]:
+    for fetch in fetches[2 if spread_here else 1 :]:
         fetch.wait()
     resid[...] = hidden[...].astype(F32) + dot(attn[...], wo[...])
     inv_two = lax.rsqrt(jnp.mean(resid[...] * resid[...], axis=-1, keepdims=True) + epsilon)
@@ -757,14 +867,16 @@
         for step in range(pairs - 1):
             gather_g.advance(expert, step)
     gather_g.finish()
-    for fetch in fetches[3:]:
-        fetch.wait()
+
+    summed = (parts.at[0], parts.at[1], shares)
+    mate_parts = (from_mate.at[0], from_mate.at[1], mate_shares)
+    far_parts = (from_far.at[0], from_far.at[1], far_shares)
 
     def mate_copy(array, expert, line):
         mine = line * 2 + 1 - my_core
         return pltpu.make_async_remote_copy(
-            src_ref=parts.at[array, expert, mine],
-            dst_ref=from_mate.at[array, expert, line],
+            src_ref=summed[array].at[expert, mine],
+            dst_ref=mate_parts[array].at[expert, line],
             send_sem=mate_send.at[array, expert, line],
             recv_sem=mate_recv.at[array, expert, line],
             device_id={"wsh": my_line * 2 + 1 - my_core},
@@ -774,8 +886,8 @@
     def far_copy(array, expert, ahead):
         line = (my_line + ahead) % pairs
         return pltpu.make_async_remote_copy(
-            src_ref=parts.at[array, expert, line * 2 + my_core],
-            dst_ref=from_far.at[array, expert, ahead - 1],
+            src_ref=summed[array].at[expert, line * 2 + my_core],
+            dst_ref=far_parts[array].at[expert, ahead - 1],
             send_sem=far_send.at[array, expert, ahead - 1],
             recv_sem=far_recv.at[array, expert, ahead - 1],
             device_id={"wsh": line * 2 + my_core},
@@ -791,51 +903,43 @@
         active, slope = gelu_parts(dot(rows, w_in[expert]))
         active = active.astype(BF16)
         hid[expert, both] = active.reshape(2, capacity, units)
-        part = dot(active, w_out[expert]).astype(BF16)
-        parts[0, expert, both] = part.reshape(2, capacity, width)
-        mate_copy(0, expert, line).start()
         share = choose(rows, router, experts, exp_dev * me + expert)[2]
         grads = all_g[expert, both].reshape(2 * capacity, width).astype(F32)
         grads = (share * grads).astype(BF16)
         all_g[expert, both] = grads.reshape(2, capacity, width)
-        grad_u = (dot(grads, w_out[expert], 1, 1) * slope).astype(BF16)
+        push = dot(grads, w_out[expert], 1, 1)
+        product = jnp.sum(push * active.astype(F32), axis=-1, keepdims=True)
+        product = jnp.transpose(jnp.broadcast_to(product, (2 * capacity, BLOCK)))
+        for core in range(2):
+            shares[expert, line * 2 + core] = product[:8, core * capacity : (core + 1) * capacity]
+        mate_copy(2, expert, line).start()
+        grad_u = (push * slope).astype(BF16)
         du[expert, both] = grad_u.reshape(2, capacity, units)
         part = dot(grad_u, w_in[expert], 1, 1).astype(BF16)
         parts[1, expert, both] = part.reshape(2, capacity, width)
         mate_copy(1, expert, line).start()
-
-    def fold(expert, ahead):
+        part = dot(active, w_out[expert]).astype(BF16)
+        parts[0, expert, both] = part.reshape(2, capacity, width)
+        mate_copy(0, expert, line).start()
+
+    def fold(array, expert, ahead):
         line = (my_line + ahead) % pairs
-        for array in range(2):
-            mate_copy(array, expert, line).wait_recv()
-            if ahead > 0:
-                both = parts[array, expert, line * 2 + my_core].astype(F32) + from_mate[
-                    array, expert, line
-                ].astype(F32)
-                parts[array, expert, line * 2 + my_core] = both.astype(BF16)
-                far_copy(array, expert, ahead).start()
-
-    for expert in range(exp_dev):
-        forth.wait(expert)
-        if expert + 1 < exp_dev:
-            forth.start(expert + 1)
-        own_x[expert] = dot(cap_map(target_ref, expert, capacity), incoming[expert]).astype(BF16)
-        gather_x.begin(expert)
-        all_x[expert, wsh_me] = own_x[expert]
-        work(expert, 0)
-        for step in range(pairs - 1):
-            gather_x.advance(expert, step)
-
-        def others(ahead, carry):
-            work(expert, ahead)
-            return carry
-
-        if pairs == 2:
-            work(expert, 1)
-        else:
-            lax.fori_loop(1, pairs, others, 0)
+        mate_copy(array, expert, line).wait_recv()
+        both = summed[array][expert, line * 2 + my_core].astype(F32) + mate_parts[array][
+            expert, line
+        ].astype(F32)
+        summed[array][expert, line * 2 + my_core] = both.astype(summed[array].dtype)
+        far_copy(array, expert, ahead).start()
+
+    def whole(array, expert):
+        mate_copy(array, expert, my_line).wait_recv()
+        total = summed[array][expert, my_line * 2 + my_core].astype(F32) + mate_parts[array][
+            expert, my_line
+        ].astype(F32)
         for ahead in range(1, pairs):
-            fold(expert, ahead)
+            far_copy(array, expert, ahead).wait_recv()
+            total = total + far_parts[array][expert, ahead - 1].astype(F32)
+        return total
 
     back = [
         Exchange(
@@ -856,44 +960,63 @@
         )
         for array in range(2)
     ]
-    for expert in range(exp_dev):
-        forth.finish(expert)
-    for expert in range(exp_dev):
+
+    def settle(expert):
         expert_rows = pl.ds(expert * ctx_count * most, ctx_count * most)
-        fold(expert, 0)
-        sums = []
-        for array in range(2):
-            line = my_line * 2 + my_core
-            total = parts[array, expert, line].astype(F32) + from_mate[
-                array, expert, my_line
-            ].astype(F32)
-            for ahead in range(1, pairs):
-                far_copy(array, expert, ahead).wait_recv()
-                total = total + from_far[array, expert, ahead - 1].astype(F32)
-            sums.append(total)
-        out_rows = sums[0].astype(BF16)
         rows = own_x[expert]
         probs, hot, share = choose(rows, router, experts, exp_dev * me + expert)
-        slot_g = own_g_ref[expert].astype(F32)
-        grad_gate = jnp.sum(slot_g * out_rows.astype(F32), axis=-1, keepdims=True)
-        grad_logits = (share * grad_gate * (hot - probs)).astype(BF16)
-        grad_rows = sums[1].astype(BF16).astype(F32) + dot(grad_logits, router, 1, 1)
+        product = jnp.transpose(whole(2, expert))[:, :1]
+        grad_logits = (product * (hot - probs)).astype(BF16)
+        grad_rows = whole(1, expert).astype(BF16).astype(F32) + dot(grad_logits, router, 1, 1)
         spread = cap_map(target_ref, expert, capacity)
         returning[1, expert_rows] = dot(spread, grad_rows.astype(BF16), 0, 0).astype(BF16)
         back[1].start(expert)
-        returning[0, expert_rows] = dot(spread, out_rows, 0, 0).astype(BF16)
-        if expert + 1 < exp_dev:
-            back[0].start(expert)
         router_part = dot(grad_logits, rows, 0, 0)[:experts]
         if expert == 0:
             grad_router_out[...] = router_part
         else:
             grad_router_out[...] += router_part
+
+    for expert in range(exp_dev):
+        early.finish(expert)
+    for expert in range(exp_dev):
+        forth.wait(expert)
+        if expert + 1 < exp_dev:
+            forth.start(expert + 1)
+        own_x[expert] = dot(cap_map(target_ref, expert, capacity), incoming[expert]).astype(BF16)
+        gather_x.begin(expert)
+        all_x[expert, wsh_me] = own_x[expert]
+        work(expert, 0)
+        if expert:
+            settle(expert - 1)
+        for step in range(pairs - 1):
+            gather_x.advance(expert, step)
+
+        def others(ahead, carry):
+            work(expert, ahead)
+            return carry
+
+        if pairs == 2:
+            work(expert, 1)
+        else:
+            lax.fori_loop(1, pairs, others, 0)
+        for ahead in range(1, pairs):
+            fold(2, expert, ahead)
+            fold(1, expert, ahead)
+    settle(exp_dev - 1)
+    for expert in range(exp_dev):
+        forth.finish(expert)
+        for ahead in range(1, pairs):
+            fold(0, expert, ahead)
+
     def in_copy(expert):
         return pltpu.make_async_copy(stage_in, grad_in_out.at[expert], out_sems.at[1])
 
+    one_stage = units == width
+    out_stage = stage_in if one_stage else stage_out
+
     def out_copy(expert):
-        return pltpu.make_async_copy(stage_out, grad_out_out.at[expert], out_sems.at[0])
+        return pltpu.make_async_copy(out_stage, grad_out_out.at[expert], out_sems.at[0])
 
     group = min(wsh_count, 4)
 
@@ -918,20 +1041,25 @@
 
     def grads_of(expert):
         if expert:
-            out_copy(expert - 1).wait()
-        slot_sum(stage_out, hid, all_g, expert)
+            (in_copy if one_stage else out_copy)(expert - 1).wait()
+        slot_sum(out_stage, hid, all_g, expert)
         out_copy(expert).start()
-        if expert:
+        if one_stage:
+            out_copy(expert).wait()
+        elif expert:
             in_copy(expert - 1).wait()
         slot_sum(stage_in, all_x, du, expert)
         in_copy(expert).start()
 
     for expert in range(exp_dev):
         grads_of(expert)
+        expert_rows = pl.ds(expert * ctx_count * most, ctx_count * most)
+        spread = cap_map(target_ref, expert, capacity)
+        out_rows = whole(0, expert).astype(BF16)
+        returning[0, expert_rows] = dot(spread, out_rows, 0, 0).astype(BF16)
     grad_up = grad[...].astype(F32)
     for expert in range(exp_dev):
         back[1].wait(expert)
-    back[0].start(exp_dev - 1)
     grad_normed = dot(placement_of(slot_ref, experts * most), home[1], 0, 0)
     scaled = grad_normed * gain_two
     mean = jnp.mean(scaled * resid[...], axis=-1, keepdims=True)
@@ -941,23 +1069,25 @@
     grad_mid_out[...] = grad_mid
     branch[home_row] = grad_mid.astype(BF16)
 
-    gather_d = LineGather(
-        "ctx",
-        lines,
-        across,
-        [lambda block: branch.at[block], lambda block: stats.at[block]],
-        [branch.at[me], stats.at[me]],
-        (branch_send, branch_recv),
-    )
     if spread_here:
-        gather_d.begin(0)
+        gather_d = RowGather(counts, branch, (branch_send, branch_recv))
+        gather_s = LineGather(
+            "ctx",
+            lines,
+            across,
+            [lambda block: stats.at[block]],
+            [stats.at[me]],
+            (stat_send, stat_recv),
+        )
+        gather_d.begin()
+    for expert in range(exp_dev):
+        back[0].start(expert)
     grad_heads = dot(branch[home_row], wo[...], 1, 1).astype(BF16)
     grad_heads_out[...] = grad_heads
     if spread_here:
         for own in range(2):
             heads[own] = grad_heads[own * BLOCK : (own + 1) * BLOCK]
-            exact_blocks[own] = exact[own * BLOCK : (own + 1) * BLOCK, :]
-    product = grad_heads.astype(F32) * exact[...]
+    product = grad_heads.astype(F32) * exact_blocks[...].reshape(tokens, width)
     head_of = lax.broadcasted_iota(jnp.int32, (width, BLOCK), 0) // HEAD_DIM
     head_hot = (head_of == lane_ids(width, BLOCK)).astype(F32)
     delta = jnp.transpose(
@@ -966,10 +1096,10 @@
         )
     )
     for pair in range(PAIRS):
-        stats[home_row, pair] = lse_ref[pair]
+        stats[home_row, pair] = lse_rows[pair]
         stats[home_row, pair, 2:4, :] = delta[2 * pair : 2 * pair + 2, :]
     if spread_here:
-        gather_d.begin(1)
+        gather_s.begin(0)
 
     grad_wo_out[...] = dot(attn[...], branch[home_row], 0, 0).astype(BF16)
 
@@ -994,14 +1124,13 @@
             delta_rep[place] = jnp.broadcast_to(
                 jnp.sum(product, axis=-1, keepdims=True), (2 * BLOCK, BLOCK)
             )
-            lse_rep[place] = lse_all[pair, own]
 
         def score_grads(place, step, extra):
             keys = tile(1, step)
-            scores = dot(stacked_q[place], keys, 1, 1)
+            part = dot(stacked_q[place], keys, 1, 1)
             if extra is not None:
-                scores = scores + extra
-            weights = jnp.exp(scores - lse_rep[place])
+                part = part + extra
+            weights = jnp.exp(part - lse_all[pair, place])
             grad_s = weights * (dot(stacked_g[place], tile(2, step), 1, 1) - delta_rep[place])
             return grad_s, dot(grad_s.astype(BF16), keys)
 
@@ -1041,22 +1170,22 @@
         share = PAIRS // (lines - 1)
         lax.fori_loop(turn * share, (turn + 1) * share, query_pair, 0)
 
-    for step in range(lines - 1):
-        if spread_here:
-            for part in range(2):
-                gather_d.advance(part, step)
-        if spread_here:
+    if spread_here:
+        for step in range(lines - 1):
             query_pairs(step)
+            gather_d.advance(step)
+            gather_s.advance(0, step)
     for expert in range(exp_dev):
         back[0].wait(expert)
     token_out = dot(placement_of(slot_ref, experts * most), home[0], 0, 0)
     output_out[...] = (resid[...] + gate * token_out).astype(BF16)
-    upper = gather_d.line // max(lines // 2, 1)
+    column = me % across
+    upper = me // across // max(lines // 2, 1)
 
     def order(step):
         ahead, line = step // lines, step % lines
         line = line + upper * (lines - 1 - 2 * line)
-        return line, ahead, line * across + (gather_d.column + across - ahead) % across
+        return line, ahead, line * across + (column + across - ahead) % across
 
     def put(slot, block):
         place = pl.ds(pl.multiple_of(block * tokens, tokens), tokens)
@@ -1071,8 +1200,8 @@
 
             @pl.when(ahead == skip)
             def _():
-                gather_d.cross_recv(0, line, skip).wait_recv()
-                gather_d.cross_recv(1, line, skip).wait_recv()
+                gather_d.wait_cross(line, skip)
+                gather_s.cross_recv(0, line, skip).wait_recv()
 
         @pl.when(step >= 2)
         def _():
@@ -1094,12 +1223,14 @@
         own_branch = pltpu.make_async_copy(heads_stage.at[0], heads_all_out, heads_sems.at[0])
         own_branch.start()
         own_branch.wait()
-    out_copy(exp_dev - 1).wait()
+    if not one_stage:
+        out_copy(exp_dev - 1).wait()
     in_copy(exp_dev - 1).wait()
     stats_copy.wait()
     for expert in range(exp_dev):
         for array in range(2):
             back[array].finish(expert)
+        for array in range(3):
             for line in range(pairs):
                 mate_copy(array, expert, line).wait_send()
             for ahead in range(1, pairs):
@@ -1107,6 +1238,7 @@
     gather_x.finish()
     if spread_here:
         gather_d.finish()
+        gather_s.finish()
 
 
 def middle(
@@ -1119,7 +1251,6 @@
     weights,
     w_in,
     w_out,
-    own_g,
     small,
     slots,
     targets,
@@ -1128,11 +1259,11 @@
     base,
     plan,
     qkv,
-    lse,
+    capacity,
 ):
     ctx_count, wsh_count = counts
     tokens, width = hidden.shape
-    exp_dev, capacity = own_g.shape[:2]
+    exp_dev = w_in.shape[0]
     units = w_in.shape[2]
     slot_count = targets.shape[1]
     all_slots = experts * (slot_count // ctx_count)
@@ -1144,12 +1275,12 @@
     spread_here = wsh_count <= 4
     held = ctx_count if spread_here else 1
     score_rows = NEAR if spread_here else 16
+    forward = forward_scratch(2 * ctx_count) if spread_here else [pltpu.VMEM((8, BLOCK), F32)] * 8
     return pl.pallas_call(
         functools.partial(middle_kernel, counts, experts, spread_here),
         in_specs=[anywhere] * 7
-        + [vmem] * 7
-        + [pl.BlockSpec(memory_space=pltpu.SMEM)]
-        + [anywhere] * 2,
+        + [vmem] * 6
+        + [pl.BlockSpec(memory_space=pltpu.SMEM), anywhere],
         out_specs=[vmem] * 3 + [anywhere] * 2 + [vmem] * 5 + [anywhere] * 2,
         out_shape=[
             jax.ShapeDtypeStruct((tokens, width), BF16),
@@ -1167,17 +1298,20 @@
         ],
         scratch_shapes=[
             pltpu.VMEM(qkv.shape if spread_here else (1, 16, BLOCK), BF16),
-            pltpu.VMEM(lse.shape if spread_here else (1, 2, 8, BLOCK), F32),
+            pltpu.VMEM((PAIRS, 2, NEAR, BLOCK) if spread_here else (1, 2, 8, BLOCK), F32),
             pltpu.VMEM((2, score_rows, BLOCK), BF16),
             pltpu.VMEM((2, score_rows, BLOCK), BF16),
             pltpu.VMEM((2, score_rows, BLOCK), F32),
-            pltpu.VMEM((2, score_rows, BLOCK), F32),
             pltpu.VMEM((score_rows, NEAR), F32),
             pltpu.VMEM((score_rows, NEAR), F32),
+            *forward[1:4],
+            *forward[5:],
+            pltpu.VMEM((PAIRS, 8, tokens), F32),
+            pltpu.VMEM((exp_dev, capacity, width), BF16),
+            pltpu.VMEM((exp_dev, slot_count, width), BF16),
             pltpu.VMEM((tokens, width), BF16),
-            pltpu.VMEM((tokens, width), F32),
             pltpu.VMEM((2, BLOCK if spread_here else 16, width), BF16),
-            pltpu.VMEM((2, BLOCK if spread_here else 8, width), F32),
+            pltpu.VMEM((2, BLOCK, width), F32),
             pltpu.VMEM((tokens, width), BF16),
             pltpu.VMEM((tokens, width), BF16),
             pltpu.VMEM((width, width), BF16),
@@ -1193,12 +1327,15 @@
             pltpu.VMEM((2, *slot_rows, width), BF16),
             pltpu.VMEM((2, exp_dev, pairs, capacity, width), BF16),
             pltpu.VMEM((2, exp_dev, max(pairs - 1, 1), capacity, width), BF16),
+            pltpu.VMEM((exp_dev, wsh_count, 8, capacity), F32),
+            pltpu.VMEM((exp_dev, pairs, 8, capacity), F32),
+            pltpu.VMEM((exp_dev, max(pairs - 1, 1), 8, capacity), F32),
             pltpu.VMEM((2, all_slots, width), BF16),
             pltpu.VMEM((2, all_slots, width), BF16),
             pltpu.VMEM((held, tokens, width), BF16),
             pltpu.VMEM((held, PAIRS, 8, tokens), F32),
             pltpu.VMEM((width, units), F32),
-            pltpu.VMEM((units, width), F32),
+            pltpu.VMEM((8, BLOCK) if units == width else (units, width), F32),
             pltpu.VMEM((2, tokens, width), BF16),
             pltpu.SemaphoreType.DMA((9,)),
             pltpu.SemaphoreType.DMA((2,)),
@@ -1206,16 +1343,18 @@
             *gather_sems(exp_dev, pairs, 2),
             *gather_sems(exp_dev, pairs, 2),
             *exchange_sems(ctx_count, exp_dev),
+            *exchange_sems(ctx_count, exp_dev),
             pltpu.SemaphoreType.DMA((2, exp_dev, ctx_count - 1)),
             pltpu.SemaphoreType.DMA((2, exp_dev, ctx_count - 1)),
-            pltpu.SemaphoreType.DMA((2, exp_dev, pairs)),
-            pltpu.SemaphoreType.DMA((2, exp_dev, pairs)),
-            pltpu.SemaphoreType.DMA((2, exp_dev, max(pairs - 1, 1))),
-            pltpu.SemaphoreType.DMA((2, exp_dev, max(pairs - 1, 1))),
-            *gather_sems(2, lines, across),
+            pltpu.SemaphoreType.DMA((3, exp_dev, pairs)),
+            pltpu.SemaphoreType.DMA((3, exp_dev, pairs)),
+            pltpu.SemaphoreType.DMA((3, exp_dev, max(pairs - 1, 1))),
+            pltpu.SemaphoreType.DMA((3, exp_dev, max(pairs - 1, 1))),
+            *gather_sems(row_parts(ctx_count, tokens), lines, across),
+            *gather_sems(1, lines, across),
         ],
         compiler_params=pltpu.CompilerParams(
-            collective_id=1, has_side_effects=True, vmem_limit_bytes=(60 if spread_here else 62) << 20
+            collective_id=1, has_side_effects=True, vmem_limit_bytes=(62 if spread_here else 63) << 20
         ),
         name="middle",
     )(
@@ -1226,7 +1365,6 @@
         weights,
         w_in,
         w_out,
-        own_g,
         small,
         slots,
         targets,
@@ -1235,7 +1373,6 @@
         base,
         plan,
         qkv,
-        lse,
     )
 
 
@@ -1250,6 +1387,9 @@
     def own(self, place):
         return self.plan[self.start + (1 - place if self.keys else place)]
 
+    def own_step(self, place):
+        return 0 if place else self.half + 1
+
     def row(self, step):
         return self.plan[self.rows_from + step]
 
@@ -1273,10 +1413,14 @@
     return slice(step * BLOCK, (step + size) * BLOCK)
 
 
+def share_of(place, wanted):
+    return place.astype(F32) if wanted else 1.0 - place.astype(F32)
+
+
 def only(place, wanted, value):
     if isinstance(place, int):
         return value if place == wanted else jnp.zeros_like(value)
-    return jnp.where(place == wanted, value, jnp.zeros_like(value))
+    return value * share_of(place, wanted).astype(value.dtype)
 
 
 def order_bias(bias, step, size, place, half):
@@ -1285,7 +1429,7 @@
     if step == half + 1:
         return bias[:, :BLOCK]
     if step == half + 2:
-        return jnp.where(place == 0, bias[:, BLOCK:], 0.0)
+        return bias[:, BLOCK:] * share_of(place, 0)
     return None
 
 
@@ -1293,11 +1437,11 @@
     half, count = tiles.half, tiles.count
     lowest = jnp.full((NEAR, BLOCK), MASKED, F32)
     for place in range(2):
-        stacked[place] = stack_heads(load(0, None, tiles.own(place)))
+        stacked[place] = stack_heads(load(0, tiles.row(tiles.own_step(place))))
     for step in range(count):
         row = tiles.row(step)
-        keys[span(step), :] = load(1, row, None)
-        tile, place = load(2, row, None), tiles.place(step)
+        keys[span(step), :] = load(1, row)
+        tile, place = load(2, row), tiles.place(step)
         values[span(step), :] = only(place, 1, tile)
         if step > half:
             others[span(step - half - 1), :] = only(place, 0, tile)
@@ -1315,7 +1459,8 @@
                 if place == wanted:
                     best[wanted] = jnp.maximum(best[wanted], part)
             else:
-                best[wanted] = jnp.maximum(best[wanted], jnp.where(place == wanted, part, MASKED))
+                share = share_of(place, wanted)
+                best[wanted] = jnp.maximum(best[wanted], part * share + MASKED * (1.0 - share))
     for wanted in range(2):
         top = jnp.max(best[wanted], axis=-1, keepdims=True)
         tops[wanted] = jnp.broadcast_to(top, (NEAR, BLOCK))
@@ -1344,8 +1489,10 @@
 
 
 def in_order(tiles, pair):
-    first = tiles.own(0) == 0
-    return jnp.where(first, pair[0], pair[1]), jnp.where(first, pair[1], pair[0])
+    kind = pair[0].dtype
+    second = tiles.own(0).astype(F32)
+    first, second = (1.0 - second).astype(kind), second.astype(kind)
+    return pair[0] * first + pair[1] * second, pair[1] * first + pair[0] * second
 
 
 def forward_kernel(
@@ -1354,13 +1501,12 @@
     blocks = q_ref.shape[0] // BLOCK
     tiles = Tiles(plan_ref, blocks, False)
     refs = (q_ref, k_ref, v_ref)
-    me = lax.axis_index("ctx")
     near = near_bias(base_ref)
     bias[...] = jnp.concatenate([near[:, BLOCK:], near[:, :BLOCK]], axis=1)
     totals = scratch[4]
 
-    def load(part, row, own):
-        return refs[part][rows_at(2 * me + own if row is None else row), :]
+    def load(part, row):
+        return refs[part][rows_at(row), :]
 
     results = forward_pair(tiles, load, bias, *scratch)
     main = in_order(tiles, [result[0] for result in results])
@@ -1527,11 +1673,11 @@
     half, count = tiles.half, tiles.count
     for place in range(2):
         for part in range(2):
-            mine[part, place] = stack_heads(load(1 + part, None, tiles.own(place)))
+            mine[part, place] = stack_heads(load(1 + part, tiles.row(tiles.own_step(place))))
     for step in range(count):
         row, place = tiles.row(step), tiles.place(step)
         for part, whole, rest in ((0, queries, rest_q), (3, grads, rest_g)):
-            tile = load(part, row, None)
+            tile = load(part, row)
             whole[0, span(step), :] = tile
             whole[1, span(step), :] = only(place, 1, tile)
             if step > half:
@@ -1571,11 +1717,10 @@
     blocks = q_ref.shape[0] // BLOCK
     tiles = Tiles(plan_ref, blocks, True)
     tile_refs = (q_ref, k_ref, v_ref, do_ref)
-    me = lax.axis_index("ctx")
     bias[...] = near_bias(base_ref)
 
-    def load(part, row, own):
-        return tile_refs[part][rows_at(2 * me + own if row is None else row), :]
+    def load(part, row):
+        return tile_refs[part][rows_at(row), :]
 
     def stat(row):
         return stats_ref[row // 2, 0, :, rows_at(row % 2)]
@@ -2043,7 +2188,7 @@
         spread[:, : rel_bias.shape[0]] = hot.T.reshape(wsh_count, -1, SPAN)
         return jnp.asarray(spread.reshape(width, SPAN), BF16)
 
-    qkv, weights, small, slot_rows, targets, own_g, plan, query_base, key_base = project(
+    qkv, weights, small, slot_rows, targets, plan, query_base, key_base = project(
         (ctx_count, wsh_count),
         capacity,
         experts,
@@ -2055,9 +2200,12 @@
         block_pairs,
         hot_rows(query_hot),
         hot_rows(key_hot),
-        cotangent[0],
-    )
-    attn_low, attn_exact, lse, lse_rows = attend_forward(plan, qkv, query_base, width)
+    )
+    if wsh_count > 4:
+        attn_low, attn_exact, lse, lse_rows = attend_forward(plan, qkv, query_base, width)
+    else:
+        attn_low = attn_exact = hidden_in[0]
+        lse_rows = query_base
     (
         output_rows,
         grad_mid,
@@ -2075,13 +2223,12 @@
         (ctx_count, wsh_count),
         experts,
         attn_low,
-        attn_exact,
+        attn_exact.reshape(2, BLOCK, width),
         hidden_in[0],
         cotangent[0],
         weights,
         w_in,
         w_out,
-        own_g,
         small,
         slot_rows,
         targets,
@@ -2090,7 +2237,7 @@
         query_base,
         plan,
         qkv.reshape(blocks, BLOCK, 3 * width),
-        lse,
+        capacity,
     )
 
     if heads_all.shape[0] == tokens:

time: 300 us -> 285 us (0.950)
  Pallas kernels: 286 us -> 271 us
    pallas_call x1 -> x0, Pallas kernels: 17.2 us -> none  [attend_forward(): pl.pallas_call(forward_kernel, grid_spec=pltpu.PrefetchScalarGridSpec(num...]
    pallas_call x1, Pallas kernels: 125 us -> 136 us  [middle(): pl.pallas_call(functools.partial(middle_kernel, counts, experts, spread_h...]
    pallas_call x1, Pallas kernels: 64.3 us -> 53.7 us  [project(): pl.pallas_call(functools.partial(project_kernel, counts, capacity), in_sp...]
where the time goes in v4:
time: 285 us; the launch traced here: 280 us
  Pallas kernels  271 us (95%)
  local copies, waits for them, and re-layouts  7.24 us (3%)
    pallas_call x1, Pallas kernels, middle(): pl.pallas_call(functools.partial(middle_kernel, counts, experts, spread_h...  136 us
    pallas_call x1, Pallas kernels, tail(): pl.pallas_call(functools.partial(tail_kernel, experts), in_specs=[vmem] *...  59.3 us
    pallas_call x1, Pallas kernels, project(): pl.pallas_call(functools.partial(project_kernel, counts, capacity), in_sp...  53.7 us
    pallas_call x1, Pallas kernels, attend_keys(): pl.pallas_call(key_kernel, grid_spec=pltpu.PrefetchScalarGridSpec(num_sca...  18.3 us

profile of v4, /device:TPU:0, one launch (start us, length us, event | category | flops | bytes accessed | tf_op | source)
XLA Modules:
  0.0 279.6 jit_solution(18107905894180590928)
XLA Ops:
  0.6 0.7 broadcast_in_dim.12
  1.3 0.7 broadcast_in_dim.13
  2.0 0.8 copy.38
  2.7 1.4 copy.40.pairs_ref
  4.1 0.7 fusion.1
  4.8 0.1 copy.39
  4.9 0.6 pad.9.small_ref
  5.5 1.5 copy.41.routes_ref
  7.0 53.7 %project.1 = (bf16[2048,2304]{1,0:T(8,128)(2,1)}, bf16[4,768,768]{2,1,0:T(8,128)(2,1)}, bf16[768,128]{1,0:T(8,128)(2,1)}, s32[8,256]{1,0:T(8,128)}, s32[8,256]{1...) custom-call(bf16[256,768]{1,0:T(8,128)(2,1)} %bitcast.9, bf16[192,768]{1,0:T(8,128)(2,1)} %wq_ref.1, ...), custom_call_target="tpu_custom_call" | custom-call | tf_op jit(solution)/shard_map/project/pallas_call | solution.py:573
  60.7 136.5 %middle.1 = (bf16[256,768]{1,0:T(8,128)(2,1)}, f32[256,768]{1,0:T(8,128)}, bf16[256,768]{1,0:T(8,128)(2,1)}, bf16[2048,768]{1,0:T(8,128)(2,1)}, f32[8,6,8,256]{3...) custom-call(bf16[256,768]{1,0:T(8,128)(2,1)} %bitcast.10, ...), custom_call_target="tpu_custom_call" | custom-call | tf_op jit(solution)/shard_map/middle/pallas_call | solution.py:1279
  197.2 18.3 %attend_keys.1 = (bf16[256,768]{1,0:T(8,128)(2,1)}, bf16[256,768]{1,0:T(8,128)(2,1)}, bf16[256,768]{1,0:T(8,128)(2,1)}, f32[2,768,768]{2,1,0:T(8,128)}, f32[2,768,768]{2,1,0:T(8,128)}) custom-call(s32[75]{0:T(128)} %get-tuple-element.50.plan_ref, bf16[2048,2304]{1,0:T(8,128)(2,1)} %get-tuple-element.51.q_ref.k_ref.v_ref, ...), custom_call_target="tpu_custom_call" | custom-call | tf_op jit(solution)/shard_map/attend_keys/pallas_call | solution.py:1757
  215.5 59.3 %tail.1 = (bf16[256,768]{1,0:T(8,128)(2,1)}, bf16[4,192,768]{2,1,0:T(8,128)(2,1)}, f32[192,16]{1,0:T(8,128)}, f32[8,192]{1,0:T(8,128)}, f32[8,12]{1,0:T(8,128)}) custom-call(bf16[256,768]{1,0:T(8,128)(2,1)} %get-tuple-element.64.dq_ref, bf16[256,768]{1,0:T(8,128)(2,1)} %get-tuple-element.65.dk_ref, bf16[256,768]{1,0:T(8,128)(2,1)} %get-tuple-element.66.dv_ref, ...), custom_call_target="tpu_custom_call" | custom-call | tf_op jit(solution)/shard_map/tail/pallas_call | solution.py:2059
  274.8 3.0 %finish.1 = (bf16[256,768]{1,0:T(8,128)(2,1)}, f32[192,768]{1,0:T(8,128)}, f32[192,768]{1,0:T(8,128)}, f32[192,768]{1,0:T(8,128)}, f32[192,768]{1,0:T(8,128)}, /...) custom-call(bf16[256,768]{1,0:T(8,128)(2,1)} %get-tuple-element.72.input_ref, ...), custom_call_target="tpu_custom_call" | custom-call | tf_op jit(solution)/shard_map/finish/pallas_call | solution.py:2111
  277.8 1.6 copy.42
